TPU v7x, 128 devices: a whole 4x4x4 slice. The times are simulated.
128 devices in a mesh: lon: 64 (over y_lo, x, z, core), lat: 2 (over y_hi).
Axes of the slice: x: 4, y: 4 (y_hi: 2, y_lo: 2; y = y_hi * 2 + y_lo), z: 4, core: 2. Of those that a mesh axis runs over, the one named last changes fastest.
Arguments:
- coords: float32 [3, 1024, 128], P(None, ('lon', 'lat')), may hold values from -64 to 64, as said below
- observed: float32 [32, 1024, 128], P(None, ('lon', 'lat')), may hold values from -6 to 6
- neighbours: int32 [4, 1024], P(None, ('lon', 'lat')), may hold values from 0 to 1023, as said below
- counts: int32 [128], replicated, may hold values from 1 to 8, as said below
- lengthscale: float32 [1], replicated, may hold values from 0.3 to 1
- nugget: float32 [1], replicated, may hold values from 0.1 to 0.5
Outputs:
- predicted: float32 [32, 1024, 128], P(None, ('lon', 'lat'))
- variance: float32 [1024, 128], P(('lon', 'lat'))
Inputs may be any that keep to these rules, and one draw needn't show every extreme that they name: `neighbours`: the 4 entries of a block are distinct and never the block itself. A block on band l, sub-band h, slot s names only blocks of either sub-band whose cycle position (band * 8 + slot) lies within 8 of l * 8 + s around the cycle of 512 positions. Entry l * 2 + h counts the live blocks of band l, sub-band h: its slots 0 to count - 1 are live. The entries equal to 8 are exactly those of a run of 8 consecutive bands around the cycle, both sub-bands; all others are at most 2. `coords`: point k of block b on band l, sub-band h, slot s is (r cos a, r sin a, h + w) with r = 64 / (2 pi), a = 2 pi (l + (s + u) / 8) / 64, and u, w in [0, 1).
All inputs are finite; a program needn't handle non-finite values.
Results may differ from a plain program's by a relative error of at most 0.0003.
Values sent between devices are 32-bit elements; how exact they have to be, the bound alone decides.
No kernel may reach another device: no remote copies, remote signals or barrier semaphores. Data moves between devices by JAX's collectives and lax.ppermute only.
A program may use at most 64 MiB of HBM per device.

v0:
```python
import jax
import jax.numpy as jnp
from jax import lax
from jax.sharding import PartitionSpec as P


def sent_to_all(shard, axis):
    length = lax.axis_size(axis)
    return lax.all_to_all(
        jnp.broadcast_to(shard[None], (length, *shard.shape)), axis, 0, 0, tiled=True
    )


def in_order(pieces, dim):
    shape = list(pieces.shape[1:])
    shape[dim] *= pieces.shape[0]
    return jnp.moveaxis(pieces, 0, dim).reshape(shape)


def collect(shard, axis, dim):
    pieces = sent_to_all(shard, axis)
    return in_order(pieces, dim)


def padded(cells, sides, width):
    for axis, dim in sides:
        count = lax.axis_size(axis)
        head = lax.slice_in_dim(cells, 0, width, axis=dim)
        tail = lax.slice_in_dim(cells, cells.shape[dim] - width, cells.shape[dim], axis=dim)
        cells = jnp.concatenate(
            [
                lax.ppermute(tail, axis, [(i, (i + 1) % count) for i in range(count)]),
                cells,
                lax.ppermute(head, axis, [((i + 1) % count, i) for i in range(count)]),
            ],
            axis=dim,
        )
    return cells


def partner(value, axis, apart):
    mask = 2**apart
    pairs = [(source, source ^ mask) for source in range(lax.axis_size(axis))]
    return lax.ppermute(value, axis, pairs)


def solve_group(points, values, target, scale, noise):
    count = points.shape[2]
    delta = points[:, :, :, None] - points[:, :, None, :]
    dist = jnp.sqrt(jnp.sum(delta * delta, axis=1))
    cov = jnp.exp(-dist / scale) + noise * jnp.eye(count, dtype=jnp.float32)
    factor = jnp.linalg.cholesky(cov)
    offset = points[:, :, :, None] - target[:, :, None, :]
    cross = jnp.exp(-jnp.sqrt(jnp.sum(offset * offset, axis=1)) / scale)
    width = cross.shape[2]
    rhs = jnp.concatenate([cross, values], axis=2)
    solved = lax.linalg.triangular_solve(factor, rhs, left_side=True, lower=True)
    weights = solved[:, :, :width]
    projected = solved[:, :, width:]
    mean = jnp.einsum("gmb,gmf->gbf", weights, projected, precision=lax.Precision.HIGHEST)
    spread = 1.0 - jnp.sum(weights * weights, axis=1)
    return (mean, spread)


def predict_slots(package, active, listed, channels, width, scale, noise):
    total = package.shape[0]
    group_size = 4
    rounded = (total + group_size - 1) // group_size * group_size
    cond_len = listed * channels * width

    def step(index, state):
        mean_buf, spread_buf = state
        piece = lax.dynamic_slice_in_dim(package, index * group_size, group_size, 0)
        cond = piece[:, :cond_len].reshape(group_size, listed, channels, width)
        target = piece[:, cond_len:].reshape(group_size, 3, width)
        points = cond[:, :, :3, :].transpose(0, 2, 1, 3).reshape(group_size, 3, listed * width)
        values = (
            cond[:, :, 3:, :]
            .transpose(0, 1, 3, 2)
            .reshape(group_size, listed * width, channels - 3)
        )
        mean, spread = solve_group(points, values, target, scale, noise)
        mean_buf = lax.dynamic_update_slice_in_dim(
            mean_buf, mean.transpose(2, 0, 1), index * group_size, 1
        )
        spread_buf = lax.dynamic_update_slice_in_dim(spread_buf, spread, index * group_size, 0)
        return (mean_buf, spread_buf)

    start_state = (
        jnp.zeros((channels - 3, rounded, width), jnp.float32),
        jnp.zeros((rounded, width), jnp.float32),
    )
    trips = (active + group_size - 1) // group_size
    mean_buf, spread_buf = lax.fori_loop(0, trips, step, start_state)
    return (mean_buf, spread_buf)


def on_device(coords, observed, neighbours, counts, lengthscale, nugget):
    scale = lengthscale[0]
    noise = nugget[0]
    bands = lax.axis_size("lon")
    subs = lax.axis_size("lat")
    slots = coords.shape[1]
    width = coords.shape[2]
    listed = neighbours.shape[0]
    features = jnp.concatenate([coords, observed], axis=0)
    channels = features.shape[0]
    my_band = lax.axis_index("lon")
    my_sub = lax.axis_index("lat")
    owner = neighbours // slots
    other_band = owner // subs
    other_sub = owner % subs
    other_slot = neighbours % slots
    offset = (other_band - my_band) % bands
    side = jnp.where(offset == 0, 1, jnp.where(offset == 1, 2, 0))
    paired = collect(features, "lat", 1)
    pool = padded(paired, (("lon", 1),), slots * subs)
    where_row = (side * subs + other_sub) * slots + other_slot
    pool_rows = pool.transpose(1, 0, 2)
    chosen = where_row.T.reshape(-1)
    cond = jnp.take(pool_rows, chosen, axis=0).reshape(slots, listed * channels * width)
    target = coords.transpose(1, 0, 2).reshape(slots, 3 * width)
    package = jnp.concatenate([cond, target], axis=1)
    alive = counts[my_band * subs + my_sub]
    half = slots // 2
    table = counts.reshape(bands, subs)
    loads = lax.dynamic_index_in_dim(table, my_sub, 1, keepdims=False)
    lanes = jnp.arange(bands, dtype=jnp.int32)
    levels = bands.bit_length() - 1
    work = jnp.concatenate([package, jnp.zeros((half, package.shape[1]), jnp.float32)], axis=0)
    history = []
    for bit in range(levels - 3, levels):
        partner_loads = loads[lanes ^ 1 << bit]
        given = jnp.maximum(0, (loads - partner_loads) // 2)
        gained = jnp.maximum(0, (partner_loads - loads) // 2)
        mine = loads[my_band]
        give = given[my_band]
        outgoing = lax.dynamic_slice_in_dim(work, mine - give, half, 0)
        incoming = partner(outgoing, "lon", bit)
        work = lax.dynamic_update_slice_in_dim(work, incoming, mine, 0)
        history.append((bit, mine, give))
        loads = loads - given + gained
    final = loads[my_band]
    mean_buf, spread_buf = predict_slots(work, final, listed, channels, width, scale, noise)
    results = jnp.concatenate([mean_buf, spread_buf[None]], axis=0)
    for bit, mine, give in reversed(history):
        sending = lax.dynamic_slice_in_dim(results, mine, half, 1)
        returned = partner(sending, "lon", bit)
        results = lax.dynamic_update_slice_in_dim(results, returned, mine - give, 1)
    mean_own = results[:-1, :slots]
    spread_own = results[-1, :slots]
    live = jnp.arange(slots, dtype=jnp.int32) < alive
    predicted = jnp.where(live[None, :, None], mean_own, jnp.zeros_like(mean_own))
    variance = jnp.where(live[:, None], spread_own, jnp.zeros_like(spread_own))
    return (predicted, variance)


def solution(mesh):
    placed = (
        P(None, ("lon", "lat"), None),
        P(None, ("lon", "lat"), None),
        P(None, ("lon", "lat")),
        P(),
        P(),
        P(),
    )
    return jax.shard_map(
        on_device,
        mesh=mesh,
        in_specs=placed,
        out_specs=(P(None, ("lon", "lat"), None), P(("lon", "lat"), None)),
        check_vma=False,
    )
```

profile of v0, /device:TPU:0, one launch (start us, length us, event | category | flops | bytes accessed | tf_op | source)
XLA Modules:
  0.0 622.7 jit_solution(10093088314021235813)
XLA Ops:
  2.3 4.5 all-to-all-start
  15.0 6.0 collective-permute-start.1
  20.9 4.7 collective-permute-done
  31.5 2.3 collective-permute-done.2
  33.8 2.7 dynamic_update_slice.24
  36.6 3.0 collective-permute-start.3
  43.0 3.0 collective-permute-done.3
  46.0 2.7 dynamic_update_slice.25
  52.8 2.9 collective-permute-done.4
  55.7 2.7 dynamic_update_slice.26
  59.1 545.2 %while.15 = (s32[]{:T(128)}, f32[32,12,128]{2,1,0:T(8,128)}, f32[12,128]{1,0:T(8,128)S(1)}, s32[]{:T(128)}, f32[12,18304]{1,0:T(8,128)S(1)}, /*index=5*/f32[]{:T...) while((s32[]{:T(128)}, f32[32,12,128]{2,1,0:T(8,128)}, ...), condition=%wide.region_12.13_spmd, body=%wide.region_0.12_spmd.sunk | while | flops 2997504000 | bytes 128684592 | solution.py:94
  59.6 3.9 multiply_reduce_fusion.7
  63.5 5.2 copy.134
  70.0 6.5 %broadcast_add_fusion.2 = f32[4,512,512]{1,2,0:T(8,128)} fusion(f32[512,512]{0,1:T(8,128)S(1)} %copy.133, f32[]{:T(128)} %get-tuple-element.254, f32[4,512,512]{1,2,0:T(8,128)} %copy.134), kind=kLoop, calls=%fused_computation.16.clone.1 | loop fusion | flops 3145728 | bytes 9437188 | tf_op jit(solution)/shard_map/while/body/add | solution.py:51
  76.5 5.2 copy.135
  81.7 6.0 fusion.122
  87.7 1.9 copy-done
  89.7 46.9 %custom-call.52 = f32[4,128,128]{2,1,0:T(8,128)S(1)} custom-call(f32[4,128,128]{2,1,0:T(8,128)S(1)} %cholesky.395), custom_call_target="Cholesky" | custom-call | tf_op jit(solution)/shard_map/while/body/jit(cholesky)/cholesky | solution.py:52
  136.6 39.7 %custom-call.53 = f32[4,1,128,128]{2,3,1,0:T(8,128)S(1)} custom-call(f32[4,1,128,128]{3,2,1,0:T(8,128)S(1)} %select_bitcast_fusion.6), custom_call_target="InvertDiagBlocksLowerTriangular" | custom-call | tf_op jit(solution)/shard_map/while/body/jit(cholesky)/cholesky | solution.py:52
  176.3 2.5 cholesky.396
  178.9 2.9 constant_dynamic-update-slice_fusion.7
  181.8 2.0 convolution_subtract_fusion.12
  183.8 46.9 %custom-call.54 = f32[4,128,128]{2,1,0:T(8,128)S(1)} custom-call(f32[4,128,128]{2,1,0:T(8,128)S(1)} %cholesky.397), custom_call_target="Cholesky" | custom-call | tf_op jit(solution)/shard_map/while/body/jit(cholesky)/cholesky | solution.py:52
  231.4 39.3 %custom-call.55 = f32[4,1,128,128]{2,3,1,0:T(8,128)S(1)} custom-call(f32[4,1,128,128]{3,2,1,0:T(8,128)S(1)} %get-tuple-element.190), custom_call_target="InvertDiagBlocksLowerTriangular" | custom-call | tf_op jit(solution)/shard_map/while/body/jit(cholesky)/cholesky | solution.py:52
  270.7 1.5 convolution_dynamic-update-slice_fusion.4
  272.2 2.6 convolution_subtract_fusion.13
  274.9 47.1 %custom-call.56 = f32[4,128,128]{2,1,0:T(8,128)S(1)} custom-call(f32[4,128,128]{2,1,0:T(8,128)S(1)} %cholesky.398), custom_call_target="Cholesky" | custom-call | tf_op jit(solution)/shard_map/while/body/jit(cholesky)/cholesky | solution.py:52
  322.7 39.3 %custom-call.57 = f32[4,1,128,128]{2,3,1,0:T(8,128)S(1)} custom-call(f32[4,1,128,128]{3,2,1,0:T(8,128)S(1)} %get-tuple-element.192), custom_call_target="InvertDiagBlocksLowerTriangular" | custom-call | tf_op jit(solution)/shard_map/while/body/jit(cholesky)/cholesky | solution.py:52
  362.0 1.1 convolution_dynamic-update-slice_fusion.5
  363.1 2.6 convolution_subtract_fusion.14
  365.7 47.1 %custom-call.58 = f32[4,128,128]{2,1,0:T(8,128)S(1)} custom-call(f32[4,128,128]{2,1,0:T(8,128)S(1)} %convolution_subtract_fusion.14), custom_call_target="Cholesky" | custom-call | tf_op jit(solution)/shard_map/while/body/jit(cholesky)/cholesky | solution.py:52
  414.3 4.9 select_select_fusion.2
  419.2 12.2 %while.16 = (s32[]{:T(128)}, f32[4,512,512]{2,1,0:T(8,128)}, s32[4,2]{0,1:T(2,128)S(1)}, f32[4,4,128,128]{3,2,0,1:T(8,128)S(1)}, s32[]{:T(128)}) while((s32[]{:T(128)}, f32[4,512,512]{2,1,0:T(8,128)}, s32[4,2]{0,1:T(2,128)S(1)}, f32[4,4,128,128]{3,2,0,1:T(8,128)S(1)}, s32[]{:T(128)}) %tuple.62), condition=%wide.while_cond, body=%wide.while_body.sunk | while | flops 2 | bytes 524397 | solution.py:57
  419.9 2.4 bitcast_dynamic-update-slice_fusion.2
  422.9 2.4 bitcast_dynamic-update-slice_fusion.2
  426.0 2.4 bitcast_dynamic-update-slice_fusion.2
  429.1 2.3 bitcast_dynamic-update-slice_fusion.2
  431.4 157.2 %custom-call.60 = f32[4,4,128,128]{2,3,1,0:T(8,128)S(1)} custom-call(f32[4,4,128,128]{3,2,1,0:T(8,128)S(1)} %bitcast.156), custom_call_target="InvertDiagBlocksLowerTriangular" | custom-call | tf_op jit(solution)/shard_map/while/body/triangular_solve | solution.py:57
  589.4 1.0 multiply_reduce_fusion.6
  590.8 1.0 divide_exponential_fusion.3
  592.3 1.6 convolution_subtract_fusion.15
  594.4 1.8 convolution_subtract_fusion.16
  596.6 2.3 convolution_subtract_fusion.17
  599.4 1.1 convolution_bitcast_fusion.2
  607.0 2.6 collective-permute-done.5
  610.0 3.6 collective-permute-start.6
  614.2 1.7 collective-permute-done.6
  617.6 2.9 collective-permute-done.7
  (111 shorter events, 31.1 us)
Async XLA Ops:
  2.3 12.5 %all-to-all-start = ((f32[2,35,8,128]{3,2,1,0:T(8,128)}), f32[2,35,8,128]{3,2,1,0:T(8,128)S(1)}, u32[]{:S(2)}, u32[]{:S(2)}) async-start(f32[2,35,8,128]{3,2,1,0:T(8,128)} %broadcast_in_dim.68), calls=%async_computation | async-start | bytes 573440 | tf_op jit(solution)/shard_map/all_to_all | solution.py:9
  6.8 19.7 %copy-start.3 = (f32[3,8,128]{2,1,0:T(8,128)S(1)}, f32[3,8,128]{2,1,0:T(8,128)}, u32[]{:S(2)}) copy-start(f32[3,8,128]{2,1,0:T(8,128)} %param.8) | copy-start | bytes 36868
  14.9 10.8 %collective-permute-start = (f32[35,16,128]{2,0,1:T(8,128)S(1)}, f32[35,16,128]{2,0,1:T(8,128)S(1)}, u32[]{:S(2)}, u32[]{:S(2)}) collective-permute-start(f32[35,16,128]{2,0,1:T(8,128)S(1)} %copy.91), channel_id=1, source_target_pairs={{0,2},{2,4},{4,6},{6,8},{8,10},{10,12},{12,14},{14,16},{16,18},{18... | collective-permute-start | bytes 860168 | tf_op jit(solution)/shard_map/ppermute | solution.py:32
  15.0 10.7 %collective-permute-start.1 = (f32[35,16,128]{2,0,1:T(8,128)S(1)}, f32[35,16,128]{2,0,1:T(8,128)S(1)}, u32[]{:S(2)}, u32[]{:S(2)}) collective-permute-start(f32[35,16,128]{2,0,1:T(8,128)S(1)} %copy.91), channel_id=1, source_target_pairs={{2,0},{4,2},{6,4},{8,6},{10,8},{12,10},{14,12},{16,14},{18,16},{20... | collective-permute-start | bytes 860168 | tf_op jit(solution)/shard_map/ppermute | solution.py:34
  26.8 7.1 %collective-permute-start.2 = (f32[4,18304]{1,0:T(4,128)S(1)}, f32[4,18304]{1,0:T(4,128)S(1)}, u32[]{:S(2)}, u32[]{:S(2)}) collective-permute-start(f32[4,18304]{1,0:T(4,128)S(1)} %constant_dynamic-slice_fusion.6), channel_id=1, source_target_pairs={{0,16},{2,18},{4,20},{6,22},{8,24},{10,26},{12,28},{14,30},{16,0},... | collective-permute-start | bytes 878600 | tf_op jit(solution)/shard_map/ppermute | solution.py:44
  36.6 9.4 %collective-permute-start.3 = (f32[4,18304]{1,0:T(4,128)S(1)}, f32[4,18304]{1,0:T(4,128)S(1)}, u32[]{:S(2)}, u32[]{:S(2)}) collective-permute-start(f32[4,18304]{1,0:T(4,128)S(1)} %constant_dynamic-slice_fusion.5), channel_id=1, source_target_pairs={{0,32},{2,34},{4,36},{6,38},{8,40},{10,42},{12,44},{14,46},{16,48}... | collective-permute-start | bytes 878600 | tf_op jit(solution)/shard_map/ppermute | solution.py:44
  48.7 7.0 %collective-permute-start.4 = (f32[4,18304]{1,0:T(4,128)S(1)}, f32[4,18304]{1,0:T(4,128)S(1)}, u32[]{:S(2)}, u32[]{:S(2)}) collective-permute-start(f32[4,18304]{1,0:T(4,128)S(1)} %constant_dynamic-slice_fusion.4), channel_id=1, source_target_pairs={{0,64},{2,66},{4,68},{6,70},{8,72},{10,74},{12,76},{14,78},{16,80}... | collective-permute-start | bytes 878600 | tf_op jit(solution)/shard_map/ppermute | solution.py:44
  59.1 554.5 %copy-start.4 = (s32[128]{0:T(128)S(1)}, s32[128]{0:T(128)}, u32[]{:S(2)}) copy-start(s32[128]{0:T(128)} %param.11) | copy-start | bytes 1540
  59.3 9.5 %copy-start.1 = (f32[12,18304]{1,0:T(8,128)}, f32[12,18304]{1,0:T(8,128)S(1)}, u32[]{:S(2)}) copy-start(f32[12,18304]{1,0:T(8,128)S(1)} %get-tuple-element.253) | copy-start | bytes 2635780 | tf_op jit(solution)/shard_map/while
  87.7 1.9 copy-start
  598.9 2.6 copy-start.2
  605.3 4.4 collective-permute-start.5
  610.0 5.9 collective-permute-start.6
  616.1 4.4 collective-permute-start.7
where the time goes:
time: 630 us; the launch traced here: 623 us
  other arithmetic  497 us (79%)
  local copies, waits for them, and re-layouts  49.2 us (8%)
  matrix products  21.2 us (3%)
  waiting for transfers between devices  20.1 us (3%)
  starting transfers between devices  19.7 us (3%)
  between operations  12.1 us (2%)
    another operation x18, other arithmetic, solve_group(): factor = jnp.linalg.cholesky(cov)  309 us
    another operation x5, other arithmetic, solve_group(): lax.linalg.triangular_solve(factor, rhs, left_side=True, lower=True)  162 us
    ppermute x6, waiting for transfers between devices, partner(): return lax.ppermute(value, axis, pairs)  15.4 us
    another operation x6, matrix products, solve_group(): factor = jnp.linalg.cholesky(cov)  12.7 us
  transfers between devices with their start and end apart: 9, of which 7 were waited for; matrix products, arithmetic and copies ran while one was open for 2% of the time, Pallas kernels for 0%

commit v1 on v0

v1 whole, which is shorter than its diff:
```python
import jax
import jax.numpy as jnp
from jax import lax
from jax.experimental import pallas as pl
from jax.experimental.pallas import tpu as pltpu
from jax.sharding import PartitionSpec as P

HIGHEST = lax.Precision.HIGHEST
LEAF = 16
TASKS = 3
NBR = 4
NF = 32
W = 128
SLOTS = 8
SHIP = SLOTS - TASKS
F32 = jnp.float32

VMEM = pl.BlockSpec(memory_space=pltpu.VMEM)
SMEM = pl.BlockSpec(memory_space=pltpu.SMEM)


def params():
    return pltpu.CompilerParams(vmem_limit_bytes=40 * 2**20)


def mm(a, b):
    return lax.dot_general(
        a, b, (((1,), (0,)), ((), ())), precision=HIGHEST, preferred_element_type=F32
    )


def mmt(a, b):
    return lax.dot_general(
        a, b, (((1,), (1,)), ((), ())), precision=HIGHEST, preferred_element_type=F32
    )


def recip(p):
    r = pl.reciprocal(p, approx=True)
    r = r * (2.0 - p * r)
    return r * (2.0 - p * r)


def sweep(panel, off, rows, lanes):
    cols = [
        jnp.broadcast_to(panel[:, off + c : off + c + 1], (LEAF, W)) for c in range(LEAF)
    ]
    for i in range(LEAF):
        r = recip(jnp.broadcast_to(cols[i][i : i + 1], (LEAF, W)))
        here = rows == i
        m = jnp.where(here, 1.0 - r, cols[i] * r)
        panel = jnp.where(lanes == off + i, jnp.where(here, 1.0, 0.0), panel)
        panel = panel - m * jnp.broadcast_to(panel[i : i + 1], (LEAF, W))
        for c in range(i + 1, LEAF):
            cols[c] = cols[c] - m * jnp.broadcast_to(cols[c][i : i + 1], (LEAF, W))
    return panel


def invert(tiles):
    rows = lax.broadcasted_iota(jnp.int32, (LEAF, W), 0)
    lanes = lax.broadcasted_iota(jnp.int32, (LEAF, W), 1)
    down = lax.broadcasted_iota(jnp.int32, (W, W), 0)
    along = lax.broadcasted_iota(jnp.int32, (W, W), 1)
    for off in range(0, W, LEAF):
        swept = [sweep(t[off : off + LEAF], off, rows, lanes) for t in tiles]
        new = []
        for t, q in zip(tiles, swept):
            low, high = off, W - off - LEAF
            wide = jnp.concatenate(
                [
                    x
                    for x in (jnp.zeros((low, W), F32), q, jnp.zeros((high, W), F32))
                    if x.shape[0]
                ],
                0,
            )
            in_rows = (down >= off) & (down < off + LEAF)
            in_cols = (along >= off) & (along < off + LEAF)
            others = jnp.where(in_rows, 0.0, t)
            u = jnp.where(in_cols, 0.0, others) - mm(others, wide)
            new.append(
                jnp.concatenate(
                    [x for x in (u[:off], q, u[off + LEAF :]) if x.shape[0]], 0
                )
            )
        tiles = new
    return tiles


def pool_row(block, my_band, my_sub, bands):
    band = block // (2 * SLOTS)
    sub = (block // SLOTS) % 2
    side = (band - my_band + 1 + bands) % bands
    flip = jnp.where(sub == my_sub, 0, 1)
    return (side * 2 + flip) * SLOTS + block % SLOTS


def pack_points(bands, nb, *refs):
    pools, own, ships, pool = refs[:6], refs[6], refs[7:-1], refs[-1]
    band, sub = lax.axis_index("lon"), lax.axis_index("lat")
    for g in range(6):
        pool[:, g * SLOTS : (g + 1) * SLOTS, :] = pools[g][...]
    for s in range(SLOTS):
        dst = own.at[s] if s < TASKS else ships[s - TASKS]
        for d in range(3):
            dst[d] = jnp.zeros((8, W), F32)
        for n in range(NBR):
            row = pool_row(nb[n, s], band, sub, bands)
            dst[:, n : n + 1, :] = pool[:, pl.ds(row, 1), :]
        dst[:, NBR : NBR + 1, :] = pools[2][:, s : s + 1, :]


def pack_values(bands, nb, *refs):
    pools, own, ships, pool = refs[:6], refs[6], refs[7:-1], refs[-1]
    band, sub = lax.axis_index("lon"), lax.axis_index("lat")
    for g in range(6):
        pool[:, g * SLOTS : (g + 1) * SLOTS, :] = pools[g][...]
    for s in range(SLOTS):
        dst = own.at[s] if s < TASKS else ships[s - TASKS]
        for n in range(NBR):
            row = pool_row(nb[n, s], band, sub, bands)
            dst[n] = pool[:, pl.ds(row, 1), :].reshape(NF, W)


def for_third(counts, bands, own_third, ships, use):
    band, sub = lax.axis_index("lon"), lax.axis_index("lat")
    apart = bands // SLOTS
    for k in range(SHIP):
        giver = (band - (k + 1) * apart + bands) % bands

        @pl.when(counts[giver * 2 + sub] > TASKS - 1)
        def _():
            use(ships[k][...])

    del apart
    return band, sub


def factor(bands, counts, scale, nugget, own, *refs):
    ships, coef, var, pts, tiles, diag = refs[:SHIP], refs[SHIP], refs[SHIP + 1], *refs[SHIP + 2 :]
    pts[...] = own[...]

    def put(x):
        pts[TASKS - 1] = x

    for_third(counts, bands, None, ships, put)
    down = lax.broadcasted_iota(jnp.int32, (W, W), 0)
    along = lax.broadcasted_iota(jnp.int32, (W, W), 1)
    minus = jnp.full((W, W), -1.0, F32) / scale[0]
    noise = jnp.where(down == along, nugget[0], 0.0)
    ones = jnp.ones((8, W), F32)

    def build(s, carry):
        rows = [pts[s, d] for d in range(3)]
        cols = [r.T for r in rows]
        for a in range(NBR + 1):
            mine = [jnp.broadcast_to(c[:, a : a + 1], (W, W)) for c in cols]
            for b in range(min(a, NBR - 1) + 1):
                total = None
                for d in range(3):
                    gap = mine[d] - jnp.broadcast_to(rows[d][b : b + 1], (W, W))
                    total = gap * gap if total is None else total + gap * gap
                value = jnp.exp(jnp.sqrt(total) * minus)
                if a == b:
                    value = value + noise
                tiles[s, a, b] = value
        var[s] = ones
        return carry

    lax.fori_loop(0, TASKS, build, 0)

    def eliminate(j, carry):
        for s, g in enumerate(invert([tiles[s, j, j] for s in range(TASKS)])):
            diag[s] = g
        for at in range(NBR):

            @pl.when(j == at)
            def _():
                def one(s, inner):
                    g = diag[s]
                    d = tiles[s, at, at]
                    left = {}
                    for a in range(at + 1, NBR + 1):
                        given = tiles[s, a, at]
                        v = mm(given, g)
                        left[a] = v + mm(given - mm(v, d), g)
                    for b in range(at + 1, NBR):
                        for a in range(b, NBR + 1):
                            tiles[s, a, b] = tiles[s, a, b] - mmt(left[a], tiles[s, b, at])
                    var[s] = var[s] - mmt(ones, left[NBR] * tiles[s, NBR, at])
                    for a in range(at + 1, NBR + 1):
                        tiles[s, a, at] = left[a]
                    return inner

                lax.fori_loop(0, TASKS, one, 0)

        return carry

    lax.fori_loop(0, NBR, eliminate, 0)

    def back(s, carry):
        done = [None] * NBR
        for at in range(NBR - 1, -1, -1):
            x = tiles[s, NBR, at]
            for a in range(at + 1, NBR):
                x = x - mm(done[a], tiles[s, a, at])
            done[at] = x
            coef[s, at] = x
        return carry

    lax.fori_loop(0, TASKS, back, 0)


def combine(bands, counts, coef, var, own, *refs):
    ships, kept, sent, values = refs[:SHIP], refs[SHIP], refs[SHIP + 1], refs[SHIP + 2]
    values[...] = own[TASKS - 1]

    def put(x):
        values[...] = x

    for_third(counts, bands, None, ships, put)
    for s in range(TASKS):
        total = None
        for n in range(NBR):
            y = values[n] if s == TASKS - 1 else own[s, n]
            part = mmt(y, coef[s, n])
            total = part if total is None else total + part
        dst = sent if s == TASKS - 1 else kept.at[s]
        dst[:NF] = total
        dst[NF:] = var[s]


def assemble(bands, counts, kept, third, *refs):
    backs, predicted, variance = refs[:SHIP], refs[SHIP], refs[SHIP + 1]
    band, sub = lax.axis_index("lon"), lax.axis_index("lat")
    alive = counts[band * 2 + sub]
    for s in range(SLOTS):
        src = kept[s] if s < TASKS - 1 else third[...] if s < TASKS else backs[s - TASKS][...]
        src = jnp.where(s < alive, src, 0.0)
        predicted[:, s : s + 1, :] = src[:NF].reshape(NF, 1, W)
        variance[s : s + 1, :] = src[NF : NF + 1]


def arr(*shape):
    return jax.ShapeDtypeStruct(shape, F32)


def cost(flops, bytes_accessed):
    return pl.CostEstimate(flops=flops, bytes_accessed=bytes_accessed, transcendentals=0)


def on_device(bands, coords, observed, neighbours, counts, lengthscale, nugget):
    axes = ("lon", "lat")
    total = bands * 2
    apart = bands // SLOTS

    def shift(x, lon, flip):
        pairs = [
            (l * 2 + h, ((l + lon) % bands) * 2 + (h ^ flip))
            for l in range(bands)
            for h in range(2)
        ]
        return lax.ppermute(x, axes, pairs)

    def pool_of(x):
        return [
            x if (away, flip) == (0, 0) else shift(x, -away, flip)
            for away in (-1, 0, 1)
            for flip in (0, 1)
        ]

    def ship(parts):
        return [shift(p, (k + 1) * apart, 0) for k, p in enumerate(parts)]

    point_pool = pool_of(coords)
    value_pool = pool_of(observed)
    own_points, *out_points = pl.pallas_call(
        lambda *r: pack_points(bands, *r),
        out_shape=[arr(TASKS, 3, 8, W)] + [arr(3, 8, W)] * SHIP,
        in_specs=[SMEM] + [VMEM] * 6,
        out_specs=[VMEM] * (1 + SHIP),
        scratch_shapes=[pltpu.VMEM((3, 6 * SLOTS, W), F32)],
        compiler_params=params(),
        name="pack_points",
    )(neighbours, *point_pool)
    in_points = ship(out_points)
    own_values, *out_values = pl.pallas_call(
        lambda *r: pack_values(bands, *r),
        out_shape=[arr(TASKS, NBR, NF, W)] + [arr(NBR, NF, W)] * SHIP,
        in_specs=[SMEM] + [VMEM] * 6,
        out_specs=[VMEM] * (1 + SHIP),
        scratch_shapes=[pltpu.VMEM((NF, 6 * SLOTS, W), F32)],
        compiler_params=params(),
        name="pack_values",
    )(neighbours, *value_pool)
    in_values = ship(out_values)
    coef, var = pl.pallas_call(
        lambda *r: factor(bands, *r),
        out_shape=[arr(TASKS, NBR, W, W), arr(TASKS, 8, W)],
        in_specs=[SMEM] * 3 + [VMEM] * (1 + SHIP),
        out_specs=[VMEM] * 2,
        scratch_shapes=[
            pltpu.VMEM((TASKS, 3, 8, W), F32),
            pltpu.VMEM((TASKS, NBR + 1, NBR, W, W), F32),
            pltpu.VMEM((TASKS, W, W), F32),
        ],
        compiler_params=params(),
        cost_estimate=cost(10**10, 10**7),
        name="factor",
    )(counts, lengthscale, nugget, own_points, *in_points)
    kept, third = pl.pallas_call(
        lambda *r: combine(bands, *r),
        out_shape=[arr(TASKS - 1, NF + 8, W), arr(NF + 8, W)],
        in_specs=[SMEM] + [VMEM] * (3 + SHIP),
        out_specs=[VMEM] * 2,
        scratch_shapes=[pltpu.VMEM((NBR, NF, W), F32)],
        compiler_params=params(),
        name="combine",
    )(counts, coef, var, own_values, *in_values)
    backs = [shift(third, -(k + 1) * apart, 0) for k in range(SHIP)]
    return pl.pallas_call(
        lambda *r: assemble(bands, *r),
        out_shape=[arr(NF, SLOTS, W), arr(SLOTS, W)],
        in_specs=[SMEM] + [VMEM] * (2 + SHIP),
        out_specs=[VMEM] * 2,
        compiler_params=params(),
        name="assemble",
    )(counts, kept, third, *backs)


def solution(mesh):
    bands = mesh.shape["lon"]
    placed = (
        P(None, ("lon", "lat"), None),
        P(None, ("lon", "lat"), None),
        P(None, ("lon", "lat")),
        P(),
        P(),
        P(),
    )

    def step(*args):
        return tuple(on_device(bands, *args))

    return jax.shard_map(
        step,
        mesh=mesh,
        in_specs=placed,
        out_specs=(P(None, ("lon", "lat"), None), P(("lon", "lat"), None)),
        check_vma=False,
    )
```

time: 630 us -> 113 us (0.18); the launches traced: 623 us -> 113 us
  other arithmetic: 497 us -> 0 us
  Pallas kernels: 0 us -> 58 us
  local copies, waits for them, and re-layouts: 49.2 us -> 2.94 us
  starting transfers between devices: 19.7 us -> 45.7 us
  matrix products: 21.2 us -> 0 us
  waiting for transfers between devices: 20.1 us -> 4.38 us
  between operations: 12.1 us -> 2.07 us
    another operation x23 -> x0, other arithmetic: 472 us -> none  [the longest x18 309 us: solve_group(): factor = jnp.linalg.cholesky(cov)]
    pallas_call x0 -> x5, Pallas kernels: none -> 58 us  [the longest x1 52.2 us: on_device(): pl.pallas_call(lambda *r: factor(bands, *r), out_shape=[arr(TASKS, NBR, W...]
    ppermute x8 -> x25, starting transfers between devices: 15.1 us -> 45.7 us  [shift(): return lax.ppermute(x, axes, pairs)]
    another operation x13 -> x0, matrix products: 20.1 us -> none  [the longest x6 12.7 us: solve_group(): factor = jnp.linalg.cholesky(cov)]
    ppermute x8 -> x25, waiting for transfers between devices: 20.1 us -> 4.38 us  [shift(): return lax.ppermute(x, axes, pairs)]
    another operation x17 -> x0, local copies, waits for them, and re-layouts: 14.7 us -> none
    dynamic_update_slice x7 -> x0, local copies, waits for them, and re-layouts: 9.36 us -> none  [the longest x3 7.97 us: on_device(): work = lax.dynamic_update_slice_in_dim(work, incoming, mine, 0)]
    add x4 -> x0, other arithmetic: 6.51 us -> none  [the longest x1 6.46 us: solve_group(): cov = jnp.exp(-dist / scale) + noise * jnp.eye(count, dtype=jnp.float32)]
  transfers between devices with their start and end apart: 9 -> 25, of which waited for: 7 -> 5; matrix products, arithmetic and copies ran while one was open for 2% -> 0% of each run, Pallas kernels for 0% -> 48%
where the time goes in v1:
time: 113 us
  Pallas kernels  58 us (51%)
  starting transfers between devices  45.7 us (40%)
  waiting for transfers between devices  4.38 us (4%)
  local copies, waits for them, and re-layouts  2.94 us (3%)
  between operations  2.07 us (2%)
    pallas_call x1, Pallas kernels, on_device(): pl.pallas_call(lambda *r: factor(bands, *r), out_shape=[arr(TASKS, NBR, W...  52.2 us
    ppermute x25, starting transfers between devices, shift(): return lax.ppermute(x, axes, pairs)  45.7 us
    ppermute x25, waiting for transfers between devices, shift(): return lax.ppermute(x, axes, pairs)  4.38 us
    unnamed x8, local copies, waits for them, and re-layouts  2.94 us
  transfers between devices with their start and end apart: 25, of which 5 were waited for; matrix products, arithmetic and copies ran while one was open for 0% of the time, Pallas kernels for 48%

profile of v1, /device:TPU:0, one launch (start us, length us, event | category | flops | bytes accessed | tf_op | source)
XLA Modules:
  0.0 113.1 jit_solution(9344795087299040629)
XLA Ops:
  0.6 6.8 %collective-permute-start.3 = (f32[3,8,128]{2,1,0:T(8,128)}, f32[3,8,128]{2,1,0:T(8,128)S(1)}, u32[]{:S(2)}, u32[]{:S(2)}) collective-permute-start(f32[3,8,128]{2,1,0:T(8,128)} %r_3_.2), channel_id=1, source_target_pairs={{0,126},{1,127},{2,0},{3,1},{4,2},{5,3},{6,4},{7,5},{8,6},{9,7},{1... | collective-permute-start | bytes 36872 | tf_op jit(solution)/shard_map/ppermute | solution.py:263
  7.5 2.9 %collective-permute-start.2 = (f32[3,8,128]{2,1,0:T(8,128)}, f32[3,8,128]{2,1,0:T(8,128)S(1)}, u32[]{:S(2)}, u32[]{:S(2)}) collective-permute-start(f32[3,8,128]{2,1,0:T(8,128)} %r_3_.2), channel_id=1, source_target_pairs={{0,1},{1,0},{2,3},{3,2},{4,5},{5,4},{6,7},{7,6},{8,9},{9,8},{10,11... | collective-permute-start | bytes 36872 | tf_op jit(solution)/shard_map/ppermute | solution.py:263
  10.4 0.0 collective-permute-start.1
  10.4 0.0 collective-permute-start
  10.4 7.2 %collective-permute-start.4 = (f32[3,8,128]{2,1,0:T(8,128)}, f32[3,8,128]{2,1,0:T(8,128)S(1)}, u32[]{:S(2)}, u32[]{:S(2)}) collective-permute-start(f32[3,8,128]{2,1,0:T(8,128)} %r_3_.2), channel_id=1, source_target_pairs={{0,127},{1,126},{2,1},{3,0},{4,3},{5,2},{6,5},{7,4},{8,7},{9,6},{1... | collective-permute-start | bytes 36872 | tf_op jit(solution)/shard_map/ppermute | solution.py:263
  17.5 0.0 collective-permute-done.3.r_5_
  17.5 1.0 collective-permute-start.13
  18.5 0.0 collective-permute-done.2.r_4_
  18.5 0.6 collective-permute-start.12
  19.2 0.1 collective-permute-done.1.r_2_
  19.3 1.7 %collective-permute-start.11 = (f32[32,8,128]{2,1,0:T(8,128)}, f32[32,8,128]{2,1,0:T(8,128)S(1)}, u32[]{:S(2)}, u32[]{:S(2)}) collective-permute-start(f32[32,8,128]{2,1,0:T(8,128)} %r_3_.3), channel_id=1, source_target_pairs={{0,3},{1,2},{2,5},{3,4},{4,7},{5,6},{6,9},{7,8},{8,11},{9,10},{10,... | collective-permute-start | bytes 393224 | tf_op jit(solution)/shard_map/ppermute | solution.py:263
  20.9 0.0 collective-permute-done.r_1_
  20.9 0.0 collective-permute-start.10
  20.9 5.7 %collective-permute-start.14 = (f32[32,8,128]{2,1,0:T(8,128)}, f32[32,8,128]{2,1,0:T(8,128)S(1)}, u32[]{:S(2)}, u32[]{:S(2)}) collective-permute-start(f32[32,8,128]{2,1,0:T(8,128)} %r_3_.3), channel_id=1, source_target_pairs={{0,127},{1,126},{2,1},{3,0},{4,3},{5,2},{6,5},{7,4},{8,7},{9,6},{1... | collective-permute-start | bytes 393224 | tf_op jit(solution)/shard_map/ppermute | solution.py:263
  26.6 0.7 copy-done.1
  27.4 0.7 copy-done.2
  28.0 1.1 pack_points.1
  29.1 0.1 collective-permute-start.5
  29.2 0.0 collective-permute-done.12.r_4_
  29.2 0.1 collective-permute-start.6
  29.3 0.5 collective-permute-done.11.r_2_
  29.8 2.3 %collective-permute-start.7 = (f32[3,8,128]{2,1,0:T(8,128)S(1)}, f32[3,8,128]{2,1,0:T(8,128)S(1)}, u32[]{:S(2)}, u32[]{:S(2)}) collective-permute-start(f32[3,8,128]{2,1,0:T(8,128)S(1)} %get-tuple-element.21), channel_id=1, source_target_pairs={{0,48},{1,49},{2,50},{3,51},{4,52},{5,53},{6,54},{7,55},{8,56},{9,... | collective-permute-start | bytes 36872 | tf_op jit(solution)/shard_map/ppermute | solution.py:263
  32.1 0.0 collective-permute-done.10.r_1_
  32.1 1.9 %collective-permute-start.8 = (f32[3,8,128]{2,1,0:T(8,128)S(1)}, f32[3,8,128]{2,1,0:T(8,128)S(1)}, u32[]{:S(2)}, u32[]{:S(2)}) collective-permute-start(f32[3,8,128]{2,1,0:T(8,128)S(1)} %get-tuple-element.22), channel_id=1, source_target_pairs={{0,64},{1,65},{2,66},{3,67},{4,68},{5,69},{6,70},{7,71},{8,72},{9,... | collective-permute-start | bytes 36872 | tf_op jit(solution)/shard_map/ppermute | solution.py:263
  34.0 0.0 collective-permute-done.14.r_6_
  34.0 0.4 collective-permute-start.9
  35.7 0.0 copy-start
  35.7 0.9 copy-done
  36.6 1.2 %pack_values.1 = (f32[3,4,32,128]{3,2,1,0:T(8,128)S(1)}, f32[4,32,128]{2,1,0:T(8,128)S(1)}, f32[4,32,128]{2,1,0:T(8,128)S(1)}, f32[4,32,128]{2,1,0:T(8,128)S(1)}...) custom-call(s32[4,8]{1,0:T(4,128)S(1)} %copy-done.2, f32[32,8,128]{2,1,0:T(8,128)S(1)} %collective-permute-done.10.r_1_, ...), custom_call_target="tpu_custom_call" | custom-call | tf_op jit(solution)/shard_map/pack_values/pallas_call | solution.py:287
  37.9 0.0 collective-permute-done.5.r_4_
  37.9 3.3 %collective-permute-start.15 = (f32[4,32,128]{2,1,0:T(8,128)S(1)}, f32[4,32,128]{2,1,0:T(8,128)S(1)}, u32[]{:S(2)}, u32[]{:S(2)}) collective-permute-start(f32[4,32,128]{2,1,0:T(8,128)S(1)} %get-tuple-element.27), channel_id=1, source_target_pairs={{0,16},{1,17},{2,18},{3,19},{4,20},{5,21},{6,22},{7,23},{8,24},{9,... | collective-permute-start | bytes 196616 | tf_op jit(solution)/shard_map/ppermute | solution.py:263
  41.2 1.0 collective-permute-start.16
  42.2 0.0 collective-permute-done.7.r_6_
  42.2 1.7 %collective-permute-start.17 = (f32[4,32,128]{2,1,0:T(8,128)S(1)}, f32[4,32,128]{2,1,0:T(8,128)S(1)}, u32[]{:S(2)}, u32[]{:S(2)}) collective-permute-start(f32[4,32,128]{2,1,0:T(8,128)S(1)} %get-tuple-element.29), channel_id=1, source_target_pairs={{0,48},{1,49},{2,50},{3,51},{4,52},{5,53},{6,54},{7,55},{8,56},{9,... | collective-permute-start | bytes 196616 | tf_op jit(solution)/shard_map/ppermute | solution.py:263
  43.9 1.5 %collective-permute-start.18 = (f32[4,32,128]{2,1,0:T(8,128)S(1)}, f32[4,32,128]{2,1,0:T(8,128)S(1)}, u32[]{:S(2)}, u32[]{:S(2)}) collective-permute-start(f32[4,32,128]{2,1,0:T(8,128)S(1)} %get-tuple-element.30), channel_id=1, source_target_pairs={{0,64},{1,65},{2,66},{3,67},{4,68},{5,69},{6,70},{7,71},{8,72},{9,... | collective-permute-start | bytes 196616 | tf_op jit(solution)/shard_map/ppermute | solution.py:263
  45.5 0.0 collective-permute-start.19
  45.5 0.6 copy-done.3
  46.1 52.2 %factor.1 = (f32[3,4,128,128]{3,2,1,0:T(8,128)S(1)}, f32[3,8,128]{2,1,0:T(8,128)S(1)}) custom-call(s32[128]{0:T(128)S(1)} %copy-done.3, f32[1]{0:T(128)S(6)} %copy.8.r_1_, f32[1]{0:T(128)S(6)} %copy.9.r_2_, f32[3,3,8,128]{3,2,1,0:T(8,128)S(1)} %get-tuple-element.18.r_3_, f32[3,8,128]{2,1,0:T(8,128)S(1)} %collective-permute-done.5.r_4_, ...), custom_call_target="tpu_custom_call" | custom-call | flops 10000000000 | bytes 10000000 | tf_op jit(solution)/shard_map/factor/pallas_call | solution.py:297
  98.4 0.0 collective-permute-done.17.r_6_
  98.4 2.2 %combine.1 = (f32[2,40,128]{2,1,0:T(8,128)S(1)}, f32[40,128]{1,0:T(8,128)S(1)}) custom-call(s32[128]{0:T(128)S(1)} %copy-done.3, f32[3,4,128,128]{3,2,1,0:T(8,128)S(1)} %get-tuple-element.24.r_1_, f32[3,8,128]{2,1,0:T(8,128)S(1)} %get-tuple-element.25.r_2_, f32[3,4,32,128]{3,2,1,0:T(8,128)S(1)} %get-tuple-element.26.r_3_, ...), custom_call_target="tpu_custom_call" | custom-call | tf_op jit(solution)/shard_map/combine/pallas_call | solution.py:311
  100.6 2.6 %collective-permute-start.24 = (f32[40,128]{1,0:T(8,128)S(1)}, f32[40,128]{1,0:T(8,128)S(1)}, u32[]{:S(2)}, u32[]{:S(2)}) collective-permute-start(f32[40,128]{1,0:T(8,128)S(1)} %get-tuple-element.33.r_2_), channel_id=1, source_target_pairs={{0,48},{1,49},{2,50},{3,51},{4,52},{5,53},{6,54},{7,55},{8,56},{9,... | collective-permute-start | bytes 61448 | tf_op jit(solution)/shard_map/ppermute | solution.py:263
  103.2 0.5 collective-permute-start.23
  103.6 0.9 collective-permute-start.22
  104.6 3.4 %collective-permute-start.21 = (f32[40,128]{1,0:T(8,128)S(1)}, f32[40,128]{1,0:T(8,128)S(1)}, u32[]{:S(2)}, u32[]{:S(2)}) collective-permute-start(f32[40,128]{1,0:T(8,128)S(1)} %get-tuple-element.33.r_2_), channel_id=1, source_target_pairs={{0,96},{1,97},{2,98},{3,99},{4,100},{5,101},{6,102},{7,103},{8,104... | collective-permute-start | bytes 61448 | tf_op jit(solution)/shard_map/ppermute | solution.py:263
  108.0 0.6 collective-permute-done.22.r_5_
  108.6 1.2 %collective-permute-done.21.r_4_ = f32[40,128]{1,0:T(8,128)S(1)} collective-permute-done((f32[40,128]{1,0:T(8,128)S(1)}, f32[40,128]{1,0:T(8,128)S(1)}, u32[]{:S(2)}, u32[]{:S(2)}) %collective-permute-start.21) | collective-permute-done | bytes 20512 | tf_op jit(solution)/shard_map/ppermute | solution.py:263
  109.9 1.9 %collective-permute-done.20.r_3_ = f32[40,128]{1,0:T(8,128)S(1)} collective-permute-done((f32[40,128]{1,0:T(8,128)S(1)}, f32[40,128]{1,0:T(8,128)S(1)}, u32[]{:S(2)}, u32[]{:S(2)}) %collective-permute-start.20) | collective-permute-done | bytes 20512 | tf_op jit(solution)/shard_map/ppermute | solution.py:263
  111.8 1.3 %assemble.1 = (f32[32,8,128]{2,1,0:T(8,128)}, f32[8,128]{1,0:T(8,128)}) custom-call(s32[128]{0:T(128)S(1)} %copy-done.3, f32[2,40,128]{2,1,0:T(8,128)S(1)} %get-tuple-element.32.r_1_, f32[40,128]{1,0:T(8,128)S(1)} %get-tuple-element.33.r_2_, f32[40,128]{1,0:T(8,128)S(1)} %collective-permute-done.20.r_3_, f32[40,128]{1,0:T(8,128)S(1)} %collective-permute-done.21.r_4_, ...), custom_call_target="tpu_custom_call" | custom-call | tf_op jit(solution)/shard_map/assemble/pallas_call | solution.py:321
  (15 shorter events, 0.0 us)
Async XLA Ops:
  0.6 16.9 %collective-permute-start.3 = (f32[3,8,128]{2,1,0:T(8,128)}, f32[3,8,128]{2,1,0:T(8,128)S(1)}, u32[]{:S(2)}, u32[]{:S(2)}) collective-permute-start(f32[3,8,128]{2,1,0:T(8,128)} %r_3_.2), channel_id=1, source_target_pairs={{0,126},{1,127},{2,0},{3,1},{4,2},{5,3},{6,4},{7,5},{8,6},{9,7},{1... | collective-permute-start | bytes 36872 | tf_op jit(solution)/shard_map/ppermute | solution.py:263
  7.5 11.1 %collective-permute-start.2 = (f32[3,8,128]{2,1,0:T(8,128)}, f32[3,8,128]{2,1,0:T(8,128)S(1)}, u32[]{:S(2)}, u32[]{:S(2)}) collective-permute-start(f32[3,8,128]{2,1,0:T(8,128)} %r_3_.2), channel_id=1, source_target_pairs={{0,1},{1,0},{2,3},{3,2},{4,5},{5,4},{6,7},{7,6},{8,9},{9,8},{10,11... | collective-permute-start | bytes 36872 | tf_op jit(solution)/shard_map/ppermute | solution.py:263
  10.4 8.9 %collective-permute-start.1 = (f32[3,8,128]{2,1,0:T(8,128)}, f32[3,8,128]{2,1,0:T(8,128)S(1)}, u32[]{:S(2)}, u32[]{:S(2)}) collective-permute-start(f32[3,8,128]{2,1,0:T(8,128)} %r_3_.2), channel_id=1, source_target_pairs={{0,3},{1,2},{2,5},{3,4},{4,7},{5,6},{6,9},{7,8},{8,11},{9,10},{10,... | collective-permute-start | bytes 36872 | tf_op jit(solution)/shard_map/ppermute | solution.py:263
  10.4 10.6 %collective-permute-start = (f32[3,8,128]{2,1,0:T(8,128)}, f32[3,8,128]{2,1,0:T(8,128)S(1)}, u32[]{:S(2)}, u32[]{:S(2)}) collective-permute-start(f32[3,8,128]{2,1,0:T(8,128)} %r_3_.2), channel_id=1, source_target_pairs={{0,2},{1,3},{2,4},{3,5},{4,6},{5,7},{6,8},{7,9},{8,10},{9,11},{10,... | collective-permute-start | bytes 36872 | tf_op jit(solution)/shard_map/ppermute | solution.py:263
  10.4 10.6 %collective-permute-start.4 = (f32[3,8,128]{2,1,0:T(8,128)}, f32[3,8,128]{2,1,0:T(8,128)S(1)}, u32[]{:S(2)}, u32[]{:S(2)}) collective-permute-start(f32[3,8,128]{2,1,0:T(8,128)} %r_3_.2), channel_id=1, source_target_pairs={{0,127},{1,126},{2,1},{3,0},{4,3},{5,2},{6,5},{7,4},{8,7},{9,6},{1... | collective-permute-start | bytes 36872 | tf_op jit(solution)/shard_map/ppermute | solution.py:263
  17.5 11.6 %collective-permute-start.13 = (f32[32,8,128]{2,1,0:T(8,128)}, f32[32,8,128]{2,1,0:T(8,128)S(1)}, u32[]{:S(2)}, u32[]{:S(2)}) collective-permute-start(f32[32,8,128]{2,1,0:T(8,128)} %r_3_.3), channel_id=1, source_target_pairs={{0,126},{1,127},{2,0},{3,1},{4,2},{5,3},{6,4},{7,5},{8,6},{9,7},{1... | collective-permute-start | bytes 393224 | tf_op jit(solution)/shard_map/ppermute | solution.py:263
  18.5 10.7 %collective-permute-start.12 = (f32[32,8,128]{2,1,0:T(8,128)}, f32[32,8,128]{2,1,0:T(8,128)S(1)}, u32[]{:S(2)}, u32[]{:S(2)}) collective-permute-start(f32[32,8,128]{2,1,0:T(8,128)} %r_3_.3), channel_id=1, source_target_pairs={{0,1},{1,0},{2,3},{3,2},{4,5},{5,4},{6,7},{7,6},{8,9},{9,8},{10,11... | collective-permute-start | bytes 393224 | tf_op jit(solution)/shard_map/ppermute | solution.py:263
  19.3 10.5 %collective-permute-start.11 = (f32[32,8,128]{2,1,0:T(8,128)}, f32[32,8,128]{2,1,0:T(8,128)S(1)}, u32[]{:S(2)}, u32[]{:S(2)}) collective-permute-start(f32[32,8,128]{2,1,0:T(8,128)} %r_3_.3), channel_id=1, source_target_pairs={{0,3},{1,2},{2,5},{3,4},{4,7},{5,6},{6,9},{7,8},{8,11},{9,10},{10,... | collective-permute-start | bytes 393224 | tf_op jit(solution)/shard_map/ppermute | solution.py:263
  20.9 11.2 %collective-permute-start.10 = (f32[32,8,128]{2,1,0:T(8,128)}, f32[32,8,128]{2,1,0:T(8,128)S(1)}, u32[]{:S(2)}, u32[]{:S(2)}) collective-permute-start(f32[32,8,128]{2,1,0:T(8,128)} %r_3_.3), channel_id=1, source_target_pairs={{0,2},{1,3},{2,4},{3,5},{4,6},{5,7},{6,8},{7,9},{8,10},{9,11},{10,... | collective-permute-start | bytes 393224 | tf_op jit(solution)/shard_map/ppermute | solution.py:263
  20.9 13.0 %collective-permute-start.14 = (f32[32,8,128]{2,1,0:T(8,128)}, f32[32,8,128]{2,1,0:T(8,128)S(1)}, u32[]{:S(2)}, u32[]{:S(2)}) collective-permute-start(f32[32,8,128]{2,1,0:T(8,128)} %r_3_.3), channel_id=1, source_target_pairs={{0,127},{1,126},{2,1},{3,0},{4,3},{5,2},{6,5},{7,4},{8,7},{9,6},{1... | collective-permute-start | bytes 393224 | tf_op jit(solution)/shard_map/ppermute | solution.py:263
  26.6 0.7 copy-start.1
  27.3 0.7 copy-start.2
  29.1 8.8 %collective-permute-start.5 = (f32[3,8,128]{2,1,0:T(8,128)S(1)}, f32[3,8,128]{2,1,0:T(8,128)S(1)}, u32[]{:S(2)}, u32[]{:S(2)}) collective-permute-start(f32[3,8,128]{2,1,0:T(8,128)S(1)} %get-tuple-element.19), channel_id=1, source_target_pairs={{0,16},{1,17},{2,18},{3,19},{4,20},{5,21},{6,22},{7,23},{8,24},{9,... | collective-permute-start | bytes 36872 | tf_op jit(solution)/shard_map/ppermute | solution.py:263
  29.2 12.0 %collective-permute-start.6 = (f32[3,8,128]{2,1,0:T(8,128)S(1)}, f32[3,8,128]{2,1,0:T(8,128)S(1)}, u32[]{:S(2)}, u32[]{:S(2)}) collective-permute-start(f32[3,8,128]{2,1,0:T(8,128)S(1)} %get-tuple-element.20), channel_id=1, source_target_pairs={{0,32},{1,33},{2,34},{3,35},{4,36},{5,37},{6,38},{7,39},{8,40},{9,... | collective-permute-start | bytes 36872 | tf_op jit(solution)/shard_map/ppermute | solution.py:263
  29.8 12.5 %collective-permute-start.7 = (f32[3,8,128]{2,1,0:T(8,128)S(1)}, f32[3,8,128]{2,1,0:T(8,128)S(1)}, u32[]{:S(2)}, u32[]{:S(2)}) collective-permute-start(f32[3,8,128]{2,1,0:T(8,128)S(1)} %get-tuple-element.21), channel_id=1, source_target_pairs={{0,48},{1,49},{2,50},{3,51},{4,52},{5,53},{6,54},{7,55},{8,56},{9,... | collective-permute-start | bytes 36872 | tf_op jit(solution)/shard_map/ppermute | solution.py:263
  32.1 11.8 %collective-permute-start.8 = (f32[3,8,128]{2,1,0:T(8,128)S(1)}, f32[3,8,128]{2,1,0:T(8,128)S(1)}, u32[]{:S(2)}, u32[]{:S(2)}) collective-permute-start(f32[3,8,128]{2,1,0:T(8,128)S(1)} %get-tuple-element.22), channel_id=1, source_target_pairs={{0,64},{1,65},{2,66},{3,67},{4,68},{5,69},{6,70},{7,71},{8,72},{9,... | collective-permute-start | bytes 36872 | tf_op jit(solution)/shard_map/ppermute | solution.py:263
  34.0 11.5 %collective-permute-start.9 = (f32[3,8,128]{2,1,0:T(8,128)S(1)}, f32[3,8,128]{2,1,0:T(8,128)S(1)}, u32[]{:S(2)}, u32[]{:S(2)}) collective-permute-start(f32[3,8,128]{2,1,0:T(8,128)S(1)} %get-tuple-element.23), channel_id=1, source_target_pairs={{0,80},{1,81},{2,82},{3,83},{4,84},{5,85},{6,86},{7,87},{8,88},{9,... | collective-permute-start | bytes 36872 | tf_op jit(solution)/shard_map/ppermute | solution.py:263
  35.7 0.9 copy-start
  37.9 60.5 %collective-permute-start.15 = (f32[4,32,128]{2,1,0:T(8,128)S(1)}, f32[4,32,128]{2,1,0:T(8,128)S(1)}, u32[]{:S(2)}, u32[]{:S(2)}) collective-permute-start(f32[4,32,128]{2,1,0:T(8,128)S(1)} %get-tuple-element.27), channel_id=1, source_target_pairs={{0,16},{1,17},{2,18},{3,19},{4,20},{5,21},{6,22},{7,23},{8,24},{9,... | collective-permute-start | bytes 196616 | tf_op jit(solution)/shard_map/ppermute | solution.py:263
  41.2 57.1 %collective-permute-start.16 = (f32[4,32,128]{2,1,0:T(8,128)S(1)}, f32[4,32,128]{2,1,0:T(8,128)S(1)}, u32[]{:S(2)}, u32[]{:S(2)}) collective-permute-start(f32[4,32,128]{2,1,0:T(8,128)S(1)} %get-tuple-element.28), channel_id=1, source_target_pairs={{0,32},{1,33},{2,34},{3,35},{4,36},{5,37},{6,38},{7,39},{8,40},{9,... | collective-permute-start | bytes 196616 | tf_op jit(solution)/shard_map/ppermute | solution.py:263
  42.2 56.2 %collective-permute-start.17 = (f32[4,32,128]{2,1,0:T(8,128)S(1)}, f32[4,32,128]{2,1,0:T(8,128)S(1)}, u32[]{:S(2)}, u32[]{:S(2)}) collective-permute-start(f32[4,32,128]{2,1,0:T(8,128)S(1)} %get-tuple-element.29), channel_id=1, source_target_pairs={{0,48},{1,49},{2,50},{3,51},{4,52},{5,53},{6,54},{7,55},{8,56},{9,... | collective-permute-start | bytes 196616 | tf_op jit(solution)/shard_map/ppermute | solution.py:263
  43.9 54.5 %collective-permute-start.18 = (f32[4,32,128]{2,1,0:T(8,128)S(1)}, f32[4,32,128]{2,1,0:T(8,128)S(1)}, u32[]{:S(2)}, u32[]{:S(2)}) collective-permute-start(f32[4,32,128]{2,1,0:T(8,128)S(1)} %get-tuple-element.30), channel_id=1, source_target_pairs={{0,64},{1,65},{2,66},{3,67},{4,68},{5,69},{6,70},{7,71},{8,72},{9,... | collective-permute-start | bytes 196616 | tf_op jit(solution)/shard_map/ppermute | solution.py:263
  45.5 0.7 copy-start.3
  45.5 52.9 %collective-permute-start.19 = (f32[4,32,128]{2,1,0:T(8,128)S(1)}, f32[4,32,128]{2,1,0:T(8,128)S(1)}, u32[]{:S(2)}, u32[]{:S(2)}) collective-permute-start(f32[4,32,128]{2,1,0:T(8,128)S(1)} %get-tuple-element.31), channel_id=1, source_target_pairs={{0,80},{1,81},{2,82},{3,83},{4,84},{5,85},{6,86},{7,87},{8,88},{9,... | collective-permute-start | bytes 196616 | tf_op jit(solution)/shard_map/ppermute | solution.py:263
  100.6 7.5 %collective-permute-start.24 = (f32[40,128]{1,0:T(8,128)S(1)}, f32[40,128]{1,0:T(8,128)S(1)}, u32[]{:S(2)}, u32[]{:S(2)}) collective-permute-start(f32[40,128]{1,0:T(8,128)S(1)} %get-tuple-element.33.r_2_), channel_id=1, source_target_pairs={{0,48},{1,49},{2,50},{3,51},{4,52},{5,53},{6,54},{7,55},{8,56},{9,... | collective-permute-start | bytes 61448 | tf_op jit(solution)/shard_map/ppermute | solution.py:263
  103.2 4.9 %collective-permute-start.23 = (f32[40,128]{1,0:T(8,128)S(1)}, f32[40,128]{1,0:T(8,128)S(1)}, u32[]{:S(2)}, u32[]{:S(2)}) collective-permute-start(f32[40,128]{1,0:T(8,128)S(1)} %get-tuple-element.33.r_2_), channel_id=1, source_target_pairs={{0,64},{1,65},{2,66},{3,67},{4,68},{5,69},{6,70},{7,71},{8,72},{9,... | collective-permute-start | bytes 61448 | tf_op jit(solution)/shard_map/ppermute | solution.py:263
  103.6 5.0 %collective-permute-start.22 = (f32[40,128]{1,0:T(8,128)S(1)}, f32[40,128]{1,0:T(8,128)S(1)}, u32[]{:S(2)}, u32[]{:S(2)}) collective-permute-start(f32[40,128]{1,0:T(8,128)S(1)} %get-tuple-element.33.r_2_), channel_id=1, source_target_pairs={{0,80},{1,81},{2,82},{3,83},{4,84},{5,85},{6,86},{7,87},{8,88},{9,... | collective-permute-start | bytes 61448 | tf_op jit(solution)/shard_map/ppermute | solution.py:263
  104.6 5.3 %collective-permute-start.21 = (f32[40,128]{1,0:T(8,128)S(1)}, f32[40,128]{1,0:T(8,128)S(1)}, u32[]{:S(2)}, u32[]{:S(2)}) collective-permute-start(f32[40,128]{1,0:T(8,128)S(1)} %get-tuple-element.33.r_2_), channel_id=1, source_target_pairs={{0,96},{1,97},{2,98},{3,99},{4,100},{5,101},{6,102},{7,103},{8,104... | collective-permute-start | bytes 61448 | tf_op jit(solution)/shard_map/ppermute | solution.py:263
  108.0 3.8 %collective-permute-start.20 = (f32[40,128]{1,0:T(8,128)S(1)}, f32[40,128]{1,0:T(8,128)S(1)}, u32[]{:S(2)}, u32[]{:S(2)}) collective-permute-start(f32[40,128]{1,0:T(8,128)S(1)} %get-tuple-element.33.r_2_), channel_id=1, source_target_pairs={{0,112},{1,113},{2,114},{3,115},{4,116},{5,117},{6,118},{7,119},{8... | collective-permute-start | bytes 61448 | tf_op jit(solution)/shard_map/ppermute | solution.py:263

commit v2 on v1

v2 whole, which is shorter than its diff:
```python
import jax
import jax.numpy as jnp
from jax import lax
from jax.experimental import pallas as pl
from jax.experimental.pallas import tpu as pltpu
from jax.sharding import PartitionSpec as P

HIGHEST = lax.Precision.HIGHEST
LEAF = 16
TASKS = 3
NBR = 4
NF = 32
W = 128
SLOTS = 8
SHIP = SLOTS - TASKS
ROWS = NBR * NF + 24
MASKS = (1, 3, 4, 5, 7)
F32 = jnp.float32

VMEM = pl.BlockSpec(memory_space=pltpu.VMEM)
SMEM = pl.BlockSpec(memory_space=pltpu.SMEM)


def params():
    return pltpu.CompilerParams(vmem_limit_bytes=40 * 2**20)


def mm(a, b):
    return lax.dot_general(
        a, b, (((1,), (0,)), ((), ())), precision=HIGHEST, preferred_element_type=F32
    )


def mmt(a, b):
    return lax.dot_general(
        a, b, (((1,), (1,)), ((), ())), precision=HIGHEST, preferred_element_type=F32
    )


def sweep(panel, off, rows, lanes):
    cols = [
        jnp.broadcast_to(panel[:, off + c : off + c + 1], (LEAF, W)) for c in range(LEAF)
    ]
    scale = jnp.zeros((LEAF, W), F32)
    for i in range(LEAF):
        here = rows == i
        r = jnp.broadcast_to(1.0 / cols[i][i : i + 1], (LEAF, W))
        others = jnp.where(here, 0.0, cols[i])
        scale = jnp.where(here, r, scale)
        if i + 1 < LEAF:
            ahead = others * jnp.broadcast_to(cols[i + 1][i : i + 1], (LEAF, W))
            cols[i + 1] = cols[i + 1] - r * ahead
        m = others * r
        panel = jnp.where(lanes == off + i, jnp.where(here, 1.0, 0.0), panel)
        panel = panel - m * jnp.broadcast_to(panel[i : i + 1], (LEAF, W))
        for c in range(i + 2, LEAF):
            cols[c] = cols[c] - m * jnp.broadcast_to(cols[c][i : i + 1], (LEAF, W))
    return panel * scale


def stack(*parts):
    return jnp.concatenate([x for x in parts if x.shape[0]], 0)


def invert(tiles):
    rows = lax.broadcasted_iota(jnp.int32, (LEAF, W), 0)
    lanes = lax.broadcasted_iota(jnp.int32, (LEAF, W), 1)
    along = lax.broadcasted_iota(jnp.int32, (W, W), 1)
    for off in range(0, W, LEAF):
        end = off + LEAF
        swept = [sweep(t[off:end], off, rows, lanes) for t in tiles]
        new = []
        in_cols = (along >= off) & (along < end)
        for t, q in zip(tiles, swept):
            wide = stack(jnp.zeros((off, W), F32), q, jnp.zeros((W - end, W), F32))
            base = jnp.where(in_cols, 0.0, t)

            def less(low, high, t=t, wide=wide, base=base):
                if low == high:
                    return t[low:high]
                return base[low:high] - mm(t[low:high], wide)

            soon = min(end + LEAF, W)
            new.append(stack(less(0, off), q, less(end, soon), less(soon, W)))
        tiles = new
    return tiles


def pool_row(block, my_band, my_sub, bands):
    band = block // (2 * SLOTS)
    sub = (block // SLOTS) % 2
    side = (band - my_band + 1 + bands) % bands
    flip = jnp.where(sub == my_sub, 0, 1)
    return (side * 2 + flip) * SLOTS + block % SLOTS


def pack(bands, nb, *refs):
    pools, own, ships, pool = refs[:6], refs[6], refs[7:-1], refs[-1]
    band, sub = lax.axis_index("lon"), lax.axis_index("lat")
    for g in range(6):
        pool[:, g * SLOTS : (g + 1) * SLOTS, :] = pools[g][...]
    for s in range(SLOTS):
        dst = own.at[s] if s < TASKS else ships[s - TASKS]
        dst[NBR * NF :, :] = jnp.zeros((24, W), F32)
        for n in range(NBR):
            row = pool_row(nb[n, s], band, sub, bands)
            got = pool[:, pl.ds(row, 1), :].reshape(NF + 3, W)
            dst[n * NF : (n + 1) * NF, :] = got[3:]
            for d in range(3):
                dst[NBR * NF + 8 * d + n : NBR * NF + 8 * d + n + 1, :] = got[d : d + 1]
        for d in range(3):
            at = NBR * NF + 8 * d + NBR
            dst[at : at + 1, :] = pools[2][d, s : s + 1, :]


def solve(bands, counts, scale, nugget, own, *refs):
    ships, kept, sent, work, tiles, diag = refs[:SHIP], *refs[SHIP:]
    band, sub = lax.axis_index("lon"), lax.axis_index("lat")
    apart = bands // SLOTS
    work[...] = own[...]
    for k, mask in enumerate(MASKS):

        @pl.when(counts[(band ^ (mask * apart)) * 2 + sub] > TASKS - 1)
        def _():
            work[TASKS - 1] = ships[k][...]

    down = lax.broadcasted_iota(jnp.int32, (W, W), 0)
    along = lax.broadcasted_iota(jnp.int32, (W, W), 1)
    minus = jnp.full((W, W), -1.0, F32) / scale[0]
    noise = jnp.where(down == along, nugget[0], 0.0)
    ones = jnp.ones((8, W), F32)

    def result(s):
        return sent if s == TASKS - 1 else kept.at[s]

    def build(s, carry):
        rows = [work[s, pl.ds(NBR * NF + 8 * d, 8), :] for d in range(3)]
        cols = [r.T for r in rows]
        for a in range(NBR + 1):
            mine = [jnp.broadcast_to(c[:, a : a + 1], (W, W)) for c in cols]
            for b in range(min(a, NBR - 1) + 1):
                total = None
                for d in range(3):
                    gap = mine[d] - jnp.broadcast_to(rows[d][b : b + 1], (W, W))
                    total = gap * gap if total is None else total + gap * gap
                value = jnp.exp(jnp.sqrt(total) * minus)
                if a == b:
                    value = value + noise
                tiles[s, a, b] = value
        return carry

    lax.fori_loop(0, TASKS, build, 0)
    for s in range(TASKS):
        result(s)[NF:] = jnp.ones((8, W), F32)

    def eliminate(j, carry):
        for s, g in enumerate(invert([tiles[s, j, j] for s in range(TASKS)])):
            diag[s] = g
        for at in range(NBR):

            @pl.when(j == at)
            def _():
                for s in range(TASKS):
                    g = diag[s]
                    d = tiles[s, at, at]
                    given = tiles[s, at + 1 :, at].reshape((NBR - at) * W, W)
                    left = mm(given, g)
                    left = left + mm(given - mm(left, d), g)
                    for b in range(at + 1, NBR):
                        fresh = mmt(left[(b - at - 1) * W :], tiles[s, b, at])
                        tiles[s, b:, b] = tiles[s, b:, b] - fresh.reshape(NBR + 1 - b, W, W)
                    result(s)[NF:] -= mmt(ones, left[-W:] * tiles[s, NBR, at])
                    tiles[s, at + 1 :, at] = left.reshape(NBR - at, W, W)

        return carry

    lax.fori_loop(0, NBR, eliminate, 0)
    for s in range(TASKS):
        done = [None] * NBR
        total = None
        for at in range(NBR - 1, -1, -1):
            x = tiles[s, NBR, at]
            for a in range(at + 1, NBR):
                x = x - mm(done[a], tiles[s, a, at])
            done[at] = x
            part = mmt(work[s, at * NF : (at + 1) * NF, :], x)
            total = part if total is None else total + part
        result(s)[:NF] = total


def assemble(bands, counts, kept, third, *refs):
    backs, predicted, variance = refs[:SHIP], refs[SHIP], refs[SHIP + 1]
    band, sub = lax.axis_index("lon"), lax.axis_index("lat")
    alive = counts[band * 2 + sub]
    for s in range(SLOTS):
        src = kept[s] if s < TASKS - 1 else third[...] if s < TASKS else backs[s - TASKS][...]
        src = jnp.where(s < alive, src, 0.0)
        predicted[:, s : s + 1, :] = src[:NF].reshape(NF, 1, W)
        variance[s : s + 1, :] = src[NF : NF + 1]


def arr(*shape):
    return jax.ShapeDtypeStruct(shape, F32)


def on_device(bands, coords, observed, neighbours, counts, lengthscale, nugget):
    axes = ("lon", "lat")
    total = bands * 2
    apart = bands // SLOTS

    def shift(x, lon, flip):
        pairs = [
            (l * 2 + h, ((l + lon) % bands) * 2 + (h ^ flip))
            for l in range(bands)
            for h in range(2)
        ]
        return lax.ppermute(x, axes, pairs)

    def pool_of(x):
        return [
            x if (away, flip) == (0, 0) else shift(x, -away, flip)
            for away in (-1, 0, 1)
            for flip in (0, 1)
        ]

    def trade(x, mask):
        pairs = [
            (l * 2 + h, (l ^ (mask * apart)) * 2 + h) for l in range(bands) for h in range(2)
        ]
        return lax.ppermute(x, axes, pairs)

    pool = pool_of(jnp.concatenate([coords, observed], axis=0))
    own, *out = pl.pallas_call(
        lambda *r: pack(bands, *r),
        out_shape=[arr(TASKS, ROWS, W)] + [arr(ROWS, W)] * SHIP,
        in_specs=[SMEM] + [VMEM] * 6,
        out_specs=[VMEM] * (1 + SHIP),
        scratch_shapes=[pltpu.VMEM((NF + 3, 6 * SLOTS, W), F32)],
        compiler_params=params(),
        name="pack",
    )(neighbours, *pool)
    ships = [trade(x, mask) for x, mask in zip(out, MASKS)]
    kept, third = pl.pallas_call(
        lambda *r: solve(bands, *r),
        out_shape=[arr(TASKS - 1, NF + 8, W), arr(NF + 8, W)],
        in_specs=[SMEM] * 3 + [VMEM] * (1 + SHIP),
        out_specs=[VMEM] * 2,
        scratch_shapes=[
            pltpu.VMEM((TASKS, ROWS, W), F32),
            pltpu.VMEM((TASKS, NBR + 1, NBR, W, W), F32),
            pltpu.VMEM((TASKS, W, W), F32),
        ],
        compiler_params=params(),
        name="solve",
    )(counts, lengthscale, nugget, own, *ships)
    backs = [trade(third, mask) for mask in MASKS]
    return pl.pallas_call(
        lambda *r: assemble(bands, *r),
        out_shape=[arr(NF, SLOTS, W), arr(SLOTS, W)],
        in_specs=[SMEM] + [VMEM] * (2 + SHIP),
        out_specs=[VMEM] * 2,
        compiler_params=params(),
        name="assemble",
    )(counts, kept, third, *backs)


def solution(mesh):
    bands = mesh.shape["lon"]
    placed = (
        P(None, ("lon", "lat"), None),
        P(None, ("lon", "lat"), None),
        P(None, ("lon", "lat")),
        P(),
        P(),
        P(),
    )

    def step(*args):
        return tuple(on_device(bands, *args))

    return jax.shard_map(
        step,
        mesh=mesh,
        in_specs=placed,
        out_specs=(P(None, ("lon", "lat"), None), P(("lon", "lat"), None)),
        check_vma=False,
    )
```

time: 113 us -> 87 us (0.77)
  starting transfers between devices: 45.7 us -> 25.2 us
  Pallas kernels: 58 us -> 46.2 us
  waiting for transfers between devices: 4.38 us -> 11.8 us
  local copies, waits for them, and re-layouts: 2.94 us -> 1.65 us
    ppermute x25 -> x5, starting transfers between devices: 45.7 us -> 12 us  [shift(): return lax.ppermute(x, axes, pairs)]
    ppermute x0 -> x10, starting transfers between devices: none -> 13.2 us  [trade(): return lax.ppermute(x, axes, pairs)]
    pallas_call x4 -> x2, Pallas kernels: 56.7 us -> 44.9 us  [the longest x1 43.6 us: on_device(): pl.pallas_call(lambda *r: solve(bands, *r), out_shape=[arr(TASKS - 1, NF...]
    ppermute x0 -> x10, waiting for transfers between devices: none -> 7.18 us  [trade(): return lax.ppermute(x, axes, pairs)]
    unnamed x8 -> x5, local copies, waits for them, and re-layouts: 2.94 us -> 0.72 us
    ppermute x25 -> x5, waiting for transfers between devices: 4.38 us -> 4.59 us  [shift(): return lax.ppermute(x, axes, pairs)]
  transfers between devices with their start and end apart: 25 -> 15, of which waited for: 5 -> 5; matrix products, arithmetic and copies ran while one was open for 0% -> 0% of each run, Pallas kernels for 48% -> 0%
where the time goes in v2:
time: 87 us; the launch traced here: 86.8 us
  Pallas kernels  46.2 us (53%)
  starting transfers between devices  25.2 us (29%)
  waiting for transfers between devices  11.8 us (14%)
  between operations  2.01 us (2%)
  local copies, waits for them, and re-layouts  1.65 us (2%)
    pallas_call x1, Pallas kernels, on_device(): pl.pallas_call(lambda *r: solve(bands, *r), out_shape=[arr(TASKS - 1, NF...  43.6 us
    ppermute x10, starting transfers between devices, trade(): return lax.ppermute(x, axes, pairs)  13.2 us
    ppermute x5, starting transfers between devices, shift(): return lax.ppermute(x, axes, pairs)  12 us
    ppermute x10, waiting for transfers between devices, trade(): return lax.ppermute(x, axes, pairs)  7.18 us
    ppermute x5, waiting for transfers between devices, shift(): return lax.ppermute(x, axes, pairs)  4.59 us
  transfers between devices with their start and end apart: 15, of which 5 were waited for; matrix products, arithmetic and copies ran while one was open for 0% of the time, Pallas kernels for 0%

profile of v2, /device:TPU:0, one launch (start us, length us, event | category | flops | bytes accessed | tf_op | source)
XLA Modules:
  0.0 86.8 jit_solution(2893947382883024281)
XLA Ops:
  0.6 0.7 constant_dynamic-update-slice_fusion.1
  1.3 0.0 copy-start
  1.3 0.9 %constant_dynamic-update-slice_fusion.r_3_ = f32[35,8,128]{2,1,0:T(8,128)S(1)} fusion(f32[35,8,128]{2,1,0:T(8,128)S(1)} %constant_dynamic-update-slice_fusion.1, f32[32,8,128]{2,1,0:T(8,128)} %param.7), kind=kLoop, calls=%fused_computation | loop fusion | bytes 262144 | tf_op jit(solution)/shard_map/concatenate | solution.py:232
  2.3 0.1 collective-permute-start
  2.4 4.9 %collective-permute-start.1 = (f32[35,8,128]{2,1,0:T(8,128)S(1)}, f32[35,8,128]{2,1,0:T(8,128)S(1)}, u32[]{:S(2)}, u32[]{:S(2)}) collective-permute-start(f32[35,8,128]{2,1,0:T(8,128)S(1)} %constant_dynamic-update-slice_fusion.r_3_), channel_id=1, source_target_pairs={{0,3},{1,2},{2,5},{3,4},{4,7},{5,6},{6,9},{7,8},{8,11},{9,10},{10,... | collective-permute-start | bytes 430088 | tf_op jit(solution)/shard_map/ppermute | solution.py:217
  7.3 0.3 collective-permute-start.2
  7.6 3.7 %collective-permute-start.3 = (f32[35,8,128]{2,1,0:T(8,128)S(1)}, f32[35,8,128]{2,1,0:T(8,128)S(1)}, u32[]{:S(2)}, u32[]{:S(2)}) collective-permute-start(f32[35,8,128]{2,1,0:T(8,128)S(1)} %constant_dynamic-update-slice_fusion.r_3_), channel_id=1, source_target_pairs={{0,126},{1,127},{2,0},{3,1},{4,2},{5,3},{6,4},{7,5},{8,6},{9,7},{1... | collective-permute-start | bytes 430088 | tf_op jit(solution)/shard_map/ppermute | solution.py:217
  11.3 3.0 %collective-permute-start.4 = (f32[35,8,128]{2,1,0:T(8,128)S(1)}, f32[35,8,128]{2,1,0:T(8,128)S(1)}, u32[]{:S(2)}, u32[]{:S(2)}) collective-permute-start(f32[35,8,128]{2,1,0:T(8,128)S(1)} %constant_dynamic-update-slice_fusion.r_3_), channel_id=1, source_target_pairs={{0,127},{1,126},{2,1},{3,0},{4,3},{5,2},{6,5},{7,4},{8,7},{9,6},{1... | collective-permute-start | bytes 430088 | tf_op jit(solution)/shard_map/ppermute | solution.py:217
  14.3 0.0 collective-permute-done.r_1_
  14.3 1.7 %collective-permute-done.1.r_2_ = f32[35,8,128]{2,1,0:T(8,128)S(1)} collective-permute-done((f32[35,8,128]{2,1,0:T(8,128)S(1)}, f32[35,8,128]{2,1,0:T(8,128)S(1)}, u32[]{:S(2)}, u32[]{:S(2)}) %collective-permute-start.1) | collective-permute-done | bytes 143392 | tf_op jit(solution)/shard_map/ppermute | solution.py:217
  15.9 0.0 collective-permute-done.2.r_4_
  15.9 0.0 collective-permute-done.3.r_5_
  16.0 2.9 %collective-permute-done.4.r_6_ = f32[35,8,128]{2,1,0:T(8,128)S(1)} collective-permute-done((f32[35,8,128]{2,1,0:T(8,128)S(1)}, f32[35,8,128]{2,1,0:T(8,128)S(1)}, u32[]{:S(2)}, u32[]{:S(2)}) %collective-permute-start.4) | collective-permute-done | bytes 143392 | tf_op jit(solution)/shard_map/ppermute | solution.py:217
  18.9 0.0 copy-done
  18.9 1.3 %pack.1 = (f32[3,152,128]{2,1,0:T(8,128)S(1)}, f32[152,128]{1,0:T(8,128)S(1)}, f32[152,128]{1,0:T(8,128)S(1)}, f32[152,128]{1,0:T(8,128)S(1)}, f32[152,128]{1,0:T(8,128)S(1)}, /*index=5*/f32[152,128]{1,0:T(8,128)S(1)}) custom-call(s32[4,8]{1,0:T(4,128)S(1)} %copy-done, f32[35,8,128]{2,1,0:T(8,128)S(1)} %collective-permute-done.r_1_, ...), custom_call_target="tpu_custom_call" | custom-call | tf_op jit(solution)/shard_map/pack/pallas_call | solution.py:233
  20.1 0.1 collective-permute-start.5
  20.2 3.0 %collective-permute-start.6 = (f32[152,128]{1,0:T(8,128)S(1)}, f32[152,128]{1,0:T(8,128)S(1)}, u32[]{:S(2)}, u32[]{:S(2)}) collective-permute-start(f32[152,128]{1,0:T(8,128)S(1)} %get-tuple-element.12), channel_id=1, source_target_pairs={{0,48},{1,49},{2,50},{3,51},{4,52},{5,53},{6,54},{7,55},{8,56},{9,... | collective-permute-start | bytes 233480 | tf_op jit(solution)/shard_map/ppermute | solution.py:230
  23.2 0.9 %collective-permute-start.7 = (f32[152,128]{1,0:T(8,128)S(1)}, f32[152,128]{1,0:T(8,128)S(1)}, u32[]{:S(2)}, u32[]{:S(2)}) collective-permute-start(f32[152,128]{1,0:T(8,128)S(1)} %get-tuple-element.13), channel_id=1, source_target_pairs={{0,64},{1,65},{2,66},{3,67},{4,68},{5,69},{6,70},{7,71},{8,72},{9,... | collective-permute-start | bytes 233480 | tf_op jit(solution)/shard_map/ppermute | solution.py:230
  24.1 1.9 %collective-permute-start.8 = (f32[152,128]{1,0:T(8,128)S(1)}, f32[152,128]{1,0:T(8,128)S(1)}, u32[]{:S(2)}, u32[]{:S(2)}) collective-permute-start(f32[152,128]{1,0:T(8,128)S(1)} %get-tuple-element.14), channel_id=1, source_target_pairs={{0,80},{1,81},{2,82},{3,83},{4,84},{5,85},{6,86},{7,87},{8,88},{9,... | collective-permute-start | bytes 233480 | tf_op jit(solution)/shard_map/ppermute | solution.py:230
  26.0 0.9 %collective-permute-start.9 = (f32[152,128]{1,0:T(8,128)S(1)}, f32[152,128]{1,0:T(8,128)S(1)}, u32[]{:S(2)}, u32[]{:S(2)}) collective-permute-start(f32[152,128]{1,0:T(8,128)S(1)} %get-tuple-element.15), channel_id=1, source_target_pairs={{0,112},{1,113},{2,114},{3,115},{4,116},{5,117},{6,118},{7,119},{8... | collective-permute-start | bytes 233480 | tf_op jit(solution)/shard_map/ppermute | solution.py:230
  28.2 0.0 copy-start.1
  28.2 0.0 collective-permute-done.5.r_4_
  28.2 0.0 collective-permute-done.6.r_5_
  28.3 0.0 collective-permute-done.7.r_6_
  28.3 1.4 %collective-permute-done.8.r_7_ = f32[152,128]{1,0:T(8,128)S(1)} collective-permute-done((f32[152,128]{1,0:T(8,128)S(1)}, f32[152,128]{1,0:T(8,128)S(1)}, u32[]{:S(2)}, u32[]{:S(2)}) %collective-permute-start.8) | collective-permute-done | bytes 77856 | tf_op jit(solution)/shard_map/ppermute | solution.py:230
  29.7 2.8 %collective-permute-done.9.r_8_ = f32[152,128]{1,0:T(8,128)S(1)} collective-permute-done((f32[152,128]{1,0:T(8,128)S(1)}, f32[152,128]{1,0:T(8,128)S(1)}, u32[]{:S(2)}, u32[]{:S(2)}) %collective-permute-start.9) | collective-permute-done | bytes 77856 | tf_op jit(solution)/shard_map/ppermute | solution.py:230
  32.5 0.0 copy-done.1
  32.5 43.6 %solve.1 = (f32[2,40,128]{2,1,0:T(8,128)S(1)}, f32[40,128]{1,0:T(8,128)S(1)}) custom-call(s32[128]{0:T(128)S(1)} %copy-done.1, f32[1]{0:T(128)S(6)} %copy.9.r_1_, f32[1]{0:T(128)S(6)} %copy.10.r_2_, f32[3,152,128]{2,1,0:T(8,128)S(1)} %get-tuple-element.10.r_3_, f32[152,128]{1,0:T(8,128)S(1)} %collective-permute-done.5.r_4_, ...), custom_call_target="tpu_custom_call" | custom-call | tf_op jit(solution)/shard_map/solve/pallas_call | solution.py:243
  76.1 0.0 collective-permute-start.10
  76.1 0.7 collective-permute-start.11
  76.8 1.0 %collective-permute-start.12 = (f32[40,128]{1,0:T(8,128)S(1)}, f32[40,128]{1,0:T(8,128)S(1)}, u32[]{:S(2)}, u32[]{:S(2)}) collective-permute-start(f32[40,128]{1,0:T(8,128)S(1)} %get-tuple-element.17.r_2_), channel_id=1, source_target_pairs={{0,64},{1,65},{2,66},{3,67},{4,68},{5,69},{6,70},{7,71},{8,72},{9,... | collective-permute-start | bytes 61448 | tf_op jit(solution)/shard_map/ppermute | solution.py:230
  77.8 1.9 %collective-permute-start.13 = (f32[40,128]{1,0:T(8,128)S(1)}, f32[40,128]{1,0:T(8,128)S(1)}, u32[]{:S(2)}, u32[]{:S(2)}) collective-permute-start(f32[40,128]{1,0:T(8,128)S(1)} %get-tuple-element.17.r_2_), channel_id=1, source_target_pairs={{0,80},{1,81},{2,82},{3,83},{4,84},{5,85},{6,86},{7,87},{8,88},{9,... | collective-permute-start | bytes 61448 | tf_op jit(solution)/shard_map/ppermute | solution.py:230
  79.6 2.9 %collective-permute-start.14 = (f32[40,128]{1,0:T(8,128)S(1)}, f32[40,128]{1,0:T(8,128)S(1)}, u32[]{:S(2)}, u32[]{:S(2)}) collective-permute-start(f32[40,128]{1,0:T(8,128)S(1)} %get-tuple-element.17.r_2_), channel_id=1, source_target_pairs={{0,112},{1,113},{2,114},{3,115},{4,116},{5,117},{6,118},{7,119},{8... | collective-permute-start | bytes 61448 | tf_op jit(solution)/shard_map/ppermute | solution.py:230
  82.6 0.0 collective-permute-done.10.r_3_
  82.6 0.0 collective-permute-done.11.r_4_
  82.6 0.0 collective-permute-done.12.r_5_
  82.6 0.0 collective-permute-done.13.r_6_
  82.6 2.9 %collective-permute-done.14.r_7_ = f32[40,128]{1,0:T(8,128)S(1)} collective-permute-done((f32[40,128]{1,0:T(8,128)S(1)}, f32[40,128]{1,0:T(8,128)S(1)}, u32[]{:S(2)}, u32[]{:S(2)}) %collective-permute-start.14) | collective-permute-done | bytes 20512 | tf_op jit(solution)/shard_map/ppermute | solution.py:230
  85.5 1.3 %assemble.1 = (f32[32,8,128]{2,1,0:T(8,128)}, f32[8,128]{1,0:T(8,128)}) custom-call(s32[128]{0:T(128)S(1)} %copy-done.1, f32[2,40,128]{2,1,0:T(8,128)S(1)} %get-tuple-element.16.r_1_, f32[40,128]{1,0:T(8,128)S(1)} %get-tuple-element.17.r_2_, f32[40,128]{1,0:T(8,128)S(1)} %collective-permute-done.10.r_3_, f32[40,128]{1,0:T(8,128)S(1)} %collective-permute-done.11.r_4_, ...), custom_call_target="tpu_custom_call" | custom-call | tf_op jit(solution)/shard_map/assemble/pallas_call | solution.py:257
Async XLA Ops:
  1.3 17.5 %copy-start = (s32[4,8]{1,0:T(4,128)S(1)}, s32[4,8]{1,0:T(4,128)}, u32[]{:S(2)}) copy-start(s32[4,8]{1,0:T(4,128)} %r_0_.3) | copy-start | bytes 388
  2.3 12.0 %collective-permute-start = (f32[35,8,128]{2,1,0:T(8,128)S(1)}, f32[35,8,128]{2,1,0:T(8,128)S(1)}, u32[]{:S(2)}, u32[]{:S(2)}) collective-permute-start(f32[35,8,128]{2,1,0:T(8,128)S(1)} %constant_dynamic-update-slice_fusion.r_3_), channel_id=1, source_target_pairs={{0,2},{1,3},{2,4},{3,5},{4,6},{5,7},{6,8},{7,9},{8,10},{9,11},{10,... | collective-permute-start | bytes 430088 | tf_op jit(solution)/shard_map/ppermute | solution.py:217
  2.4 13.6 %collective-permute-start.1 = (f32[35,8,128]{2,1,0:T(8,128)S(1)}, f32[35,8,128]{2,1,0:T(8,128)S(1)}, u32[]{:S(2)}, u32[]{:S(2)}) collective-permute-start(f32[35,8,128]{2,1,0:T(8,128)S(1)} %constant_dynamic-update-slice_fusion.r_3_), channel_id=1, source_target_pairs={{0,3},{1,2},{2,5},{3,4},{4,7},{5,6},{6,9},{7,8},{8,11},{9,10},{10,... | collective-permute-start | bytes 430088 | tf_op jit(solution)/shard_map/ppermute | solution.py:217
  7.3 8.7 %collective-permute-start.2 = (f32[35,8,128]{2,1,0:T(8,128)S(1)}, f32[35,8,128]{2,1,0:T(8,128)S(1)}, u32[]{:S(2)}, u32[]{:S(2)}) collective-permute-start(f32[35,8,128]{2,1,0:T(8,128)S(1)} %constant_dynamic-update-slice_fusion.r_3_), channel_id=1, source_target_pairs={{0,1},{1,0},{2,3},{3,2},{4,5},{5,4},{6,7},{7,6},{8,9},{9,8},{10,11... | collective-permute-start | bytes 430088 | tf_op jit(solution)/shard_map/ppermute | solution.py:217
  7.6 8.4 %collective-permute-start.3 = (f32[35,8,128]{2,1,0:T(8,128)S(1)}, f32[35,8,128]{2,1,0:T(8,128)S(1)}, u32[]{:S(2)}, u32[]{:S(2)}) collective-permute-start(f32[35,8,128]{2,1,0:T(8,128)S(1)} %constant_dynamic-update-slice_fusion.r_3_), channel_id=1, source_target_pairs={{0,126},{1,127},{2,0},{3,1},{4,2},{5,3},{6,4},{7,5},{8,6},{9,7},{1... | collective-permute-start | bytes 430088 | tf_op jit(solution)/shard_map/ppermute | solution.py:217
  11.3 7.6 %collective-permute-start.4 = (f32[35,8,128]{2,1,0:T(8,128)S(1)}, f32[35,8,128]{2,1,0:T(8,128)S(1)}, u32[]{:S(2)}, u32[]{:S(2)}) collective-permute-start(f32[35,8,128]{2,1,0:T(8,128)S(1)} %constant_dynamic-update-slice_fusion.r_3_), channel_id=1, source_target_pairs={{0,127},{1,126},{2,1},{3,0},{4,3},{5,2},{6,5},{7,4},{8,7},{9,6},{1... | collective-permute-start | bytes 430088 | tf_op jit(solution)/shard_map/ppermute | solution.py:217
  20.1 8.1 %collective-permute-start.5 = (f32[152,128]{1,0:T(8,128)S(1)}, f32[152,128]{1,0:T(8,128)S(1)}, u32[]{:S(2)}, u32[]{:S(2)}) collective-permute-start(f32[152,128]{1,0:T(8,128)S(1)} %get-tuple-element.11), channel_id=1, source_target_pairs={{0,16},{1,17},{2,18},{3,19},{4,20},{5,21},{6,22},{7,23},{8,24},{9,... | collective-permute-start | bytes 233480 | tf_op jit(solution)/shard_map/ppermute | solution.py:230
  20.2 8.0 %collective-permute-start.6 = (f32[152,128]{1,0:T(8,128)S(1)}, f32[152,128]{1,0:T(8,128)S(1)}, u32[]{:S(2)}, u32[]{:S(2)}) collective-permute-start(f32[152,128]{1,0:T(8,128)S(1)} %get-tuple-element.12), channel_id=1, source_target_pairs={{0,48},{1,49},{2,50},{3,51},{4,52},{5,53},{6,54},{7,55},{8,56},{9,... | collective-permute-start | bytes 233480 | tf_op jit(solution)/shard_map/ppermute | solution.py:230
  23.2 5.0 %collective-permute-start.7 = (f32[152,128]{1,0:T(8,128)S(1)}, f32[152,128]{1,0:T(8,128)S(1)}, u32[]{:S(2)}, u32[]{:S(2)}) collective-permute-start(f32[152,128]{1,0:T(8,128)S(1)} %get-tuple-element.13), channel_id=1, source_target_pairs={{0,64},{1,65},{2,66},{3,67},{4,68},{5,69},{6,70},{7,71},{8,72},{9,... | collective-permute-start | bytes 233480 | tf_op jit(solution)/shard_map/ppermute | solution.py:230
  24.1 5.6 %collective-permute-start.8 = (f32[152,128]{1,0:T(8,128)S(1)}, f32[152,128]{1,0:T(8,128)S(1)}, u32[]{:S(2)}, u32[]{:S(2)}) collective-permute-start(f32[152,128]{1,0:T(8,128)S(1)} %get-tuple-element.14), channel_id=1, source_target_pairs={{0,80},{1,81},{2,82},{3,83},{4,84},{5,85},{6,86},{7,87},{8,88},{9,... | collective-permute-start | bytes 233480 | tf_op jit(solution)/shard_map/ppermute | solution.py:230
  26.0 6.5 %collective-permute-start.9 = (f32[152,128]{1,0:T(8,128)S(1)}, f32[152,128]{1,0:T(8,128)S(1)}, u32[]{:S(2)}, u32[]{:S(2)}) collective-permute-start(f32[152,128]{1,0:T(8,128)S(1)} %get-tuple-element.15), channel_id=1, source_target_pairs={{0,112},{1,113},{2,114},{3,115},{4,116},{5,117},{6,118},{7,119},{8... | collective-permute-start | bytes 233480 | tf_op jit(solution)/shard_map/ppermute | solution.py:230
  28.2 4.3 %copy-start.1 = (s32[128]{0:T(128)S(1)}, s32[128]{0:T(128)}, u32[]{:S(2)}) copy-start(s32[128]{0:T(128)} %r_0_.5) | copy-start | bytes 1540
  76.1 6.5 %collective-permute-start.10 = (f32[40,128]{1,0:T(8,128)S(1)}, f32[40,128]{1,0:T(8,128)S(1)}, u32[]{:S(2)}, u32[]{:S(2)}) collective-permute-start(f32[40,128]{1,0:T(8,128)S(1)} %get-tuple-element.17.r_2_), channel_id=1, source_target_pairs={{0,16},{1,17},{2,18},{3,19},{4,20},{5,21},{6,22},{7,23},{8,24},{9,... | collective-permute-start | bytes 61448 | tf_op jit(solution)/shard_map/ppermute | solution.py:230
  76.1 6.5 %collective-permute-start.11 = (f32[40,128]{1,0:T(8,128)S(1)}, f32[40,128]{1,0:T(8,128)S(1)}, u32[]{:S(2)}, u32[]{:S(2)}) collective-permute-start(f32[40,128]{1,0:T(8,128)S(1)} %get-tuple-element.17.r_2_), channel_id=1, source_target_pairs={{0,48},{1,49},{2,50},{3,51},{4,52},{5,53},{6,54},{7,55},{8,56},{9,... | collective-permute-start | bytes 61448 | tf_op jit(solution)/shard_map/ppermute | solution.py:230
  76.8 5.8 %collective-permute-start.12 = (f32[40,128]{1,0:T(8,128)S(1)}, f32[40,128]{1,0:T(8,128)S(1)}, u32[]{:S(2)}, u32[]{:S(2)}) collective-permute-start(f32[40,128]{1,0:T(8,128)S(1)} %get-tuple-element.17.r_2_), channel_id=1, source_target_pairs={{0,64},{1,65},{2,66},{3,67},{4,68},{5,69},{6,70},{7,71},{8,72},{9,... | collective-permute-start | bytes 61448 | tf_op jit(solution)/shard_map/ppermute | solution.py:230
  77.8 4.8 %collective-permute-start.13 = (f32[40,128]{1,0:T(8,128)S(1)}, f32[40,128]{1,0:T(8,128)S(1)}, u32[]{:S(2)}, u32[]{:S(2)}) collective-permute-start(f32[40,128]{1,0:T(8,128)S(1)} %get-tuple-element.17.r_2_), channel_id=1, source_target_pairs={{0,80},{1,81},{2,82},{3,83},{4,84},{5,85},{6,86},{7,87},{8,88},{9,... | collective-permute-start | bytes 61448 | tf_op jit(solution)/shard_map/ppermute | solution.py:230
  79.6 5.9 %collective-permute-start.14 = (f32[40,128]{1,0:T(8,128)S(1)}, f32[40,128]{1,0:T(8,128)S(1)}, u32[]{:S(2)}, u32[]{:S(2)}) collective-permute-start(f32[40,128]{1,0:T(8,128)S(1)} %get-tuple-element.17.r_2_), channel_id=1, source_target_pairs={{0,112},{1,113},{2,114},{3,115},{4,116},{5,117},{6,118},{7,119},{8... | collective-permute-start | bytes 61448 | tf_op jit(solution)/shard_map/ppermute | solution.py:230

commit v3 on v2

--- a/solution.py
+++ b/solution.py
@@ -1,3 +1,5 @@
+import functools
+
 import jax
 import jax.numpy as jnp
 from jax import lax
@@ -37,51 +39,121 @@
     )
 
 
-def sweep(panel, off, rows, lanes):
-    cols = [
-        jnp.broadcast_to(panel[:, off + c : off + c + 1], (LEAF, W)) for c in range(LEAF)
-    ]
-    scale = jnp.zeros((LEAF, W), F32)
-    for i in range(LEAF):
-        here = rows == i
-        r = jnp.broadcast_to(1.0 / cols[i][i : i + 1], (LEAF, W))
-        others = jnp.where(here, 0.0, cols[i])
-        scale = jnp.where(here, r, scale)
-        if i + 1 < LEAF:
-            ahead = others * jnp.broadcast_to(cols[i + 1][i : i + 1], (LEAF, W))
-            cols[i + 1] = cols[i + 1] - r * ahead
-        m = others * r
-        panel = jnp.where(lanes == off + i, jnp.where(here, 1.0, 0.0), panel)
-        panel = panel - m * jnp.broadcast_to(panel[i : i + 1], (LEAF, W))
-        for c in range(i + 2, LEAF):
-            cols[c] = cols[c] - m * jnp.broadcast_to(cols[c][i : i + 1], (LEAF, W))
-    return panel * scale
+def halves(a):
+    high = a.astype(jnp.bfloat16)
+    return high, (a - high.astype(F32)).astype(jnp.bfloat16)
+
+
+def mm1(a, b):
+    return lax.dot_general(
+        a.astype(jnp.bfloat16),
+        b.astype(jnp.bfloat16),
+        (((1,), (0,)), ((), ())),
+        preferred_element_type=F32,
+    )
+
+
+def mm3(a, b):
+    (ah, al), (bh, bl) = halves(a), halves(b)
+    return mm1(ah, bh) + (mm1(ah, bl) + mm1(al, bh))
 
 
 def stack(*parts):
     return jnp.concatenate([x for x in parts if x.shape[0]], 0)
 
 
-def invert(tiles):
-    rows = lax.broadcasted_iota(jnp.int32, (LEAF, W), 0)
-    lanes = lax.broadcasted_iota(jnp.int32, (LEAF, W), 1)
+def sweeps(panels, off, tick):
+    half = LEAF // 2
+    down = lax.broadcasted_iota(jnp.int32, (half, W), 0)
+    lane = lax.broadcasted_iota(jnp.int32, (half, W), 1)
+    pairs = [[p[:half], p[half:]] for p in panels]
+
+    def spread(x, at):
+        return [jnp.broadcast_to(x[:, at + c : at + c + 1], (half, W)) for c in range(half)]
+
+    for h in range(2):
+        at = off + half * h
+        inside = (lane >= at) & (lane < at + half)
+        cols = [spread(p[h], at) for p in pairs]
+        far = [spread(p[1 - h], at) for p in pairs]
+        mine = [jnp.where(inside, jnp.where(lane == down + at, 1.0, 0.0), p[h]) for p in pairs]
+        for i in range(0, half, 2):
+            for s, col in enumerate(cols):
+                p, q, r = (
+                    jnp.broadcast_to(col[c][k : k + 1], (half, W))
+                    for c, k in ((i, i), (i + 1, i), (i + 1, i + 1))
+                )
+                over = 1.0 / (p * r - q * q)
+                x = jnp.where(down == i, col[i] - 1.0, col[i])
+                y = jnp.where(down == i + 1, col[i + 1] - 1.0, col[i + 1])
+                x, y = r * x - q * y, p * y - q * x
+                for c in range(i + 2, min(i + 4, half)):
+                    ahead = x * jnp.broadcast_to(col[c][i : i + 1], (half, W)) + y * jnp.broadcast_to(
+                        col[c][i + 1 : i + 2], (half, W)
+                    )
+                    col[c] = col[c] - over * ahead
+                x, y = over * x, over * y
+                mine[s] = mine[s] - (
+                    x * jnp.broadcast_to(mine[s][i : i + 1], (half, W))
+                    + y * jnp.broadcast_to(mine[s][i + 1 : i + 2], (half, W))
+                )
+                for c in range(i + 4, half):
+                    col[c] = col[c] - (
+                        x * jnp.broadcast_to(col[c][i : i + 1], (half, W))
+                        + y * jnp.broadcast_to(col[c][i + 1 : i + 2], (half, W))
+                    )
+            tick()
+            tick()
+        for s, p in enumerate(pairs):
+            own = mine[s]
+            gone = total_of(
+                [far[s][c] * jnp.broadcast_to(own[c : c + 1], (half, W)) for c in range(half)]
+            )
+            p[h], p[1 - h] = own, jnp.where(inside, 0.0, p[1 - h]) - gone
+    return [jnp.concatenate(p, 0) for p in pairs]
+
+
+def total_of(terms):
+    while len(terms) > 1:
+        terms = [sum(terms[k : k + 2][1:], terms[k]) for k in range(0, len(terms), 2)]
+    return terms[0]
+
+
+def outer(column, q, off):
+    return total_of(
+        [
+            jnp.broadcast_to(column[:, off + c : off + c + 1], (LEAF, W))
+            * jnp.broadcast_to(q[c : c + 1], (LEAF, W))
+            for c in range(LEAF)
+        ]
+    )
+
+
+def invert(tiles, behind):
     along = lax.broadcasted_iota(jnp.int32, (W, W), 1)
+    state = {"ticks": 0, "done": 0}
+
+    def tick():
+        state["ticks"] += 1
+        while state["done"] * W < state["ticks"] * len(behind):
+            behind[state["done"]]()
+            state["done"] += 1
+
     for off in range(0, W, LEAF):
         end = off + LEAF
-        swept = [sweep(t[off:end], off, rows, lanes) for t in tiles]
+        swept = sweeps([t[off:end] for t in tiles], off, tick)
         new = []
         in_cols = (along >= off) & (along < end)
         for t, q in zip(tiles, swept):
             wide = stack(jnp.zeros((off, W), F32), q, jnp.zeros((W - end, W), F32))
-            base = jnp.where(in_cols, 0.0, t)
-
-            def less(low, high, t=t, wide=wide, base=base):
-                if low == high:
-                    return t[low:high]
-                return base[low:high] - mm(t[low:high], wide)
-
+            u = jnp.where(in_cols, 0.0, t) - mm(t, wide)
             soon = min(end + LEAF, W)
-            new.append(stack(less(0, off), q, less(end, soon), less(soon, W)))
+            parts = [u[:off], q]
+            if soon > end:
+                parts.append(
+                    jnp.where(in_cols[:LEAF], 0.0, t[end:soon]) - outer(t[end:soon], q, off)
+                )
+            new.append(stack(*parts, u[soon:]))
         tiles = new
     return tiles
 
@@ -114,7 +186,7 @@
 
 
 def solve(bands, counts, scale, nugget, own, *refs):
-    ships, kept, sent, work, tiles, diag = refs[:SHIP], *refs[SHIP:]
+    ships, kept, sent, work, tiles, diag, left = refs[:SHIP], *refs[SHIP:]
     band, sub = lax.axis_index("lon"), lax.axis_index("lat")
     apart = bands // SLOTS
     work[...] = own[...]
@@ -126,66 +198,81 @@
 
     down = lax.broadcasted_iota(jnp.int32, (W, W), 0)
     along = lax.broadcasted_iota(jnp.int32, (W, W), 1)
-    minus = jnp.full((W, W), -1.0, F32) / scale[0]
+    minus = jnp.full((W, W), -1.4426950408889634, F32) / scale[0]
     noise = jnp.where(down == along, nugget[0], 0.0)
     ones = jnp.ones((8, W), F32)
 
     def result(s):
         return sent if s == TASKS - 1 else kept.at[s]
 
-    def build(s, carry):
-        rows = [work[s, pl.ds(NBR * NF + 8 * d, 8), :] for d in range(3)]
-        cols = [r.T for r in rows]
-        for a in range(NBR + 1):
-            mine = [jnp.broadcast_to(c[:, a : a + 1], (W, W)) for c in cols]
-            for b in range(min(a, NBR - 1) + 1):
-                total = None
-                for d in range(3):
-                    gap = mine[d] - jnp.broadcast_to(rows[d][b : b + 1], (W, W))
-                    total = gap * gap if total is None else total + gap * gap
-                value = jnp.exp(jnp.sqrt(total) * minus)
-                if a == b:
-                    value = value + noise
-                tiles[s, a, b] = value
-        return carry
-
-    lax.fori_loop(0, TASKS, build, 0)
-    for s in range(TASKS):
-        result(s)[NF:] = jnp.ones((8, W), F32)
-
-    def eliminate(j, carry):
-        for s, g in enumerate(invert([tiles[s, j, j] for s in range(TASKS)])):
-            diag[s] = g
-        for at in range(NBR):
-
-            @pl.when(j == at)
-            def _():
-                for s in range(TASKS):
-                    g = diag[s]
-                    d = tiles[s, at, at]
-                    given = tiles[s, at + 1 :, at].reshape((NBR - at) * W, W)
-                    left = mm(given, g)
-                    left = left + mm(given - mm(left, d), g)
-                    for b in range(at + 1, NBR):
-                        fresh = mmt(left[(b - at - 1) * W :], tiles[s, b, at])
-                        tiles[s, b:, b] = tiles[s, b:, b] - fresh.reshape(NBR + 1 - b, W, W)
-                    result(s)[NF:] -= mmt(ones, left[-W:] * tiles[s, NBR, at])
-                    tiles[s, at + 1 :, at] = left.reshape(NBR - at, W, W)
-
-        return carry
-
-    lax.fori_loop(0, NBR, eliminate, 0)
-    for s in range(TASKS):
-        done = [None] * NBR
+    points = {}
+
+    def build(s, a, b):
+        if s not in points:
+            rows = [work[s, NBR * NF + 8 * d : NBR * NF + 8 * d + 8, :] for d in range(3)]
+            points[s] = rows, [r.T for r in rows]
+        rows, cols = points[s]
         total = None
-        for at in range(NBR - 1, -1, -1):
-            x = tiles[s, NBR, at]
-            for a in range(at + 1, NBR):
-                x = x - mm(done[a], tiles[s, a, at])
-            done[at] = x
-            part = mmt(work[s, at * NF : (at + 1) * NF, :], x)
-            total = part if total is None else total + part
-        result(s)[:NF] = total
+        for d in range(3):
+            gap = jnp.broadcast_to(cols[d][:, a : a + 1], (W, W)) - jnp.broadcast_to(
+                rows[d][b : b + 1], (W, W)
+            )
+            total = gap * gap if total is None else total + gap * gap
+        value = jnp.exp2(total * lax.rsqrt(jnp.maximum(total, 1e-30)) * minus)
+        tiles[s, a, b] = value + noise if a == b else value
+
+    def rows_of(s, b, low):
+        return stack(
+            tiles[s, low:, b].reshape((NBR + 1 - low) * W, W), work[s, b * NF : (b + 1) * NF, :]
+        )
+
+    def factor(s, j, given):
+        g = diag[j % 2, s]
+        left = mm3(given, g)
+        return left + mm3(given - mm(left, tiles[s, j, j]), g)
+
+    def near(s, j):
+        v = factor(s, j, tiles[s, j + 1, j])
+        tiles[s, j + 1, j + 1] -= mmt(v, tiles[s, j + 1, j])
+
+    def rest(s, j):
+        low = j + 2 if j + 1 < NBR else NBR
+        given = rows_of(s, j, low)
+        v = factor(s, j, given)
+        left[s, : v.shape[0]] = v
+        result(s)[NF:] -= mmt(ones, v[-W - NF : -NF] * tiles[s, NBR, j])
+        result(s)[:NF] += mmt(v[-NF:], tiles[s, NBR, j])
+
+    def update(s, j, b):
+        low = max(b, j + 2)
+        size = (NBR + 1 - low) * W
+        start = (low - (j + 2)) * W
+        fresh = mmt(left[s, start : start + size + NF], tiles[s, b, j])
+        tiles[s, low:, b] -= fresh[:size].reshape(NBR + 1 - low, W, W)
+        work[s, b * NF : (b + 1) * NF, :] -= fresh[size:]
+
+    tasks = range(TASKS)
+    for s in tasks:
+        result(s)[:NF] = jnp.zeros((NF, W), F32)
+        result(s)[NF:] = ones
+        build(s, 0, 0)
+    behind = [
+        functools.partial(build, s, a, b)
+        for a in range(1, NBR + 1)
+        for s in tasks
+        for b in range(min(a, NBR - 1) + 1)
+    ]
+    for j in range(NBR):
+        for s, g in enumerate(invert([tiles[s, j, j] for s in tasks], behind)):
+            diag[j % 2, s] = g
+        if j + 1 < NBR:
+            for s in tasks:
+                near(s, j)
+            behind = [functools.partial(rest, s, j) for s in tasks]
+            behind += [functools.partial(update, s, j, b) for b in range(j + 1, NBR) for s in tasks]
+        else:
+            for s in tasks:
+                rest(s, j)
 
 
 def assemble(bands, counts, kept, third, *refs):
@@ -248,7 +335,8 @@
         scratch_shapes=[
             pltpu.VMEM((TASKS, ROWS, W), F32),
             pltpu.VMEM((TASKS, NBR + 1, NBR, W, W), F32),
-            pltpu.VMEM((TASKS, W, W), F32),
+            pltpu.VMEM((2, TASKS, W, W), F32),
+            pltpu.VMEM((TASKS, (NBR - 1) * W + NF, W), F32),
         ],
         compiler_params=params(),
         name="solve",

time: 87 us -> 75.5 us (0.87)
  Pallas kernels: 46.2 us -> 34.6 us
    pallas_call x1, Pallas kernels: 43.6 us -> 32.1 us  [on_device(): pl.pallas_call(lambda *r: solve(bands, *r), out_shape=[arr(TASKS - 1, NF...]
where the time goes in v3:
time: 75.5 us; the launch traced here: 75.3 us
  Pallas kernels  34.6 us (46%)
  starting transfers between devices  25.2 us (33%)
  waiting for transfers between devices  11.8 us (16%)
  between operations  2.01 us (3%)
  local copies, waits for them, and re-layouts  1.65 us (2%)
    pallas_call x1, Pallas kernels, on_device(): pl.pallas_call(lambda *r: solve(bands, *r), out_shape=[arr(TASKS - 1, NF...  32.1 us
    ppermute x10, starting transfers between devices, trade(): return lax.ppermute(x, axes, pairs)  13.2 us
    ppermute x5, starting transfers between devices, shift(): return lax.ppermute(x, axes, pairs)  12 us
    ppermute x10, waiting for transfers between devices, trade(): return lax.ppermute(x, axes, pairs)  7.18 us
    ppermute x5, waiting for transfers between devices, shift(): return lax.ppermute(x, axes, pairs)  4.59 us
  transfers between devices with their start and end apart: 15, of which 5 were waited for; matrix products, arithmetic and copies ran while one was open for 0% of the time, Pallas kernels for 0%

profile of v3, /device:TPU:0, one launch (start us, length us, event | category | flops | bytes accessed | tf_op | source)
XLA Modules:
  0.0 75.3 jit_solution(577285415471356835)
XLA Ops:
  0.6 0.7 constant_dynamic-update-slice_fusion.1
  1.3 0.0 copy-start
  1.3 0.9 %constant_dynamic-update-slice_fusion.r_3_ = f32[35,8,128]{2,1,0:T(8,128)S(1)} fusion(f32[35,8,128]{2,1,0:T(8,128)S(1)} %constant_dynamic-update-slice_fusion.1, f32[32,8,128]{2,1,0:T(8,128)} %param.7), kind=kLoop, calls=%fused_computation | loop fusion | bytes 262144 | tf_op jit(solution)/shard_map/concatenate | solution.py:319
  2.3 0.1 collective-permute-start
  2.4 4.9 %collective-permute-start.1 = (f32[35,8,128]{2,1,0:T(8,128)S(1)}, f32[35,8,128]{2,1,0:T(8,128)S(1)}, u32[]{:S(2)}, u32[]{:S(2)}) collective-permute-start(f32[35,8,128]{2,1,0:T(8,128)S(1)} %constant_dynamic-update-slice_fusion.r_3_), channel_id=1, source_target_pairs={{0,3},{1,2},{2,5},{3,4},{4,7},{5,6},{6,9},{7,8},{8,11},{9,10},{10,... | collective-permute-start | bytes 430088 | tf_op jit(solution)/shard_map/ppermute | solution.py:304
  7.3 0.3 collective-permute-start.2
  7.6 3.7 %collective-permute-start.3 = (f32[35,8,128]{2,1,0:T(8,128)S(1)}, f32[35,8,128]{2,1,0:T(8,128)S(1)}, u32[]{:S(2)}, u32[]{:S(2)}) collective-permute-start(f32[35,8,128]{2,1,0:T(8,128)S(1)} %constant_dynamic-update-slice_fusion.r_3_), channel_id=1, source_target_pairs={{0,126},{1,127},{2,0},{3,1},{4,2},{5,3},{6,4},{7,5},{8,6},{9,7},{1... | collective-permute-start | bytes 430088 | tf_op jit(solution)/shard_map/ppermute | solution.py:304
  11.3 3.0 %collective-permute-start.4 = (f32[35,8,128]{2,1,0:T(8,128)S(1)}, f32[35,8,128]{2,1,0:T(8,128)S(1)}, u32[]{:S(2)}, u32[]{:S(2)}) collective-permute-start(f32[35,8,128]{2,1,0:T(8,128)S(1)} %constant_dynamic-update-slice_fusion.r_3_), channel_id=1, source_target_pairs={{0,127},{1,126},{2,1},{3,0},{4,3},{5,2},{6,5},{7,4},{8,7},{9,6},{1... | collective-permute-start | bytes 430088 | tf_op jit(solution)/shard_map/ppermute | solution.py:304
  14.3 0.0 collective-permute-done.r_1_
  14.3 1.7 %collective-permute-done.1.r_2_ = f32[35,8,128]{2,1,0:T(8,128)S(1)} collective-permute-done((f32[35,8,128]{2,1,0:T(8,128)S(1)}, f32[35,8,128]{2,1,0:T(8,128)S(1)}, u32[]{:S(2)}, u32[]{:S(2)}) %collective-permute-start.1) | collective-permute-done | bytes 143392 | tf_op jit(solution)/shard_map/ppermute | solution.py:304
  15.9 0.0 collective-permute-done.2.r_4_
  15.9 0.0 collective-permute-done.3.r_5_
  16.0 2.9 %collective-permute-done.4.r_6_ = f32[35,8,128]{2,1,0:T(8,128)S(1)} collective-permute-done((f32[35,8,128]{2,1,0:T(8,128)S(1)}, f32[35,8,128]{2,1,0:T(8,128)S(1)}, u32[]{:S(2)}, u32[]{:S(2)}) %collective-permute-start.4) | collective-permute-done | bytes 143392 | tf_op jit(solution)/shard_map/ppermute | solution.py:304
  18.9 0.0 copy-done
  18.9 1.3 %pack.1 = (f32[3,152,128]{2,1,0:T(8,128)S(1)}, f32[152,128]{1,0:T(8,128)S(1)}, f32[152,128]{1,0:T(8,128)S(1)}, f32[152,128]{1,0:T(8,128)S(1)}, f32[152,128]{1,0:T(8,128)S(1)}, /*index=5*/f32[152,128]{1,0:T(8,128)S(1)}) custom-call(s32[4,8]{1,0:T(4,128)S(1)} %copy-done, f32[35,8,128]{2,1,0:T(8,128)S(1)} %collective-permute-done.r_1_, ...), custom_call_target="tpu_custom_call" | custom-call | tf_op jit(solution)/shard_map/pack/pallas_call | solution.py:320
  20.1 0.1 collective-permute-start.5
  20.2 3.0 %collective-permute-start.6 = (f32[152,128]{1,0:T(8,128)S(1)}, f32[152,128]{1,0:T(8,128)S(1)}, u32[]{:S(2)}, u32[]{:S(2)}) collective-permute-start(f32[152,128]{1,0:T(8,128)S(1)} %get-tuple-element.12), channel_id=1, source_target_pairs={{0,48},{1,49},{2,50},{3,51},{4,52},{5,53},{6,54},{7,55},{8,56},{9,... | collective-permute-start | bytes 233480 | tf_op jit(solution)/shard_map/ppermute | solution.py:317
  23.2 0.9 %collective-permute-start.7 = (f32[152,128]{1,0:T(8,128)S(1)}, f32[152,128]{1,0:T(8,128)S(1)}, u32[]{:S(2)}, u32[]{:S(2)}) collective-permute-start(f32[152,128]{1,0:T(8,128)S(1)} %get-tuple-element.13), channel_id=1, source_target_pairs={{0,64},{1,65},{2,66},{3,67},{4,68},{5,69},{6,70},{7,71},{8,72},{9,... | collective-permute-start | bytes 233480 | tf_op jit(solution)/shard_map/ppermute | solution.py:317
  24.1 1.9 %collective-permute-start.8 = (f32[152,128]{1,0:T(8,128)S(1)}, f32[152,128]{1,0:T(8,128)S(1)}, u32[]{:S(2)}, u32[]{:S(2)}) collective-permute-start(f32[152,128]{1,0:T(8,128)S(1)} %get-tuple-element.14), channel_id=1, source_target_pairs={{0,80},{1,81},{2,82},{3,83},{4,84},{5,85},{6,86},{7,87},{8,88},{9,... | collective-permute-start | bytes 233480 | tf_op jit(solution)/shard_map/ppermute | solution.py:317
  26.0 0.9 %collective-permute-start.9 = (f32[152,128]{1,0:T(8,128)S(1)}, f32[152,128]{1,0:T(8,128)S(1)}, u32[]{:S(2)}, u32[]{:S(2)}) collective-permute-start(f32[152,128]{1,0:T(8,128)S(1)} %get-tuple-element.15), channel_id=1, source_target_pairs={{0,112},{1,113},{2,114},{3,115},{4,116},{5,117},{6,118},{7,119},{8... | collective-permute-start | bytes 233480 | tf_op jit(solution)/shard_map/ppermute | solution.py:317
  28.2 0.0 copy-start.1
  28.2 0.0 collective-permute-done.5.r_4_
  28.2 0.0 collective-permute-done.6.r_5_
  28.3 0.0 collective-permute-done.7.r_6_
  28.3 1.4 %collective-permute-done.8.r_7_ = f32[152,128]{1,0:T(8,128)S(1)} collective-permute-done((f32[152,128]{1,0:T(8,128)S(1)}, f32[152,128]{1,0:T(8,128)S(1)}, u32[]{:S(2)}, u32[]{:S(2)}) %collective-permute-start.8) | collective-permute-done | bytes 77856 | tf_op jit(solution)/shard_map/ppermute | solution.py:317
  29.7 2.8 %collective-permute-done.9.r_8_ = f32[152,128]{1,0:T(8,128)S(1)} collective-permute-done((f32[152,128]{1,0:T(8,128)S(1)}, f32[152,128]{1,0:T(8,128)S(1)}, u32[]{:S(2)}, u32[]{:S(2)}) %collective-permute-start.9) | collective-permute-done | bytes 77856 | tf_op jit(solution)/shard_map/ppermute | solution.py:317
  32.5 0.0 copy-done.1
  32.5 32.1 %solve.1 = (f32[2,40,128]{2,1,0:T(8,128)S(1)}, f32[40,128]{1,0:T(8,128)S(1)}) custom-call(s32[128]{0:T(128)S(1)} %copy-done.1, f32[1]{0:T(128)S(6)} %copy.9.r_1_, f32[1]{0:T(128)S(6)} %copy.10.r_2_, f32[3,152,128]{2,1,0:T(8,128)S(1)} %get-tuple-element.10.r_3_, f32[152,128]{1,0:T(8,128)S(1)} %collective-permute-done.5.r_4_, ...), custom_call_target="tpu_custom_call" | custom-call | tf_op jit(solution)/shard_map/solve/pallas_call | solution.py:330
  64.6 0.0 collective-permute-start.10
  64.6 0.7 collective-permute-start.11
  65.3 1.0 %collective-permute-start.12 = (f32[40,128]{1,0:T(8,128)S(1)}, f32[40,128]{1,0:T(8,128)S(1)}, u32[]{:S(2)}, u32[]{:S(2)}) collective-permute-start(f32[40,128]{1,0:T(8,128)S(1)} %get-tuple-element.17.r_2_), channel_id=1, source_target_pairs={{0,64},{1,65},{2,66},{3,67},{4,68},{5,69},{6,70},{7,71},{8,72},{9,... | collective-permute-start | bytes 61448 | tf_op jit(solution)/shard_map/ppermute | solution.py:317
  66.2 1.9 %collective-permute-start.13 = (f32[40,128]{1,0:T(8,128)S(1)}, f32[40,128]{1,0:T(8,128)S(1)}, u32[]{:S(2)}, u32[]{:S(2)}) collective-permute-start(f32[40,128]{1,0:T(8,128)S(1)} %get-tuple-element.17.r_2_), channel_id=1, source_target_pairs={{0,80},{1,81},{2,82},{3,83},{4,84},{5,85},{6,86},{7,87},{8,88},{9,... | collective-permute-start | bytes 61448 | tf_op jit(solution)/shard_map/ppermute | solution.py:317
  68.1 2.9 %collective-permute-start.14 = (f32[40,128]{1,0:T(8,128)S(1)}, f32[40,128]{1,0:T(8,128)S(1)}, u32[]{:S(2)}, u32[]{:S(2)}) collective-permute-start(f32[40,128]{1,0:T(8,128)S(1)} %get-tuple-element.17.r_2_), channel_id=1, source_target_pairs={{0,112},{1,113},{2,114},{3,115},{4,116},{5,117},{6,118},{7,119},{8... | collective-permute-start | bytes 61448 | tf_op jit(solution)/shard_map/ppermute | solution.py:317
  71.0 0.0 collective-permute-done.10.r_3_
  71.0 0.0 collective-permute-done.11.r_4_
  71.0 0.0 collective-permute-done.12.r_5_
  71.0 0.0 collective-permute-done.13.r_6_
  71.0 2.9 %collective-permute-done.14.r_7_ = f32[40,128]{1,0:T(8,128)S(1)} collective-permute-done((f32[40,128]{1,0:T(8,128)S(1)}, f32[40,128]{1,0:T(8,128)S(1)}, u32[]{:S(2)}, u32[]{:S(2)}) %collective-permute-start.14) | collective-permute-done | bytes 20512 | tf_op jit(solution)/shard_map/ppermute | solution.py:317
  74.0 1.3 %assemble.1 = (f32[32,8,128]{2,1,0:T(8,128)}, f32[8,128]{1,0:T(8,128)}) custom-call(s32[128]{0:T(128)S(1)} %copy-done.1, f32[2,40,128]{2,1,0:T(8,128)S(1)} %get-tuple-element.16.r_1_, f32[40,128]{1,0:T(8,128)S(1)} %get-tuple-element.17.r_2_, f32[40,128]{1,0:T(8,128)S(1)} %collective-permute-done.10.r_3_, f32[40,128]{1,0:T(8,128)S(1)} %collective-permute-done.11.r_4_, ...), custom_call_target="tpu_custom_call" | custom-call | tf_op jit(solution)/shard_map/assemble/pallas_call | solution.py:345
Async XLA Ops:
  1.3 17.5 %copy-start = (s32[4,8]{1,0:T(4,128)S(1)}, s32[4,8]{1,0:T(4,128)}, u32[]{:S(2)}) copy-start(s32[4,8]{1,0:T(4,128)} %r_0_.3) | copy-start | bytes 388
  2.3 12.0 %collective-permute-start = (f32[35,8,128]{2,1,0:T(8,128)S(1)}, f32[35,8,128]{2,1,0:T(8,128)S(1)}, u32[]{:S(2)}, u32[]{:S(2)}) collective-permute-start(f32[35,8,128]{2,1,0:T(8,128)S(1)} %constant_dynamic-update-slice_fusion.r_3_), channel_id=1, source_target_pairs={{0,2},{1,3},{2,4},{3,5},{4,6},{5,7},{6,8},{7,9},{8,10},{9,11},{10,... | collective-permute-start | bytes 430088 | tf_op jit(solution)/shard_map/ppermute | solution.py:304
  2.4 13.6 %collective-permute-start.1 = (f32[35,8,128]{2,1,0:T(8,128)S(1)}, f32[35,8,128]{2,1,0:T(8,128)S(1)}, u32[]{:S(2)}, u32[]{:S(2)}) collective-permute-start(f32[35,8,128]{2,1,0:T(8,128)S(1)} %constant_dynamic-update-slice_fusion.r_3_), channel_id=1, source_target_pairs={{0,3},{1,2},{2,5},{3,4},{4,7},{5,6},{6,9},{7,8},{8,11},{9,10},{10,... | collective-permute-start | bytes 430088 | tf_op jit(solution)/shard_map/ppermute | solution.py:304
  7.3 8.7 %collective-permute-start.2 = (f32[35,8,128]{2,1,0:T(8,128)S(1)}, f32[35,8,128]{2,1,0:T(8,128)S(1)}, u32[]{:S(2)}, u32[]{:S(2)}) collective-permute-start(f32[35,8,128]{2,1,0:T(8,128)S(1)} %constant_dynamic-update-slice_fusion.r_3_), channel_id=1, source_target_pairs={{0,1},{1,0},{2,3},{3,2},{4,5},{5,4},{6,7},{7,6},{8,9},{9,8},{10,11... | collective-permute-start | bytes 430088 | tf_op jit(solution)/shard_map/ppermute | solution.py:304
  7.6 8.4 %collective-permute-start.3 = (f32[35,8,128]{2,1,0:T(8,128)S(1)}, f32[35,8,128]{2,1,0:T(8,128)S(1)}, u32[]{:S(2)}, u32[]{:S(2)}) collective-permute-start(f32[35,8,128]{2,1,0:T(8,128)S(1)} %constant_dynamic-update-slice_fusion.r_3_), channel_id=1, source_target_pairs={{0,126},{1,127},{2,0},{3,1},{4,2},{5,3},{6,4},{7,5},{8,6},{9,7},{1... | collective-permute-start | bytes 430088 | tf_op jit(solution)/shard_map/ppermute | solution.py:304
  11.3 7.6 %collective-permute-start.4 = (f32[35,8,128]{2,1,0:T(8,128)S(1)}, f32[35,8,128]{2,1,0:T(8,128)S(1)}, u32[]{:S(2)}, u32[]{:S(2)}) collective-permute-start(f32[35,8,128]{2,1,0:T(8,128)S(1)} %constant_dynamic-update-slice_fusion.r_3_), channel_id=1, source_target_pairs={{0,127},{1,126},{2,1},{3,0},{4,3},{5,2},{6,5},{7,4},{8,7},{9,6},{1... | collective-permute-start | bytes 430088 | tf_op jit(solution)/shard_map/ppermute | solution.py:304
  20.1 8.1 %collective-permute-start.5 = (f32[152,128]{1,0:T(8,128)S(1)}, f32[152,128]{1,0:T(8,128)S(1)}, u32[]{:S(2)}, u32[]{:S(2)}) collective-permute-start(f32[152,128]{1,0:T(8,128)S(1)} %get-tuple-element.11), channel_id=1, source_target_pairs={{0,16},{1,17},{2,18},{3,19},{4,20},{5,21},{6,22},{7,23},{8,24},{9,... | collective-permute-start | bytes 233480 | tf_op jit(solution)/shard_map/ppermute | solution.py:317
  20.2 8.0 %collective-permute-start.6 = (f32[152,128]{1,0:T(8,128)S(1)}, f32[152,128]{1,0:T(8,128)S(1)}, u32[]{:S(2)}, u32[]{:S(2)}) collective-permute-start(f32[152,128]{1,0:T(8,128)S(1)} %get-tuple-element.12), channel_id=1, source_target_pairs={{0,48},{1,49},{2,50},{3,51},{4,52},{5,53},{6,54},{7,55},{8,56},{9,... | collective-permute-start | bytes 233480 | tf_op jit(solution)/shard_map/ppermute | solution.py:317
  23.2 5.0 %collective-permute-start.7 = (f32[152,128]{1,0:T(8,128)S(1)}, f32[152,128]{1,0:T(8,128)S(1)}, u32[]{:S(2)}, u32[]{:S(2)}) collective-permute-start(f32[152,128]{1,0:T(8,128)S(1)} %get-tuple-element.13), channel_id=1, source_target_pairs={{0,64},{1,65},{2,66},{3,67},{4,68},{5,69},{6,70},{7,71},{8,72},{9,... | collective-permute-start | bytes 233480 | tf_op jit(solution)/shard_map/ppermute | solution.py:317
  24.1 5.6 %collective-permute-start.8 = (f32[152,128]{1,0:T(8,128)S(1)}, f32[152,128]{1,0:T(8,128)S(1)}, u32[]{:S(2)}, u32[]{:S(2)}) collective-permute-start(f32[152,128]{1,0:T(8,128)S(1)} %get-tuple-element.14), channel_id=1, source_target_pairs={{0,80},{1,81},{2,82},{3,83},{4,84},{5,85},{6,86},{7,87},{8,88},{9,... | collective-permute-start | bytes 233480 | tf_op jit(solution)/shard_map/ppermute | solution.py:317
  26.0 6.5 %collective-permute-start.9 = (f32[152,128]{1,0:T(8,128)S(1)}, f32[152,128]{1,0:T(8,128)S(1)}, u32[]{:S(2)}, u32[]{:S(2)}) collective-permute-start(f32[152,128]{1,0:T(8,128)S(1)} %get-tuple-element.15), channel_id=1, source_target_pairs={{0,112},{1,113},{2,114},{3,115},{4,116},{5,117},{6,118},{7,119},{8... | collective-permute-start | bytes 233480 | tf_op jit(solution)/shard_map/ppermute | solution.py:317
  28.2 4.3 %copy-start.1 = (s32[128]{0:T(128)S(1)}, s32[128]{0:T(128)}, u32[]{:S(2)}) copy-start(s32[128]{0:T(128)} %r_0_.5) | copy-start | bytes 1540
  64.6 6.5 %collective-permute-start.10 = (f32[40,128]{1,0:T(8,128)S(1)}, f32[40,128]{1,0:T(8,128)S(1)}, u32[]{:S(2)}, u32[]{:S(2)}) collective-permute-start(f32[40,128]{1,0:T(8,128)S(1)} %get-tuple-element.17.r_2_), channel_id=1, source_target_pairs={{0,16},{1,17},{2,18},{3,19},{4,20},{5,21},{6,22},{7,23},{8,24},{9,... | collective-permute-start | bytes 61448 | tf_op jit(solution)/shard_map/ppermute | solution.py:317
  64.6 6.5 %collective-permute-start.11 = (f32[40,128]{1,0:T(8,128)S(1)}, f32[40,128]{1,0:T(8,128)S(1)}, u32[]{:S(2)}, u32[]{:S(2)}) collective-permute-start(f32[40,128]{1,0:T(8,128)S(1)} %get-tuple-element.17.r_2_), channel_id=1, source_target_pairs={{0,48},{1,49},{2,50},{3,51},{4,52},{5,53},{6,54},{7,55},{8,56},{9,... | collective-permute-start | bytes 61448 | tf_op jit(solution)/shard_map/ppermute | solution.py:317
  65.3 5.8 %collective-permute-start.12 = (f32[40,128]{1,0:T(8,128)S(1)}, f32[40,128]{1,0:T(8,128)S(1)}, u32[]{:S(2)}, u32[]{:S(2)}) collective-permute-start(f32[40,128]{1,0:T(8,128)S(1)} %get-tuple-element.17.r_2_), channel_id=1, source_target_pairs={{0,64},{1,65},{2,66},{3,67},{4,68},{5,69},{6,70},{7,71},{8,72},{9,... | collective-permute-start | bytes 61448 | tf_op jit(solution)/shard_map/ppermute | solution.py:317
  66.2 4.8 %collective-permute-start.13 = (f32[40,128]{1,0:T(8,128)S(1)}, f32[40,128]{1,0:T(8,128)S(1)}, u32[]{:S(2)}, u32[]{:S(2)}) collective-permute-start(f32[40,128]{1,0:T(8,128)S(1)} %get-tuple-element.17.r_2_), channel_id=1, source_target_pairs={{0,80},{1,81},{2,82},{3,83},{4,84},{5,85},{6,86},{7,87},{8,88},{9,... | collective-permute-start | bytes 61448 | tf_op jit(solution)/shard_map/ppermute | solution.py:317
  68.1 5.9 %collective-permute-start.14 = (f32[40,128]{1,0:T(8,128)S(1)}, f32[40,128]{1,0:T(8,128)S(1)}, u32[]{:S(2)}, u32[]{:S(2)}) collective-permute-start(f32[40,128]{1,0:T(8,128)S(1)} %get-tuple-element.17.r_2_), channel_id=1, source_target_pairs={{0,112},{1,113},{2,114},{3,115},{4,116},{5,117},{6,118},{7,119},{8... | collective-permute-start | bytes 61448 | tf_op jit(solution)/shard_map/ppermute | solution.py:317

commit v4 on v3

--- a/solution.py
+++ b/solution.py
@@ -7,7 +7,6 @@
 from jax.experimental.pallas import tpu as pltpu
 from jax.sharding import PartitionSpec as P
 
-HIGHEST = lax.Precision.HIGHEST
 LEAF = 16
 TASKS = 3
 NBR = 4
@@ -16,7 +15,7 @@
 SLOTS = 8
 SHIP = SLOTS - TASKS
 ROWS = NBR * NF + 24
-MASKS = (1, 3, 4, 5, 7)
+MASKS = (7, 5, 4, 3, 1)
 F32 = jnp.float32
 
 VMEM = pl.BlockSpec(memory_space=pltpu.VMEM)
@@ -27,35 +26,59 @@
     return pltpu.CompilerParams(vmem_limit_bytes=40 * 2**20)
 
 
+BF16 = jnp.bfloat16
+
+
+def dot(a, b, across):
+    return lax.dot_general(
+        a, b, (((1,), (1 if across else 0,)), ((), ())), preferred_element_type=F32
+    )
+
+
+def thirds(a):
+    high = a.astype(BF16)
+    gap = a - high.astype(F32)
+    middle = gap.astype(BF16)
+    return high, middle, (gap - middle.astype(F32)).astype(BF16)
+
+
+def halves(a):
+    high = a.astype(BF16)
+    return high, (a - high.astype(F32)).astype(BF16)
+
+
+def six(a, b, across):
+    a1, a2, a3 = a
+    b1, b2, b3 = b
+    return dot(
+        jnp.concatenate([a3, a1, a2, a2, a1, a1], 1),
+        jnp.concatenate([b1, b3, b2, b1, b2, b1], 1 if across else 0),
+        across,
+    )
+
+
+def turned(a, b):
+    a1, a2, a3 = thirds(a)
+    b1, b2, b3 = thirds(b)
+    return lax.dot_general(
+        jnp.concatenate([a3, a1, a2, a2, a1, a1], 0),
+        jnp.concatenate([b1, b3, b2, b1, b2, b1], 0),
+        (((0,), (0,)), ((), ())),
+        preferred_element_type=F32,
+    )
+
+
 def mm(a, b):
-    return lax.dot_general(
-        a, b, (((1,), (0,)), ((), ())), precision=HIGHEST, preferred_element_type=F32
-    )
+    return six(thirds(a), thirds(b), False)
 
 
 def mmt(a, b):
-    return lax.dot_general(
-        a, b, (((1,), (1,)), ((), ())), precision=HIGHEST, preferred_element_type=F32
-    )
-
-
-def halves(a):
-    high = a.astype(jnp.bfloat16)
-    return high, (a - high.astype(F32)).astype(jnp.bfloat16)
-
-
-def mm1(a, b):
-    return lax.dot_general(
-        a.astype(jnp.bfloat16),
-        b.astype(jnp.bfloat16),
-        (((1,), (0,)), ((), ())),
-        preferred_element_type=F32,
-    )
+    return six(thirds(a), thirds(b), True)
 
 
 def mm3(a, b):
-    (ah, al), (bh, bl) = halves(a), halves(b)
-    return mm1(ah, bh) + (mm1(ah, bl) + mm1(al, bh))
+    (a1, a2), (b1, b2) = halves(a), halves(b)
+    return dot(jnp.concatenate([a2, a1, a1], 1), jnp.concatenate([b1, b2, b1], 0), False)
 
 
 def stack(*parts):
@@ -119,16 +142,6 @@
     return terms[0]
 
 
-def outer(column, q, off):
-    return total_of(
-        [
-            jnp.broadcast_to(column[:, off + c : off + c + 1], (LEAF, W))
-            * jnp.broadcast_to(q[c : c + 1], (LEAF, W))
-            for c in range(LEAF)
-        ]
-    )
-
-
 def invert(tiles, behind):
     along = lax.broadcasted_iota(jnp.int32, (W, W), 1)
     state = {"ticks": 0, "done": 0}
@@ -144,16 +157,10 @@
         swept = sweeps([t[off:end] for t in tiles], off, tick)
         new = []
         in_cols = (along >= off) & (along < end)
+        swept_lanes = along[:LEAF] < off
         for t, q in zip(tiles, swept):
-            wide = stack(jnp.zeros((off, W), F32), q, jnp.zeros((W - end, W), F32))
-            u = jnp.where(in_cols, 0.0, t) - mm(t, wide)
-            soon = min(end + LEAF, W)
-            parts = [u[:off], q]
-            if soon > end:
-                parts.append(
-                    jnp.where(in_cols[:LEAF], 0.0, t[end:soon]) - outer(t[end:soon], q, off)
-                )
-            new.append(stack(*parts, u[soon:]))
+            u = jnp.where(in_cols, 0.0, t) - turned(jnp.where(swept_lanes, -t[off:end], t[off:end]), q)
+            new.append(stack(u[:off], q, u[end:]))
         tiles = new
     return tiles
 
@@ -207,19 +214,19 @@
 
     points = {}
 
-    def build(s, a, b):
+    def build(s, a):
         if s not in points:
             rows = [work[s, NBR * NF + 8 * d : NBR * NF + 8 * d + 8, :] for d in range(3)]
             points[s] = rows, [r.T for r in rows]
         rows, cols = points[s]
-        total = None
-        for d in range(3):
-            gap = jnp.broadcast_to(cols[d][:, a : a + 1], (W, W)) - jnp.broadcast_to(
-                rows[d][b : b + 1], (W, W)
-            )
-            total = gap * gap if total is None else total + gap * gap
-        value = jnp.exp2(total * lax.rsqrt(jnp.maximum(total, 1e-30)) * minus)
-        tiles[s, a, b] = value + noise if a == b else value
+        mine = [jnp.broadcast_to(c[:, a : a + 1], (W, W)) for c in cols]
+        for b in range(min(a, NBR - 1) + 1):
+            total = None
+            for d in range(3):
+                gap = mine[d] - jnp.broadcast_to(rows[d][b : b + 1], (W, W))
+                total = gap * gap if total is None else total + gap * gap
+            value = jnp.exp2(total * lax.rsqrt(jnp.maximum(total, 1e-30)) * minus)
+            tiles[s, a, b] = value + noise if a == b else value
 
     def rows_of(s, b, low):
         return stack(
@@ -255,13 +262,8 @@
     for s in tasks:
         result(s)[:NF] = jnp.zeros((NF, W), F32)
         result(s)[NF:] = ones
-        build(s, 0, 0)
-    behind = [
-        functools.partial(build, s, a, b)
-        for a in range(1, NBR + 1)
-        for s in tasks
-        for b in range(min(a, NBR - 1) + 1)
-    ]
+        build(s, 0)
+    behind = [functools.partial(build, s, a) for a in range(1, NBR + 1) for s in tasks]
     for j in range(NBR):
         for s, g in enumerate(invert([tiles[s, j, j] for s in tasks], behind)):
             diag[j % 2, s] = g
@@ -304,11 +306,9 @@
         return lax.ppermute(x, axes, pairs)
 
     def pool_of(x):
-        return [
-            x if (away, flip) == (0, 0) else shift(x, -away, flip)
-            for away in (-1, 0, 1)
-            for flip in (0, 1)
-        ]
+        other = shift(x, 0, 1)
+        before, after = shift(x, 1, 0), shift(x, -1, 0)
+        return [before, shift(other, 1, 0), x, other, after, shift(other, -1, 0)]
 
     def trade(x, mask):
         pairs = [

time: 75.5 us -> 71.8 us (0.951)
  waiting for transfers between devices: 11.8 us -> 7.83 us
  starting transfers between devices: 25.2 us -> 28.3 us
  Pallas kernels: 34.6 us -> 31.8 us
    ppermute x5, starting transfers between devices: 12 us -> 15.3 us  [shift(): return lax.ppermute(x, axes, pairs)]
    pallas_call x1, Pallas kernels: 32.1 us -> 29.3 us  [on_device(): pl.pallas_call(lambda *r: solve(bands, *r), out_shape=[arr(TASKS - 1, NF...]
    ppermute x10, waiting for transfers between devices: 7.18 us -> 5.05 us  [trade(): return lax.ppermute(x, axes, pairs)]
    ppermute x5, waiting for transfers between devices: 4.59 us -> 2.78 us  [shift(): return lax.ppermute(x, axes, pairs)]
  transfers between devices with their start and end apart: 15 -> 15, of which waited for: 5 -> 4; matrix products, arithmetic and copies ran while one was open for 0% -> 0% of each run, Pallas kernels for 0% -> 0%
where the time goes in v4:
time: 71.8 us; the launch traced here: 71.6 us
  Pallas kernels  31.8 us (44%)
  starting transfers between devices  28.3 us (39%)
  waiting for transfers between devices  7.83 us (11%)
  between operations  2.01 us (3%)
  local copies, waits for them, and re-layouts  1.65 us (2%)
    pallas_call x1, Pallas kernels, on_device(): pl.pallas_call(lambda *r: solve(bands, *r), out_shape=[arr(TASKS - 1, NF...  29.3 us
    ppermute x5, starting transfers between devices, shift(): return lax.ppermute(x, axes, pairs)  15.3 us
    ppermute x10, starting transfers between devices, trade(): return lax.ppermute(x, axes, pairs)  13 us
    ppermute x10, waiting for transfers between devices, trade(): return lax.ppermute(x, axes, pairs)  5.05 us
    ppermute x5, waiting for transfers between devices, shift(): return lax.ppermute(x, axes, pairs)  2.78 us
  transfers between devices with their start and end apart: 15, of which 4 were waited for; matrix products, arithmetic and copies ran while one was open for 0% of the time, Pallas kernels for 0%

profile of v4, /device:TPU:0, one launch (start us, length us, event | category | flops | bytes accessed | tf_op | source)
XLA Modules:
  0.0 71.6 jit_solution(4355376218959160014)
XLA Ops:
  0.6 0.7 constant_dynamic-update-slice_fusion.1
  1.3 0.0 copy-start
  1.3 0.9 %constant_dynamic-update-slice_fusion.r_3_ = f32[35,8,128]{2,1,0:T(8,128)S(1)} fusion(f32[35,8,128]{2,1,0:T(8,128)S(1)} %constant_dynamic-update-slice_fusion.1, f32[32,8,128]{2,1,0:T(8,128)} %param.7), kind=kLoop, calls=%fused_computation | loop fusion | bytes 262144 | tf_op jit(solution)/shard_map/concatenate | solution.py:319
  2.3 3.4 %collective-permute-start.1 = (f32[35,8,128]{2,1,0:T(8,128)S(1)}, f32[35,8,128]{2,1,0:T(8,128)S(1)}, u32[]{:S(2)}, u32[]{:S(2)}) collective-permute-start(f32[35,8,128]{2,1,0:T(8,128)S(1)} %constant_dynamic-update-slice_fusion.r_3_), channel_id=1, source_target_pairs={{0,1},{1,0},{2,3},{3,2},{4,5},{5,4},{6,7},{7,6},{8,9},{9,8},{10,11... | collective-permute-start | bytes 430088 | tf_op jit(solution)/shard_map/ppermute | solution.py:306
  5.6 0.0 collective-permute-start
  5.6 6.0 %collective-permute-start.3 = (f32[35,8,128]{2,1,0:T(8,128)S(1)}, f32[35,8,128]{2,1,0:T(8,128)S(1)}, u32[]{:S(2)}, u32[]{:S(2)}) collective-permute-start(f32[35,8,128]{2,1,0:T(8,128)S(1)} %constant_dynamic-update-slice_fusion.r_3_), channel_id=1, source_target_pairs={{0,126},{1,127},{2,0},{3,1},{4,2},{5,3},{6,4},{7,5},{8,6},{9,7},{1... | collective-permute-start | bytes 430088 | tf_op jit(solution)/shard_map/ppermute | solution.py:306
  11.6 0.0 collective-permute-done.1.r_4_
  11.6 0.0 collective-permute-start.2
  11.6 6.0 %collective-permute-start.4 = (f32[35,8,128]{2,1,0:T(8,128)S(1)}, f32[35,8,128]{2,1,0:T(8,128)S(1)}, u32[]{:S(2)}, u32[]{:S(2)}) collective-permute-start(f32[35,8,128]{2,1,0:T(8,128)S(1)} %collective-permute-done.1.r_4_), channel_id=1, source_target_pairs={{0,126},{1,127},{2,0},{3,1},{4,2},{5,3},{6,4},{7,5},{8,6},{9,7},{1... | collective-permute-start | bytes 430088 | tf_op jit(solution)/shard_map/ppermute | solution.py:306
  17.6 0.0 collective-permute-done.r_1_
  17.6 0.0 collective-permute-done.3.r_5_
  17.6 2.8 %collective-permute-done.2.r_2_ = f32[35,8,128]{2,1,0:T(8,128)S(1)} collective-permute-done((f32[35,8,128]{2,1,0:T(8,128)S(1)}, f32[35,8,128]{2,1,0:T(8,128)S(1)}, u32[]{:S(2)}, u32[]{:S(2)}) %collective-permute-start.2) | collective-permute-done | bytes 143392 | tf_op jit(solution)/shard_map/ppermute | solution.py:306
  20.3 0.0 collective-permute-done.4.r_6_
  20.3 0.0 copy-done
  20.3 1.3 %pack.1 = (f32[3,152,128]{2,1,0:T(8,128)S(1)}, f32[152,128]{1,0:T(8,128)S(1)}, f32[152,128]{1,0:T(8,128)S(1)}, f32[152,128]{1,0:T(8,128)S(1)}, f32[152,128]{1,0:T(8,128)S(1)}, /*index=5*/f32[152,128]{1,0:T(8,128)S(1)}) custom-call(s32[4,8]{1,0:T(4,128)S(1)} %copy-done, f32[35,8,128]{2,1,0:T(8,128)S(1)} %collective-permute-done.r_1_, ...), custom_call_target="tpu_custom_call" | custom-call | tf_op jit(solution)/shard_map/pack/pallas_call | solution.py:320
  21.6 0.1 collective-permute-start.5
  21.7 0.1 collective-permute-start.6
  21.8 1.1 %collective-permute-start.7 = (f32[152,128]{1,0:T(8,128)S(1)}, f32[152,128]{1,0:T(8,128)S(1)}, u32[]{:S(2)}, u32[]{:S(2)}) collective-permute-start(f32[152,128]{1,0:T(8,128)S(1)} %get-tuple-element.13), channel_id=1, source_target_pairs={{0,64},{1,65},{2,66},{3,67},{4,68},{5,69},{6,70},{7,71},{8,72},{9,... | collective-permute-start | bytes 233480 | tf_op jit(solution)/shard_map/ppermute | solution.py:317
  22.9 3.5 %collective-permute-start.8 = (f32[152,128]{1,0:T(8,128)S(1)}, f32[152,128]{1,0:T(8,128)S(1)}, u32[]{:S(2)}, u32[]{:S(2)}) collective-permute-start(f32[152,128]{1,0:T(8,128)S(1)} %get-tuple-element.14), channel_id=1, source_target_pairs={{0,48},{1,49},{2,50},{3,51},{4,52},{5,53},{6,54},{7,55},{8,56},{9,... | collective-permute-start | bytes 233480 | tf_op jit(solution)/shard_map/ppermute | solution.py:317
  26.4 1.7 %collective-permute-start.9 = (f32[152,128]{1,0:T(8,128)S(1)}, f32[152,128]{1,0:T(8,128)S(1)}, u32[]{:S(2)}, u32[]{:S(2)}) collective-permute-start(f32[152,128]{1,0:T(8,128)S(1)} %get-tuple-element.15), channel_id=1, source_target_pairs={{0,16},{1,17},{2,18},{3,19},{4,20},{5,21},{6,22},{7,23},{8,24},{9,... | collective-permute-start | bytes 233480 | tf_op jit(solution)/shard_map/ppermute | solution.py:317
  29.5 0.0 copy-start.1
  29.5 0.0 collective-permute-done.5.r_4_
  29.5 0.0 collective-permute-done.6.r_5_
  29.5 0.0 collective-permute-done.7.r_6_
  29.5 0.0 collective-permute-done.8.r_7_
  29.5 1.3 %collective-permute-done.9.r_8_ = f32[152,128]{1,0:T(8,128)S(1)} collective-permute-done((f32[152,128]{1,0:T(8,128)S(1)}, f32[152,128]{1,0:T(8,128)S(1)}, u32[]{:S(2)}, u32[]{:S(2)}) %collective-permute-start.9) | collective-permute-done | bytes 77856 | tf_op jit(solution)/shard_map/ppermute | solution.py:317
  30.8 0.0 copy-done.1
  30.8 29.3 %solve.1 = (f32[2,40,128]{2,1,0:T(8,128)S(1)}, f32[40,128]{1,0:T(8,128)S(1)}) custom-call(s32[128]{0:T(128)S(1)} %copy-done.1, f32[1]{0:T(128)S(6)} %copy.9.r_1_, f32[1]{0:T(128)S(6)} %copy.10.r_2_, f32[3,152,128]{2,1,0:T(8,128)S(1)} %get-tuple-element.10.r_3_, f32[152,128]{1,0:T(8,128)S(1)} %collective-permute-done.5.r_4_, ...), custom_call_target="tpu_custom_call" | custom-call | tf_op jit(solution)/shard_map/solve/pallas_call | solution.py:330
  60.1 1.6 %collective-permute-start.10 = (f32[40,128]{1,0:T(8,128)S(1)}, f32[40,128]{1,0:T(8,128)S(1)}, u32[]{:S(2)}, u32[]{:S(2)}) collective-permute-start(f32[40,128]{1,0:T(8,128)S(1)} %get-tuple-element.17.r_2_), channel_id=1, source_target_pairs={{0,112},{1,113},{2,114},{3,115},{4,116},{5,117},{6,118},{7,119},{8... | collective-permute-start | bytes 61448 | tf_op jit(solution)/shard_map/ppermute | solution.py:317
  61.7 1.1 %collective-permute-start.11 = (f32[40,128]{1,0:T(8,128)S(1)}, f32[40,128]{1,0:T(8,128)S(1)}, u32[]{:S(2)}, u32[]{:S(2)}) collective-permute-start(f32[40,128]{1,0:T(8,128)S(1)} %get-tuple-element.17.r_2_), channel_id=1, source_target_pairs={{0,80},{1,81},{2,82},{3,83},{4,84},{5,85},{6,86},{7,87},{8,88},{9,... | collective-permute-start | bytes 61448 | tf_op jit(solution)/shard_map/ppermute | solution.py:317
  62.8 1.1 %collective-permute-start.12 = (f32[40,128]{1,0:T(8,128)S(1)}, f32[40,128]{1,0:T(8,128)S(1)}, u32[]{:S(2)}, u32[]{:S(2)}) collective-permute-start(f32[40,128]{1,0:T(8,128)S(1)} %get-tuple-element.17.r_2_), channel_id=1, source_target_pairs={{0,64},{1,65},{2,66},{3,67},{4,68},{5,69},{6,70},{7,71},{8,72},{9,... | collective-permute-start | bytes 61448 | tf_op jit(solution)/shard_map/ppermute | solution.py:317
  63.9 2.6 %collective-permute-start.13 = (f32[40,128]{1,0:T(8,128)S(1)}, f32[40,128]{1,0:T(8,128)S(1)}, u32[]{:S(2)}, u32[]{:S(2)}) collective-permute-start(f32[40,128]{1,0:T(8,128)S(1)} %get-tuple-element.17.r_2_), channel_id=1, source_target_pairs={{0,48},{1,49},{2,50},{3,51},{4,52},{5,53},{6,54},{7,55},{8,56},{9,... | collective-permute-start | bytes 61448 | tf_op jit(solution)/shard_map/ppermute | solution.py:317
  66.5 0.0 collective-permute-start.14
  66.6 0.0 collective-permute-done.10.r_3_
  66.6 0.0 collective-permute-done.11.r_4_
  66.6 0.0 collective-permute-done.12.r_5_
  66.6 2.3 %collective-permute-done.13.r_6_ = f32[40,128]{1,0:T(8,128)S(1)} collective-permute-done((f32[40,128]{1,0:T(8,128)S(1)}, f32[40,128]{1,0:T(8,128)S(1)}, u32[]{:S(2)}, u32[]{:S(2)}) %collective-permute-start.13) | collective-permute-done | bytes 20512 | tf_op jit(solution)/shard_map/ppermute | solution.py:317
  68.9 1.4 %collective-permute-done.14.r_7_ = f32[40,128]{1,0:T(8,128)S(1)} collective-permute-done((f32[40,128]{1,0:T(8,128)S(1)}, f32[40,128]{1,0:T(8,128)S(1)}, u32[]{:S(2)}, u32[]{:S(2)}) %collective-permute-start.14) | collective-permute-done | bytes 20512 | tf_op jit(solution)/shard_map/ppermute | solution.py:317
  70.3 1.3 %assemble.1 = (f32[32,8,128]{2,1,0:T(8,128)}, f32[8,128]{1,0:T(8,128)}) custom-call(s32[128]{0:T(128)S(1)} %copy-done.1, f32[2,40,128]{2,1,0:T(8,128)S(1)} %get-tuple-element.16.r_1_, f32[40,128]{1,0:T(8,128)S(1)} %get-tuple-element.17.r_2_, f32[40,128]{1,0:T(8,128)S(1)} %collective-permute-done.10.r_3_, f32[40,128]{1,0:T(8,128)S(1)} %collective-permute-done.11.r_4_, ...), custom_call_target="tpu_custom_call" | custom-call | tf_op jit(solution)/shard_map/assemble/pallas_call | solution.py:345
Async XLA Ops:
  1.3 19.0 %copy-start = (s32[4,8]{1,0:T(4,128)S(1)}, s32[4,8]{1,0:T(4,128)}, u32[]{:S(2)}) copy-start(s32[4,8]{1,0:T(4,128)} %r_0_.3) | copy-start | bytes 388
  2.3 9.3 %collective-permute-start.1 = (f32[35,8,128]{2,1,0:T(8,128)S(1)}, f32[35,8,128]{2,1,0:T(8,128)S(1)}, u32[]{:S(2)}, u32[]{:S(2)}) collective-permute-start(f32[35,8,128]{2,1,0:T(8,128)S(1)} %constant_dynamic-update-slice_fusion.r_3_), channel_id=1, source_target_pairs={{0,1},{1,0},{2,3},{3,2},{4,5},{5,4},{6,7},{7,6},{8,9},{9,8},{10,11... | collective-permute-start | bytes 430088 | tf_op jit(solution)/shard_map/ppermute | solution.py:306
  5.6 11.9 %collective-permute-start = (f32[35,8,128]{2,1,0:T(8,128)S(1)}, f32[35,8,128]{2,1,0:T(8,128)S(1)}, u32[]{:S(2)}, u32[]{:S(2)}) collective-permute-start(f32[35,8,128]{2,1,0:T(8,128)S(1)} %constant_dynamic-update-slice_fusion.r_3_), channel_id=1, source_target_pairs={{0,2},{1,3},{2,4},{3,5},{4,6},{5,7},{6,8},{7,9},{8,10},{9,11},{10,... | collective-permute-start | bytes 430088 | tf_op jit(solution)/shard_map/ppermute | solution.py:306
  5.6 11.9 %collective-permute-start.3 = (f32[35,8,128]{2,1,0:T(8,128)S(1)}, f32[35,8,128]{2,1,0:T(8,128)S(1)}, u32[]{:S(2)}, u32[]{:S(2)}) collective-permute-start(f32[35,8,128]{2,1,0:T(8,128)S(1)} %constant_dynamic-update-slice_fusion.r_3_), channel_id=1, source_target_pairs={{0,126},{1,127},{2,0},{3,1},{4,2},{5,3},{6,4},{7,5},{8,6},{9,7},{1... | collective-permute-start | bytes 430088 | tf_op jit(solution)/shard_map/ppermute | solution.py:306
  11.6 8.7 %collective-permute-start.2 = (f32[35,8,128]{2,1,0:T(8,128)S(1)}, f32[35,8,128]{2,1,0:T(8,128)S(1)}, u32[]{:S(2)}, u32[]{:S(2)}) collective-permute-start(f32[35,8,128]{2,1,0:T(8,128)S(1)} %collective-permute-done.1.r_4_), channel_id=1, source_target_pairs={{0,2},{1,3},{2,4},{3,5},{4,6},{5,7},{6,8},{7,9},{8,10},{9,11},{10,... | collective-permute-start | bytes 430088 | tf_op jit(solution)/shard_map/ppermute | solution.py:306
  11.6 8.7 %collective-permute-start.4 = (f32[35,8,128]{2,1,0:T(8,128)S(1)}, f32[35,8,128]{2,1,0:T(8,128)S(1)}, u32[]{:S(2)}, u32[]{:S(2)}) collective-permute-start(f32[35,8,128]{2,1,0:T(8,128)S(1)} %collective-permute-done.1.r_4_), channel_id=1, source_target_pairs={{0,126},{1,127},{2,0},{3,1},{4,2},{5,3},{6,4},{7,5},{8,6},{9,7},{1... | collective-permute-start | bytes 430088 | tf_op jit(solution)/shard_map/ppermute | solution.py:306
  21.6 7.8 %collective-permute-start.5 = (f32[152,128]{1,0:T(8,128)S(1)}, f32[152,128]{1,0:T(8,128)S(1)}, u32[]{:S(2)}, u32[]{:S(2)}) collective-permute-start(f32[152,128]{1,0:T(8,128)S(1)} %get-tuple-element.11), channel_id=1, source_target_pairs={{0,112},{1,113},{2,114},{3,115},{4,116},{5,117},{6,118},{7,119},{8... | collective-permute-start | bytes 233480 | tf_op jit(solution)/shard_map/ppermute | solution.py:317
  21.7 7.8 %collective-permute-start.6 = (f32[152,128]{1,0:T(8,128)S(1)}, f32[152,128]{1,0:T(8,128)S(1)}, u32[]{:S(2)}, u32[]{:S(2)}) collective-permute-start(f32[152,128]{1,0:T(8,128)S(1)} %get-tuple-element.12), channel_id=1, source_target_pairs={{0,80},{1,81},{2,82},{3,83},{4,84},{5,85},{6,86},{7,87},{8,88},{9,... | collective-permute-start | bytes 233480 | tf_op jit(solution)/shard_map/ppermute | solution.py:317
  21.8 7.7 %collective-permute-start.7 = (f32[152,128]{1,0:T(8,128)S(1)}, f32[152,128]{1,0:T(8,128)S(1)}, u32[]{:S(2)}, u32[]{:S(2)}) collective-permute-start(f32[152,128]{1,0:T(8,128)S(1)} %get-tuple-element.13), channel_id=1, source_target_pairs={{0,64},{1,65},{2,66},{3,67},{4,68},{5,69},{6,70},{7,71},{8,72},{9,... | collective-permute-start | bytes 233480 | tf_op jit(solution)/shard_map/ppermute | solution.py:317
  22.9 6.6 %collective-permute-start.8 = (f32[152,128]{1,0:T(8,128)S(1)}, f32[152,128]{1,0:T(8,128)S(1)}, u32[]{:S(2)}, u32[]{:S(2)}) collective-permute-start(f32[152,128]{1,0:T(8,128)S(1)} %get-tuple-element.14), channel_id=1, source_target_pairs={{0,48},{1,49},{2,50},{3,51},{4,52},{5,53},{6,54},{7,55},{8,56},{9,... | collective-permute-start | bytes 233480 | tf_op jit(solution)/shard_map/ppermute | solution.py:317
  26.4 4.4 %collective-permute-start.9 = (f32[152,128]{1,0:T(8,128)S(1)}, f32[152,128]{1,0:T(8,128)S(1)}, u32[]{:S(2)}, u32[]{:S(2)}) collective-permute-start(f32[152,128]{1,0:T(8,128)S(1)} %get-tuple-element.15), channel_id=1, source_target_pairs={{0,16},{1,17},{2,18},{3,19},{4,20},{5,21},{6,22},{7,23},{8,24},{9,... | collective-permute-start | bytes 233480 | tf_op jit(solution)/shard_map/ppermute | solution.py:317
  29.5 1.4 %copy-start.1 = (s32[128]{0:T(128)S(1)}, s32[128]{0:T(128)}, u32[]{:S(2)}) copy-start(s32[128]{0:T(128)} %r_0_.5) | copy-start | bytes 1540
  60.1 6.5 %collective-permute-start.10 = (f32[40,128]{1,0:T(8,128)S(1)}, f32[40,128]{1,0:T(8,128)S(1)}, u32[]{:S(2)}, u32[]{:S(2)}) collective-permute-start(f32[40,128]{1,0:T(8,128)S(1)} %get-tuple-element.17.r_2_), channel_id=1, source_target_pairs={{0,112},{1,113},{2,114},{3,115},{4,116},{5,117},{6,118},{7,119},{8... | collective-permute-start | bytes 61448 | tf_op jit(solution)/shard_map/ppermute | solution.py:317
  61.7 4.9 %collective-permute-start.11 = (f32[40,128]{1,0:T(8,128)S(1)}, f32[40,128]{1,0:T(8,128)S(1)}, u32[]{:S(2)}, u32[]{:S(2)}) collective-permute-start(f32[40,128]{1,0:T(8,128)S(1)} %get-tuple-element.17.r_2_), channel_id=1, source_target_pairs={{0,80},{1,81},{2,82},{3,83},{4,84},{5,85},{6,86},{7,87},{8,88},{9,... | collective-permute-start | bytes 61448 | tf_op jit(solution)/shard_map/ppermute | solution.py:317
  62.8 3.8 %collective-permute-start.12 = (f32[40,128]{1,0:T(8,128)S(1)}, f32[40,128]{1,0:T(8,128)S(1)}, u32[]{:S(2)}, u32[]{:S(2)}) collective-permute-start(f32[40,128]{1,0:T(8,128)S(1)} %get-tuple-element.17.r_2_), channel_id=1, source_target_pairs={{0,64},{1,65},{2,66},{3,67},{4,68},{5,69},{6,70},{7,71},{8,72},{9,... | collective-permute-start | bytes 61448 | tf_op jit(solution)/shard_map/ppermute | solution.py:317
  63.9 5.0 %collective-permute-start.13 = (f32[40,128]{1,0:T(8,128)S(1)}, f32[40,128]{1,0:T(8,128)S(1)}, u32[]{:S(2)}, u32[]{:S(2)}) collective-permute-start(f32[40,128]{1,0:T(8,128)S(1)} %get-tuple-element.17.r_2_), channel_id=1, source_target_pairs={{0,48},{1,49},{2,50},{3,51},{4,52},{5,53},{6,54},{7,55},{8,56},{9,... | collective-permute-start | bytes 61448 | tf_op jit(solution)/shard_map/ppermute | solution.py:317
  66.5 3.8 %collective-permute-start.14 = (f32[40,128]{1,0:T(8,128)S(1)}, f32[40,128]{1,0:T(8,128)S(1)}, u32[]{:S(2)}, u32[]{:S(2)}) collective-permute-start(f32[40,128]{1,0:T(8,128)S(1)} %get-tuple-element.17.r_2_), channel_id=1, source_target_pairs={{0,16},{1,17},{2,18},{3,19},{4,20},{5,21},{6,22},{7,23},{8,24},{9,... | collective-permute-start | bytes 61448 | tf_op jit(solution)/shard_map/ppermute | solution.py:317

commit v5 on v4

--- a/solution.py
+++ b/solution.py
@@ -74,6 +74,11 @@
 
 def mmt(a, b):
     return six(thirds(a), thirds(b), True)
+
+
+def mm3t(a, b):
+    (a1, a2), (b1, b2) = halves(a), halves(b)
+    return dot(jnp.concatenate([a2, a1, a1], 1), jnp.concatenate([b1, b2, b1], 1), True)
 
 
 def mm3(a, b):
@@ -173,11 +178,17 @@
     return (side * 2 + flip) * SLOTS + block % SLOTS
 
 
+def join(points, values, other_points, other_values, pair):
+    for k, (p, v) in enumerate(((points, values), (other_points, other_values))):
+        pair[k, :3] = p[...]
+        pair[k, 3:] = v[...]
+
+
 def pack(bands, nb, *refs):
-    pools, own, ships, pool = refs[:6], refs[6], refs[7:-1], refs[-1]
+    pools, own, ships, pool = refs[:3], refs[3], refs[4:-1], refs[-1]
     band, sub = lax.axis_index("lon"), lax.axis_index("lat")
     for g in range(6):
-        pool[:, g * SLOTS : (g + 1) * SLOTS, :] = pools[g][...]
+        pool[:, g * SLOTS : (g + 1) * SLOTS, :] = pools[g // 2][g % 2]
     for s in range(SLOTS):
         dst = own.at[s] if s < TASKS else ships[s - TASKS]
         dst[NBR * NF :, :] = jnp.zeros((24, W), F32)
@@ -189,7 +200,7 @@
                 dst[NBR * NF + 8 * d + n : NBR * NF + 8 * d + n + 1, :] = got[d : d + 1]
         for d in range(3):
             at = NBR * NF + 8 * d + NBR
-            dst[at : at + 1, :] = pools[2][d, s : s + 1, :]
+            dst[at : at + 1, :] = pools[1][0, d, s : s + 1, :]
 
 
 def solve(bands, counts, scale, nugget, own, *refs):
@@ -239,8 +250,10 @@
         return left + mm3(given - mm(left, tiles[s, j, j]), g)
 
     def near(s, j):
-        v = factor(s, j, tiles[s, j + 1, j])
-        tiles[s, j + 1, j + 1] -= mmt(v, tiles[s, j + 1, j])
+        given = tiles[s, j + 1, j]
+        v = mm3(given, diag[j % 2, s])
+        gap = given - mm(v, tiles[s, j, j])
+        tiles[s, j + 1, j + 1] -= mmt(v, given) + mm3t(gap, v)
 
     def rest(s, j):
         low = j + 2 if j + 1 < NBR else NBR
@@ -305,22 +318,25 @@
         ]
         return lax.ppermute(x, axes, pairs)
 
-    def pool_of(x):
-        other = shift(x, 0, 1)
-        before, after = shift(x, 1, 0), shift(x, -1, 0)
-        return [before, shift(other, 1, 0), x, other, after, shift(other, -1, 0)]
-
     def trade(x, mask):
         pairs = [
             (l * 2 + h, (l ^ (mask * apart)) * 2 + h) for l in range(bands) for h in range(2)
         ]
         return lax.ppermute(x, axes, pairs)
 
-    pool = pool_of(jnp.concatenate([coords, observed], axis=0))
+    pair = pl.pallas_call(
+        join,
+        out_shape=arr(2, NF + 3, SLOTS, W),
+        in_specs=[VMEM] * 4,
+        out_specs=VMEM,
+        compiler_params=params(),
+        name="join",
+    )(coords, observed, shift(coords, 0, 1), shift(observed, 0, 1))
+    pool = [shift(pair, 1, 0), pair, shift(pair, -1, 0)]
     own, *out = pl.pallas_call(
         lambda *r: pack(bands, *r),
         out_shape=[arr(TASKS, ROWS, W)] + [arr(ROWS, W)] * SHIP,
-        in_specs=[SMEM] + [VMEM] * 6,
+        in_specs=[SMEM] + [VMEM] * 3,
         out_specs=[VMEM] * (1 + SHIP),
         scratch_shapes=[pltpu.VMEM((NF + 3, 6 * SLOTS, W), F32)],
         compiler_params=params(),
@@ -341,7 +357,7 @@
         compiler_params=params(),
         name="solve",
     )(counts, lengthscale, nugget, own, *ships)
-    backs = [trade(third, mask) for mask in MASKS]
+    backs = [trade(third, mask) for mask in reversed(MASKS)][::-1]
     return pl.pallas_call(
         lambda *r: assemble(bands, *r),
         out_shape=[arr(NF, SLOTS, W), arr(SLOTS, W)],

time: 71.8 us -> 72.4 us (level)
  waiting for transfers between devices: 7.83 us -> 14 us
  starting transfers between devices: 28.3 us -> 23 us
    ppermute x5 -> x4, waiting for transfers between devices: 2.78 us -> 9.48 us  [shift(): return lax.ppermute(x, axes, pairs)]
    ppermute x5 -> x4, starting transfers between devices: 15.3 us -> 9.64 us  [shift(): return lax.ppermute(x, axes, pairs)]
    concatenate x1 -> x0, local copies, waits for them, and re-layouts: 0.93 us -> none  [on_device(): pool = pool_of(jnp.concatenate([coords, observed], axis=0))]
    unnamed x5 -> x8, local copies, waits for them, and re-layouts: 0.72 us -> 1.62 us
  transfers between devices with their start and end apart: 15 -> 14, of which waited for: 4 -> 6; matrix products, arithmetic and copies ran while one was open for 0% -> 0% of each run, Pallas kernels for 0% -> 0%
where the time goes in v5:
time: 72.4 us; the launch traced here: 72.2 us
  Pallas kernels  31.6 us (44%)
  starting transfers between devices  23 us (32%)
  waiting for transfers between devices  14 us (19%)
  between operations  1.99 us (3%)
  local copies, waits for them, and re-layouts  1.62 us (2%)
    pallas_call x1, Pallas kernels, on_device(): pl.pallas_call(lambda *r: solve(bands, *r), out_shape=[arr(TASKS - 1, NF...  29 us
    ppermute x10, starting transfers between devices, trade(): return lax.ppermute(x, axes, pairs)  13.4 us
    ppermute x4, starting transfers between devices, shift(): return lax.ppermute(x, axes, pairs)  9.64 us
    ppermute x4, waiting for transfers between devices, shift(): return lax.ppermute(x, axes, pairs)  9.48 us
    ppermute x10, waiting for transfers between devices, trade(): return lax.ppermute(x, axes, pairs)  4.51 us
    unnamed x8, local copies, waits for them, and re-layouts  1.62 us
  transfers between devices with their start and end apart: 14, of which 6 were waited for; matrix products, arithmetic and copies ran while one was open for 0% of the time, Pallas kernels for 0%

profile of v5, /device:TPU:0, one launch (start us, length us, event | category | flops | bytes accessed | tf_op | source)
XLA Modules:
  0.0 72.2 jit_solution(699232699254226504)
XLA Ops:
  0.6 3.4 %collective-permute-start.1 = (f32[32,8,128]{2,1,0:T(8,128)}, f32[32,8,128]{2,1,0:T(8,128)S(1)}, u32[]{:S(2)}, u32[]{:S(2)}) collective-permute-start(f32[32,8,128]{2,1,0:T(8,128)} %values.1), channel_id=1, source_target_pairs={{0,1},{1,0},{2,3},{3,2},{4,5},{5,4},{6,7},{7,6},{8,9},{9,8},{10,11... | collective-permute-start | bytes 393224 | tf_op jit(solution)/shard_map/ppermute | solution.py:319
  4.0 0.3 collective-permute-start
  4.2 5.2 %collective-permute-done.other_points = f32[3,8,128]{2,1,0:T(8,128)S(1)} collective-permute-done((f32[3,8,128]{2,1,0:T(8,128)}, f32[3,8,128]{2,1,0:T(8,128)S(1)}, u32[]{:S(2)}, u32[]{:S(2)}) %collective-permute-start) | collective-permute-done | bytes 12320 | tf_op jit(solution)/shard_map/ppermute | solution.py:319
  9.4 0.0 collective-permute-done.1.other_values
  9.4 0.0 copy-start
  9.4 0.9 %copy-done = f32[32,8,128]{2,1,0:T(8,128)S(1)} copy-done((f32[32,8,128]{2,1,0:T(8,128)S(1)}, f32[32,8,128]{2,1,0:T(8,128)}, u32[]{:S(2)}) %copy-start) | copy-done | bytes 131096
  10.3 0.0 copy-start.1
  10.3 0.7 copy-done.1
  11.0 0.0 copy-start.2
  11.0 0.1 collective-permute-start.2
  11.1 6.0 %collective-permute-start.3 = (f32[2,35,8,128]{3,2,1,0:T(8,128)S(1)}, f32[2,35,8,128]{3,2,1,0:T(8,128)S(1)}, u32[]{:S(2)}, u32[]{:S(2)}) collective-permute-start(f32[2,35,8,128]{3,2,1,0:T(8,128)S(1)} %join.1.r_2_), channel_id=1, source_target_pairs={{0,126},{1,127},{2,0},{3,1},{4,2},{5,3},{6,4},{7,5},{8,6},{9,7},{1... | collective-permute-start | bytes 860168 | tf_op jit(solution)/shard_map/ppermute | solution.py:319
  17.1 4.3 %collective-permute-done.2.r_1_ = f32[2,35,8,128]{3,2,1,0:T(8,128)S(1)} collective-permute-done((f32[2,35,8,128]{3,2,1,0:T(8,128)S(1)}, f32[2,35,8,128]{3,2,1,0:T(8,128)S(1)}, u32[]{:S(2)}, u32[]{:S(2)}) %collective-permute-start.2) | collective-permute-done | bytes 286752 | tf_op jit(solution)/shard_map/ppermute | solution.py:319
  21.4 0.0 collective-permute-done.3.r_3_
  21.4 0.0 copy-done.2
  21.4 1.3 %pack.1 = (f32[3,152,128]{2,1,0:T(8,128)S(1)}, f32[152,128]{1,0:T(8,128)S(1)}, f32[152,128]{1,0:T(8,128)S(1)}, f32[152,128]{1,0:T(8,128)S(1)}, f32[152,128]{1,0:T(8,128)S(1)}, /*index=5*/f32[152,128]{1,0:T(8,128)S(1)}) custom-call(s32[4,8]{1,0:T(4,128)S(1)} %copy-done.2, f32[2,35,8,128]{3,2,1,0:T(8,128)S(1)} %collective-permute-done.2.r_1_, ...), custom_call_target="tpu_custom_call" | custom-call | tf_op jit(solution)/shard_map/pack/pallas_call | solution.py:336
  22.7 0.8 %collective-permute-start.4 = (f32[152,128]{1,0:T(8,128)S(1)}, f32[152,128]{1,0:T(8,128)S(1)}, u32[]{:S(2)}, u32[]{:S(2)}) collective-permute-start(f32[152,128]{1,0:T(8,128)S(1)} %get-tuple-element.11), channel_id=1, source_target_pairs={{0,112},{1,113},{2,114},{3,115},{4,116},{5,117},{6,118},{7,119},{8... | collective-permute-start | bytes 233480 | tf_op jit(solution)/shard_map/ppermute | solution.py:325
  23.5 1.0 %collective-permute-start.5 = (f32[152,128]{1,0:T(8,128)S(1)}, f32[152,128]{1,0:T(8,128)S(1)}, u32[]{:S(2)}, u32[]{:S(2)}) collective-permute-start(f32[152,128]{1,0:T(8,128)S(1)} %get-tuple-element.12), channel_id=1, source_target_pairs={{0,80},{1,81},{2,82},{3,83},{4,84},{5,85},{6,86},{7,87},{8,88},{9,... | collective-permute-start | bytes 233480 | tf_op jit(solution)/shard_map/ppermute | solution.py:325
  24.5 0.7 collective-permute-start.6
  25.2 2.3 %collective-permute-start.7 = (f32[152,128]{1,0:T(8,128)S(1)}, f32[152,128]{1,0:T(8,128)S(1)}, u32[]{:S(2)}, u32[]{:S(2)}) collective-permute-start(f32[152,128]{1,0:T(8,128)S(1)} %get-tuple-element.14), channel_id=1, source_target_pairs={{0,48},{1,49},{2,50},{3,51},{4,52},{5,53},{6,54},{7,55},{8,56},{9,... | collective-permute-start | bytes 233480 | tf_op jit(solution)/shard_map/ppermute | solution.py:325
  27.5 1.5 %collective-permute-start.8 = (f32[152,128]{1,0:T(8,128)S(1)}, f32[152,128]{1,0:T(8,128)S(1)}, u32[]{:S(2)}, u32[]{:S(2)}) collective-permute-start(f32[152,128]{1,0:T(8,128)S(1)} %get-tuple-element.15), channel_id=1, source_target_pairs={{0,16},{1,17},{2,18},{3,19},{4,20},{5,21},{6,22},{7,23},{8,24},{9,... | collective-permute-start | bytes 233480 | tf_op jit(solution)/shard_map/ppermute | solution.py:325
  30.3 0.0 copy-start.3
  30.3 0.0 collective-permute-done.4.r_4_
  30.3 0.0 collective-permute-done.5.r_5_
  30.3 0.5 collective-permute-done.6.r_6_
  30.8 0.0 collective-permute-done.7.r_7_
  30.8 1.0 %collective-permute-done.8.r_8_ = f32[152,128]{1,0:T(8,128)S(1)} collective-permute-done((f32[152,128]{1,0:T(8,128)S(1)}, f32[152,128]{1,0:T(8,128)S(1)}, u32[]{:S(2)}, u32[]{:S(2)}) %collective-permute-start.8) | collective-permute-done | bytes 77856 | tf_op jit(solution)/shard_map/ppermute | solution.py:325
  31.9 0.0 copy-done.3
  31.9 29.0 %solve.1 = (f32[2,40,128]{2,1,0:T(8,128)S(1)}, f32[40,128]{1,0:T(8,128)S(1)}) custom-call(s32[128]{0:T(128)S(1)} %copy-done.3, f32[1]{0:T(128)S(6)} %copy.8.r_1_, f32[1]{0:T(128)S(6)} %copy.9.r_2_, f32[3,152,128]{2,1,0:T(8,128)S(1)} %get-tuple-element.10.r_3_, f32[152,128]{1,0:T(8,128)S(1)} %collective-permute-done.4.r_4_, ...), custom_call_target="tpu_custom_call" | custom-call | tf_op jit(solution)/shard_map/solve/pallas_call | solution.py:346
  60.9 2.4 %collective-permute-start.10 = (f32[40,128]{1,0:T(8,128)S(1)}, f32[40,128]{1,0:T(8,128)S(1)}, u32[]{:S(2)}, u32[]{:S(2)}) collective-permute-start(f32[40,128]{1,0:T(8,128)S(1)} %get-tuple-element.17.r_2_), channel_id=1, source_target_pairs={{0,80},{1,81},{2,82},{3,83},{4,84},{5,85},{6,86},{7,87},{8,88},{9,... | collective-permute-start | bytes 61448 | tf_op jit(solution)/shard_map/ppermute | solution.py:325
  63.2 0.7 collective-permute-start.11
  63.9 0.7 collective-permute-start.12
  64.6 0.5 collective-permute-start.13
  65.0 2.9 %collective-permute-start.9 = (f32[40,128]{1,0:T(8,128)S(1)}, f32[40,128]{1,0:T(8,128)S(1)}, u32[]{:S(2)}, u32[]{:S(2)}) collective-permute-start(f32[40,128]{1,0:T(8,128)S(1)} %get-tuple-element.17.r_2_), channel_id=1, source_target_pairs={{0,112},{1,113},{2,114},{3,115},{4,116},{5,117},{6,118},{7,119},{8... | collective-permute-start | bytes 61448 | tf_op jit(solution)/shard_map/ppermute | solution.py:325
  67.9 0.0 collective-permute-done.10.r_4_
  67.9 0.0 collective-permute-done.11.r_5_
  68.0 1.0 %collective-permute-done.12.r_6_ = f32[40,128]{1,0:T(8,128)S(1)} collective-permute-done((f32[40,128]{1,0:T(8,128)S(1)}, f32[40,128]{1,0:T(8,128)S(1)}, u32[]{:S(2)}, u32[]{:S(2)}) %collective-permute-start.12) | collective-permute-done | bytes 20512 | tf_op jit(solution)/shard_map/ppermute | solution.py:325
  68.9 0.0 collective-permute-done.13.r_7_
  68.9 2.0 %collective-permute-done.9.r_3_ = f32[40,128]{1,0:T(8,128)S(1)} collective-permute-done((f32[40,128]{1,0:T(8,128)S(1)}, f32[40,128]{1,0:T(8,128)S(1)}, u32[]{:S(2)}, u32[]{:S(2)}) %collective-permute-start.9) | collective-permute-done | bytes 20512 | tf_op jit(solution)/shard_map/ppermute | solution.py:325
  70.9 1.3 %assemble.1 = (f32[32,8,128]{2,1,0:T(8,128)}, f32[8,128]{1,0:T(8,128)}) custom-call(s32[128]{0:T(128)S(1)} %copy-done.3, f32[2,40,128]{2,1,0:T(8,128)S(1)} %get-tuple-element.16.r_1_, f32[40,128]{1,0:T(8,128)S(1)} %get-tuple-element.17.r_2_, f32[40,128]{1,0:T(8,128)S(1)} %collective-permute-done.9.r_3_, f32[40,128]{1,0:T(8,128)S(1)} %collective-permute-done.10.r_4_, ...), custom_call_target="tpu_custom_call" | custom-call | tf_op jit(solution)/shard_map/assemble/pallas_call | solution.py:361
  (1 shorter events, 0.0 us)
Async XLA Ops:
  0.6 8.8 %collective-permute-start.1 = (f32[32,8,128]{2,1,0:T(8,128)}, f32[32,8,128]{2,1,0:T(8,128)S(1)}, u32[]{:S(2)}, u32[]{:S(2)}) collective-permute-start(f32[32,8,128]{2,1,0:T(8,128)} %values.1), channel_id=1, source_target_pairs={{0,1},{1,0},{2,3},{3,2},{4,5},{5,4},{6,7},{7,6},{8,9},{9,8},{10,11... | collective-permute-start | bytes 393224 | tf_op jit(solution)/shard_map/ppermute | solution.py:319
  4.0 5.4 %collective-permute-start = (f32[3,8,128]{2,1,0:T(8,128)}, f32[3,8,128]{2,1,0:T(8,128)S(1)}, u32[]{:S(2)}, u32[]{:S(2)}) collective-permute-start(f32[3,8,128]{2,1,0:T(8,128)} %points.1), channel_id=1, source_target_pairs={{0,1},{1,0},{2,3},{3,2},{4,5},{5,4},{6,7},{7,6},{8,9},{9,8},{10,11... | collective-permute-start | bytes 36872 | tf_op jit(solution)/shard_map/ppermute | solution.py:319
  9.4 0.9 %copy-start = (f32[32,8,128]{2,1,0:T(8,128)S(1)}, f32[32,8,128]{2,1,0:T(8,128)}, u32[]{:S(2)}) copy-start(f32[32,8,128]{2,1,0:T(8,128)} %values.1) | copy-start | bytes 393220
  10.3 0.7 copy-start.1
  11.0 10.4 %copy-start.2 = (s32[4,8]{1,0:T(4,128)S(1)}, s32[4,8]{1,0:T(4,128)}, u32[]{:S(2)}) copy-start(s32[4,8]{1,0:T(4,128)} %r_0_.3) | copy-start | bytes 388
  11.0 10.3 %collective-permute-start.2 = (f32[2,35,8,128]{3,2,1,0:T(8,128)S(1)}, f32[2,35,8,128]{3,2,1,0:T(8,128)S(1)}, u32[]{:S(2)}, u32[]{:S(2)}) collective-permute-start(f32[2,35,8,128]{3,2,1,0:T(8,128)S(1)} %join.1.r_2_), channel_id=1, source_target_pairs={{0,2},{1,3},{2,4},{3,5},{4,6},{5,7},{6,8},{7,9},{8,10},{9,11},{10,... | collective-permute-start | bytes 860168 | tf_op jit(solution)/shard_map/ppermute | solution.py:319
  11.1 10.3 %collective-permute-start.3 = (f32[2,35,8,128]{3,2,1,0:T(8,128)S(1)}, f32[2,35,8,128]{3,2,1,0:T(8,128)S(1)}, u32[]{:S(2)}, u32[]{:S(2)}) collective-permute-start(f32[2,35,8,128]{3,2,1,0:T(8,128)S(1)} %join.1.r_2_), channel_id=1, source_target_pairs={{0,126},{1,127},{2,0},{3,1},{4,2},{5,3},{6,4},{7,5},{8,6},{9,7},{1... | collective-permute-start | bytes 860168 | tf_op jit(solution)/shard_map/ppermute | solution.py:319
  22.7 7.6 %collective-permute-start.4 = (f32[152,128]{1,0:T(8,128)S(1)}, f32[152,128]{1,0:T(8,128)S(1)}, u32[]{:S(2)}, u32[]{:S(2)}) collective-permute-start(f32[152,128]{1,0:T(8,128)S(1)} %get-tuple-element.11), channel_id=1, source_target_pairs={{0,112},{1,113},{2,114},{3,115},{4,116},{5,117},{6,118},{7,119},{8... | collective-permute-start | bytes 233480 | tf_op jit(solution)/shard_map/ppermute | solution.py:325
  23.5 6.8 %collective-permute-start.5 = (f32[152,128]{1,0:T(8,128)S(1)}, f32[152,128]{1,0:T(8,128)S(1)}, u32[]{:S(2)}, u32[]{:S(2)}) collective-permute-start(f32[152,128]{1,0:T(8,128)S(1)} %get-tuple-element.12), channel_id=1, source_target_pairs={{0,80},{1,81},{2,82},{3,83},{4,84},{5,85},{6,86},{7,87},{8,88},{9,... | collective-permute-start | bytes 233480 | tf_op jit(solution)/shard_map/ppermute | solution.py:325
  24.5 6.3 %collective-permute-start.6 = (f32[152,128]{1,0:T(8,128)S(1)}, f32[152,128]{1,0:T(8,128)S(1)}, u32[]{:S(2)}, u32[]{:S(2)}) collective-permute-start(f32[152,128]{1,0:T(8,128)S(1)} %get-tuple-element.13), channel_id=1, source_target_pairs={{0,64},{1,65},{2,66},{3,67},{4,68},{5,69},{6,70},{7,71},{8,72},{9,... | collective-permute-start | bytes 233480 | tf_op jit(solution)/shard_map/ppermute | solution.py:325
  25.2 5.6 %collective-permute-start.7 = (f32[152,128]{1,0:T(8,128)S(1)}, f32[152,128]{1,0:T(8,128)S(1)}, u32[]{:S(2)}, u32[]{:S(2)}) collective-permute-start(f32[152,128]{1,0:T(8,128)S(1)} %get-tuple-element.14), channel_id=1, source_target_pairs={{0,48},{1,49},{2,50},{3,51},{4,52},{5,53},{6,54},{7,55},{8,56},{9,... | collective-permute-start | bytes 233480 | tf_op jit(solution)/shard_map/ppermute | solution.py:325
  27.5 4.4 %collective-permute-start.8 = (f32[152,128]{1,0:T(8,128)S(1)}, f32[152,128]{1,0:T(8,128)S(1)}, u32[]{:S(2)}, u32[]{:S(2)}) collective-permute-start(f32[152,128]{1,0:T(8,128)S(1)} %get-tuple-element.15), channel_id=1, source_target_pairs={{0,16},{1,17},{2,18},{3,19},{4,20},{5,21},{6,22},{7,23},{8,24},{9,... | collective-permute-start | bytes 233480 | tf_op jit(solution)/shard_map/ppermute | solution.py:325
  30.3 1.6 %copy-start.3 = (s32[128]{0:T(128)S(1)}, s32[128]{0:T(128)}, u32[]{:S(2)}) copy-start(s32[128]{0:T(128)} %r_0_.5) | copy-start | bytes 1540
  60.9 7.1 %collective-permute-start.10 = (f32[40,128]{1,0:T(8,128)S(1)}, f32[40,128]{1,0:T(8,128)S(1)}, u32[]{:S(2)}, u32[]{:S(2)}) collective-permute-start(f32[40,128]{1,0:T(8,128)S(1)} %get-tuple-element.17.r_2_), channel_id=1, source_target_pairs={{0,80},{1,81},{2,82},{3,83},{4,84},{5,85},{6,86},{7,87},{8,88},{9,... | collective-permute-start | bytes 61448 | tf_op jit(solution)/shard_map/ppermute | solution.py:325
  63.2 4.7 %collective-permute-start.11 = (f32[40,128]{1,0:T(8,128)S(1)}, f32[40,128]{1,0:T(8,128)S(1)}, u32[]{:S(2)}, u32[]{:S(2)}) collective-permute-start(f32[40,128]{1,0:T(8,128)S(1)} %get-tuple-element.17.r_2_), channel_id=1, source_target_pairs={{0,64},{1,65},{2,66},{3,67},{4,68},{5,69},{6,70},{7,71},{8,72},{9,... | collective-permute-start | bytes 61448 | tf_op jit(solution)/shard_map/ppermute | solution.py:325
  63.9 5.0 %collective-permute-start.12 = (f32[40,128]{1,0:T(8,128)S(1)}, f32[40,128]{1,0:T(8,128)S(1)}, u32[]{:S(2)}, u32[]{:S(2)}) collective-permute-start(f32[40,128]{1,0:T(8,128)S(1)} %get-tuple-element.17.r_2_), channel_id=1, source_target_pairs={{0,48},{1,49},{2,50},{3,51},{4,52},{5,53},{6,54},{7,55},{8,56},{9,... | collective-permute-start | bytes 61448 | tf_op jit(solution)/shard_map/ppermute | solution.py:325
  64.6 4.3 %collective-permute-start.13 = (f32[40,128]{1,0:T(8,128)S(1)}, f32[40,128]{1,0:T(8,128)S(1)}, u32[]{:S(2)}, u32[]{:S(2)}) collective-permute-start(f32[40,128]{1,0:T(8,128)S(1)} %get-tuple-element.17.r_2_), channel_id=1, source_target_pairs={{0,16},{1,17},{2,18},{3,19},{4,20},{5,21},{6,22},{7,23},{8,24},{9,... | collective-permute-start | bytes 61448 | tf_op jit(solution)/shard_map/ppermute | solution.py:325
  65.0 5.9 %collective-permute-start.9 = (f32[40,128]{1,0:T(8,128)S(1)}, f32[40,128]{1,0:T(8,128)S(1)}, u32[]{:S(2)}, u32[]{:S(2)}) collective-permute-start(f32[40,128]{1,0:T(8,128)S(1)} %get-tuple-element.17.r_2_), channel_id=1, source_target_pairs={{0,112},{1,113},{2,114},{3,115},{4,116},{5,117},{6,118},{7,119},{8... | collective-permute-start | bytes 61448 | tf_op jit(solution)/shard_map/ppermute | solution.py:325

commit v6 on v4

--- a/solution.py
+++ b/solution.py
@@ -74,6 +74,11 @@
 
 def mmt(a, b):
     return six(thirds(a), thirds(b), True)
+
+
+def mm3t(a, b):
+    (a1, a2), (b1, b2) = halves(a), halves(b)
+    return dot(jnp.concatenate([a2, a1, a1], 1), jnp.concatenate([b1, b2, b1], 1), True)
 
 
 def mm3(a, b):
@@ -169,6 +174,7 @@
     band = block // (2 * SLOTS)
     sub = (block // SLOTS) % 2
     side = (band - my_band + 1 + bands) % bands
+    side = jnp.where(my_band % 2 == 1, side, 2 - side)
     flip = jnp.where(sub == my_sub, 0, 1)
     return (side * 2 + flip) * SLOTS + block % SLOTS
 
@@ -239,8 +245,10 @@
         return left + mm3(given - mm(left, tiles[s, j, j]), g)
 
     def near(s, j):
-        v = factor(s, j, tiles[s, j + 1, j])
-        tiles[s, j + 1, j + 1] -= mmt(v, tiles[s, j + 1, j])
+        given = tiles[s, j + 1, j]
+        v = mm3(given, diag[j % 2, s])
+        gap = given - mm(v, tiles[s, j, j])
+        tiles[s, j + 1, j + 1] -= mmt(v, given) + mm3t(gap, v)
 
     def rest(s, j):
         low = j + 2 if j + 1 < NBR else NBR
@@ -305,10 +313,16 @@
         ]
         return lax.ppermute(x, axes, pairs)
 
+    def swap(x, odd):
+        pairs = [
+            (l * 2 + h, (((l + odd) ^ 1) - odd) % bands * 2 + h) for l in range(bands) for h in range(2)
+        ]
+        return lax.ppermute(x, axes, pairs)
+
     def pool_of(x):
         other = shift(x, 0, 1)
-        before, after = shift(x, 1, 0), shift(x, -1, 0)
-        return [before, shift(other, 1, 0), x, other, after, shift(other, -1, 0)]
+        chip, far = swap(x, 0), swap(x, 1)
+        return [chip, swap(other, 0), x, other, far, swap(other, 1)]
 
     def trade(x, mask):
         pairs = [

time: 71.8 us -> 72 us (level)
    ppermute x5 -> x1, starting transfers between devices: 15.3 us -> 3.36 us  [shift(): return lax.ppermute(x, axes, pairs)]
    ppermute x0 -> x4, starting transfers between devices: none -> 11.2 us  [swap(): return lax.ppermute(x, axes, pairs)]
    ppermute x0 -> x4, waiting for transfers between devices: none -> 4.04 us  [swap(): return lax.ppermute(x, axes, pairs)]
    ppermute x5 -> x1, waiting for transfers between devices: 2.78 us -> 0.01 us  [shift(): return lax.ppermute(x, axes, pairs)]
    ppermute x10, waiting for transfers between devices: 5.05 us -> 4.31 us  [trade(): return lax.ppermute(x, axes, pairs)]
    ppermute x10, starting transfers between devices: 13 us -> 13.7 us  [trade(): return lax.ppermute(x, axes, pairs)]
where the time goes in v6:
time: 72 us; the launch traced here: 71.9 us
  Pallas kernels  31.6 us (44%)
  starting transfers between devices  28.2 us (39%)
  waiting for transfers between devices  8.35 us (12%)
  between operations  2.01 us (3%)
  local copies, waits for them, and re-layouts  1.65 us (2%)
    pallas_call x1, Pallas kernels, on_device(): pl.pallas_call(lambda *r: solve(bands, *r), out_shape=[arr(TASKS - 1, NF...  29 us
    ppermute x10, starting transfers between devices, trade(): return lax.ppermute(x, axes, pairs)  13.7 us
    ppermute x4, starting transfers between devices, swap(): return lax.ppermute(x, axes, pairs)  11.2 us
    ppermute x10, waiting for transfers between devices, trade(): return lax.ppermute(x, axes, pairs)  4.31 us
    ppermute x4, waiting for transfers between devices, swap(): return lax.ppermute(x, axes, pairs)  4.04 us
    ppermute x1, starting transfers between devices, shift(): return lax.ppermute(x, axes, pairs)  3.36 us
  transfers between devices with their start and end apart: 15, of which 4 were waited for; matrix products, arithmetic and copies ran while one was open for 0% of the time, Pallas kernels for 0%

profile of v6, /device:TPU:0, one launch (start us, length us, event | category | flops | bytes accessed | tf_op | source)
XLA Modules:
  0.0 71.9 jit_solution(3034490290466841946)
XLA Ops:
  0.6 0.7 constant_dynamic-update-slice_fusion.1
  1.3 0.0 copy-start
  1.3 0.9 %constant_dynamic-update-slice_fusion.r_3_ = f32[35,8,128]{2,1,0:T(8,128)S(1)} fusion(f32[35,8,128]{2,1,0:T(8,128)S(1)} %constant_dynamic-update-slice_fusion.1, f32[32,8,128]{2,1,0:T(8,128)} %param.7), kind=kLoop, calls=%fused_computation | loop fusion | bytes 262144 | tf_op jit(solution)/shard_map/concatenate | solution.py:333
  2.3 3.4 %collective-permute-start.1 = (f32[35,8,128]{2,1,0:T(8,128)S(1)}, f32[35,8,128]{2,1,0:T(8,128)S(1)}, u32[]{:S(2)}, u32[]{:S(2)}) collective-permute-start(f32[35,8,128]{2,1,0:T(8,128)S(1)} %constant_dynamic-update-slice_fusion.r_3_), channel_id=1, source_target_pairs={{0,1},{1,0},{2,3},{3,2},{4,5},{5,4},{6,7},{7,6},{8,9},{9,8},{10,11... | collective-permute-start | bytes 430088 | tf_op jit(solution)/shard_map/ppermute | solution.py:314
  5.6 0.0 collective-permute-start
  5.6 6.5 %collective-permute-start.3 = (f32[35,8,128]{2,1,0:T(8,128)S(1)}, f32[35,8,128]{2,1,0:T(8,128)S(1)}, u32[]{:S(2)}, u32[]{:S(2)}) collective-permute-start(f32[35,8,128]{2,1,0:T(8,128)S(1)} %constant_dynamic-update-slice_fusion.r_3_), channel_id=1, source_target_pairs={{0,126},{1,127},{2,4},{3,5},{4,2},{5,3},{6,8},{7,9},{8,6},{9,7},{1... | collective-permute-start | bytes 430088 | tf_op jit(solution)/shard_map/ppermute | solution.py:320
  12.1 0.0 collective-permute-done.1.r_4_
  12.1 0.0 collective-permute-start.2
  12.1 4.7 %collective-permute-start.4 = (f32[35,8,128]{2,1,0:T(8,128)S(1)}, f32[35,8,128]{2,1,0:T(8,128)S(1)}, u32[]{:S(2)}, u32[]{:S(2)}) collective-permute-start(f32[35,8,128]{2,1,0:T(8,128)S(1)} %collective-permute-done.1.r_4_), channel_id=1, source_target_pairs={{0,126},{1,127},{2,4},{3,5},{4,2},{5,3},{6,8},{7,9},{8,6},{9,7},{1... | collective-permute-start | bytes 430088 | tf_op jit(solution)/shard_map/ppermute | solution.py:320
  16.8 0.0 collective-permute-done.r_1_
  16.8 0.0 collective-permute-done.3.r_5_
  16.8 0.0 collective-permute-done.2.r_2_
  16.8 4.0 %collective-permute-done.4.r_6_ = f32[35,8,128]{2,1,0:T(8,128)S(1)} collective-permute-done((f32[35,8,128]{2,1,0:T(8,128)S(1)}, f32[35,8,128]{2,1,0:T(8,128)S(1)}, u32[]{:S(2)}, u32[]{:S(2)}) %collective-permute-start.4) | collective-permute-done | bytes 143392 | tf_op jit(solution)/shard_map/ppermute | solution.py:320
  20.8 0.0 copy-done
  20.8 1.3 %pack.1 = (f32[3,152,128]{2,1,0:T(8,128)S(1)}, f32[152,128]{1,0:T(8,128)S(1)}, f32[152,128]{1,0:T(8,128)S(1)}, f32[152,128]{1,0:T(8,128)S(1)}, f32[152,128]{1,0:T(8,128)S(1)}, /*index=5*/f32[152,128]{1,0:T(8,128)S(1)}) custom-call(s32[4,8]{1,0:T(4,128)S(1)} %copy-done, f32[35,8,128]{2,1,0:T(8,128)S(1)} %collective-permute-done.r_1_, ...), custom_call_target="tpu_custom_call" | custom-call | tf_op jit(solution)/shard_map/pack/pallas_call | solution.py:334
  22.1 0.1 collective-permute-start.5
  22.2 0.1 collective-permute-start.6
  22.3 1.4 %collective-permute-start.7 = (f32[152,128]{1,0:T(8,128)S(1)}, f32[152,128]{1,0:T(8,128)S(1)}, u32[]{:S(2)}, u32[]{:S(2)}) collective-permute-start(f32[152,128]{1,0:T(8,128)S(1)} %get-tuple-element.13), channel_id=1, source_target_pairs={{0,64},{1,65},{2,66},{3,67},{4,68},{5,69},{6,70},{7,71},{8,72},{9,... | collective-permute-start | bytes 233480 | tf_op jit(solution)/shard_map/ppermute | solution.py:331
  23.7 3.2 %collective-permute-start.8 = (f32[152,128]{1,0:T(8,128)S(1)}, f32[152,128]{1,0:T(8,128)S(1)}, u32[]{:S(2)}, u32[]{:S(2)}) collective-permute-start(f32[152,128]{1,0:T(8,128)S(1)} %get-tuple-element.14), channel_id=1, source_target_pairs={{0,48},{1,49},{2,50},{3,51},{4,52},{5,53},{6,54},{7,55},{8,56},{9,... | collective-permute-start | bytes 233480 | tf_op jit(solution)/shard_map/ppermute | solution.py:331
  26.9 2.2 %collective-permute-start.9 = (f32[152,128]{1,0:T(8,128)S(1)}, f32[152,128]{1,0:T(8,128)S(1)}, u32[]{:S(2)}, u32[]{:S(2)}) collective-permute-start(f32[152,128]{1,0:T(8,128)S(1)} %get-tuple-element.15), channel_id=1, source_target_pairs={{0,16},{1,17},{2,18},{3,19},{4,20},{5,21},{6,22},{7,23},{8,24},{9,... | collective-permute-start | bytes 233480 | tf_op jit(solution)/shard_map/ppermute | solution.py:331
  30.4 0.0 copy-start.1
  30.4 0.0 collective-permute-done.5.r_4_
  30.4 0.0 collective-permute-done.6.r_5_
  30.4 0.0 collective-permute-done.7.r_6_
  30.4 0.0 collective-permute-done.8.r_7_
  30.5 1.0 %collective-permute-done.9.r_8_ = f32[152,128]{1,0:T(8,128)S(1)} collective-permute-done((f32[152,128]{1,0:T(8,128)S(1)}, f32[152,128]{1,0:T(8,128)S(1)}, u32[]{:S(2)}, u32[]{:S(2)}) %collective-permute-start.9) | collective-permute-done | bytes 77856 | tf_op jit(solution)/shard_map/ppermute | solution.py:331
  31.5 0.0 copy-done.1
  31.5 29.0 %solve.1 = (f32[2,40,128]{2,1,0:T(8,128)S(1)}, f32[40,128]{1,0:T(8,128)S(1)}) custom-call(s32[128]{0:T(128)S(1)} %copy-done.1, f32[1]{0:T(128)S(6)} %copy.9.r_1_, f32[1]{0:T(128)S(6)} %copy.10.r_2_, f32[3,152,128]{2,1,0:T(8,128)S(1)} %get-tuple-element.10.r_3_, f32[152,128]{1,0:T(8,128)S(1)} %collective-permute-done.5.r_4_, ...), custom_call_target="tpu_custom_call" | custom-call | tf_op jit(solution)/shard_map/solve/pallas_call | solution.py:344
  60.5 1.9 %collective-permute-start.10 = (f32[40,128]{1,0:T(8,128)S(1)}, f32[40,128]{1,0:T(8,128)S(1)}, u32[]{:S(2)}, u32[]{:S(2)}) collective-permute-start(f32[40,128]{1,0:T(8,128)S(1)} %get-tuple-element.17.r_2_), channel_id=1, source_target_pairs={{0,112},{1,113},{2,114},{3,115},{4,116},{5,117},{6,118},{7,119},{8... | collective-permute-start | bytes 61448 | tf_op jit(solution)/shard_map/ppermute | solution.py:331
  62.4 1.1 %collective-permute-start.11 = (f32[40,128]{1,0:T(8,128)S(1)}, f32[40,128]{1,0:T(8,128)S(1)}, u32[]{:S(2)}, u32[]{:S(2)}) collective-permute-start(f32[40,128]{1,0:T(8,128)S(1)} %get-tuple-element.17.r_2_), channel_id=1, source_target_pairs={{0,80},{1,81},{2,82},{3,83},{4,84},{5,85},{6,86},{7,87},{8,88},{9,... | collective-permute-start | bytes 61448 | tf_op jit(solution)/shard_map/ppermute | solution.py:331
  63.5 0.7 collective-permute-start.12
  64.2 2.6 %collective-permute-start.13 = (f32[40,128]{1,0:T(8,128)S(1)}, f32[40,128]{1,0:T(8,128)S(1)}, u32[]{:S(2)}, u32[]{:S(2)}) collective-permute-start(f32[40,128]{1,0:T(8,128)S(1)} %get-tuple-element.17.r_2_), channel_id=1, source_target_pairs={{0,48},{1,49},{2,50},{3,51},{4,52},{5,53},{6,54},{7,55},{8,56},{9,... | collective-permute-start | bytes 61448 | tf_op jit(solution)/shard_map/ppermute | solution.py:331
  66.8 0.5 collective-permute-start.14
  67.3 0.0 collective-permute-done.10.r_3_
  67.3 0.0 collective-permute-done.11.r_4_
  67.3 0.0 collective-permute-done.12.r_5_
  67.3 1.9 %collective-permute-done.13.r_6_ = f32[40,128]{1,0:T(8,128)S(1)} collective-permute-done((f32[40,128]{1,0:T(8,128)S(1)}, f32[40,128]{1,0:T(8,128)S(1)}, u32[]{:S(2)}, u32[]{:S(2)}) %collective-permute-start.13) | collective-permute-done | bytes 20512 | tf_op jit(solution)/shard_map/ppermute | solution.py:331
  69.2 1.4 %collective-permute-done.14.r_7_ = f32[40,128]{1,0:T(8,128)S(1)} collective-permute-done((f32[40,128]{1,0:T(8,128)S(1)}, f32[40,128]{1,0:T(8,128)S(1)}, u32[]{:S(2)}, u32[]{:S(2)}) %collective-permute-start.14) | collective-permute-done | bytes 20512 | tf_op jit(solution)/shard_map/ppermute | solution.py:331
  70.6 1.3 %assemble.1 = (f32[32,8,128]{2,1,0:T(8,128)}, f32[8,128]{1,0:T(8,128)}) custom-call(s32[128]{0:T(128)S(1)} %copy-done.1, f32[2,40,128]{2,1,0:T(8,128)S(1)} %get-tuple-element.16.r_1_, f32[40,128]{1,0:T(8,128)S(1)} %get-tuple-element.17.r_2_, f32[40,128]{1,0:T(8,128)S(1)} %collective-permute-done.10.r_3_, f32[40,128]{1,0:T(8,128)S(1)} %collective-permute-done.11.r_4_, ...), custom_call_target="tpu_custom_call" | custom-call | tf_op jit(solution)/shard_map/assemble/pallas_call | solution.py:359
Async XLA Ops:
  1.3 19.5 %copy-start = (s32[4,8]{1,0:T(4,128)S(1)}, s32[4,8]{1,0:T(4,128)}, u32[]{:S(2)}) copy-start(s32[4,8]{1,0:T(4,128)} %r_0_.3) | copy-start | bytes 388
  2.3 9.8 %collective-permute-start.1 = (f32[35,8,128]{2,1,0:T(8,128)S(1)}, f32[35,8,128]{2,1,0:T(8,128)S(1)}, u32[]{:S(2)}, u32[]{:S(2)}) collective-permute-start(f32[35,8,128]{2,1,0:T(8,128)S(1)} %constant_dynamic-update-slice_fusion.r_3_), channel_id=1, source_target_pairs={{0,1},{1,0},{2,3},{3,2},{4,5},{5,4},{6,7},{7,6},{8,9},{9,8},{10,11... | collective-permute-start | bytes 430088 | tf_op jit(solution)/shard_map/ppermute | solution.py:314
  5.6 11.2 %collective-permute-start = (f32[35,8,128]{2,1,0:T(8,128)S(1)}, f32[35,8,128]{2,1,0:T(8,128)S(1)}, u32[]{:S(2)}, u32[]{:S(2)}) collective-permute-start(f32[35,8,128]{2,1,0:T(8,128)S(1)} %constant_dynamic-update-slice_fusion.r_3_), channel_id=1, source_target_pairs={{0,2},{1,3},{2,0},{3,1},{4,6},{5,7},{6,4},{7,5},{8,10},{9,11},{10,... | collective-permute-start | bytes 430088 | tf_op jit(solution)/shard_map/ppermute | solution.py:320
  5.6 11.2 %collective-permute-start.3 = (f32[35,8,128]{2,1,0:T(8,128)S(1)}, f32[35,8,128]{2,1,0:T(8,128)S(1)}, u32[]{:S(2)}, u32[]{:S(2)}) collective-permute-start(f32[35,8,128]{2,1,0:T(8,128)S(1)} %constant_dynamic-update-slice_fusion.r_3_), channel_id=1, source_target_pairs={{0,126},{1,127},{2,4},{3,5},{4,2},{5,3},{6,8},{7,9},{8,6},{9,7},{1... | collective-permute-start | bytes 430088 | tf_op jit(solution)/shard_map/ppermute | solution.py:320
  12.1 4.7 %collective-permute-start.2 = (f32[35,8,128]{2,1,0:T(8,128)S(1)}, f32[35,8,128]{2,1,0:T(8,128)S(1)}, u32[]{:S(2)}, u32[]{:S(2)}) collective-permute-start(f32[35,8,128]{2,1,0:T(8,128)S(1)} %collective-permute-done.1.r_4_), channel_id=1, source_target_pairs={{0,2},{1,3},{2,0},{3,1},{4,6},{5,7},{6,4},{7,5},{8,10},{9,11},{10,... | collective-permute-start | bytes 430088 | tf_op jit(solution)/shard_map/ppermute | solution.py:320
  12.1 8.7 %collective-permute-start.4 = (f32[35,8,128]{2,1,0:T(8,128)S(1)}, f32[35,8,128]{2,1,0:T(8,128)S(1)}, u32[]{:S(2)}, u32[]{:S(2)}) collective-permute-start(f32[35,8,128]{2,1,0:T(8,128)S(1)} %collective-permute-done.1.r_4_), channel_id=1, source_target_pairs={{0,126},{1,127},{2,4},{3,5},{4,2},{5,3},{6,8},{7,9},{8,6},{9,7},{1... | collective-permute-start | bytes 430088 | tf_op jit(solution)/shard_map/ppermute | solution.py:320
  22.1 8.3 %collective-permute-start.5 = (f32[152,128]{1,0:T(8,128)S(1)}, f32[152,128]{1,0:T(8,128)S(1)}, u32[]{:S(2)}, u32[]{:S(2)}) collective-permute-start(f32[152,128]{1,0:T(8,128)S(1)} %get-tuple-element.11), channel_id=1, source_target_pairs={{0,112},{1,113},{2,114},{3,115},{4,116},{5,117},{6,118},{7,119},{8... | collective-permute-start | bytes 233480 | tf_op jit(solution)/shard_map/ppermute | solution.py:331
  22.2 8.2 %collective-permute-start.6 = (f32[152,128]{1,0:T(8,128)S(1)}, f32[152,128]{1,0:T(8,128)S(1)}, u32[]{:S(2)}, u32[]{:S(2)}) collective-permute-start(f32[152,128]{1,0:T(8,128)S(1)} %get-tuple-element.12), channel_id=1, source_target_pairs={{0,80},{1,81},{2,82},{3,83},{4,84},{5,85},{6,86},{7,87},{8,88},{9,... | collective-permute-start | bytes 233480 | tf_op jit(solution)/shard_map/ppermute | solution.py:331
  22.3 8.1 %collective-permute-start.7 = (f32[152,128]{1,0:T(8,128)S(1)}, f32[152,128]{1,0:T(8,128)S(1)}, u32[]{:S(2)}, u32[]{:S(2)}) collective-permute-start(f32[152,128]{1,0:T(8,128)S(1)} %get-tuple-element.13), channel_id=1, source_target_pairs={{0,64},{1,65},{2,66},{3,67},{4,68},{5,69},{6,70},{7,71},{8,72},{9,... | collective-permute-start | bytes 233480 | tf_op jit(solution)/shard_map/ppermute | solution.py:331
  23.7 6.7 %collective-permute-start.8 = (f32[152,128]{1,0:T(8,128)S(1)}, f32[152,128]{1,0:T(8,128)S(1)}, u32[]{:S(2)}, u32[]{:S(2)}) collective-permute-start(f32[152,128]{1,0:T(8,128)S(1)} %get-tuple-element.14), channel_id=1, source_target_pairs={{0,48},{1,49},{2,50},{3,51},{4,52},{5,53},{6,54},{7,55},{8,56},{9,... | collective-permute-start | bytes 233480 | tf_op jit(solution)/shard_map/ppermute | solution.py:331
  26.9 4.6 %collective-permute-start.9 = (f32[152,128]{1,0:T(8,128)S(1)}, f32[152,128]{1,0:T(8,128)S(1)}, u32[]{:S(2)}, u32[]{:S(2)}) collective-permute-start(f32[152,128]{1,0:T(8,128)S(1)} %get-tuple-element.15), channel_id=1, source_target_pairs={{0,16},{1,17},{2,18},{3,19},{4,20},{5,21},{6,22},{7,23},{8,24},{9,... | collective-permute-start | bytes 233480 | tf_op jit(solution)/shard_map/ppermute | solution.py:331
  30.4 1.1 %copy-start.1 = (s32[128]{0:T(128)S(1)}, s32[128]{0:T(128)}, u32[]{:S(2)}) copy-start(s32[128]{0:T(128)} %r_0_.5) | copy-start | bytes 1540
  60.5 6.8 %collective-permute-start.10 = (f32[40,128]{1,0:T(8,128)S(1)}, f32[40,128]{1,0:T(8,128)S(1)}, u32[]{:S(2)}, u32[]{:S(2)}) collective-permute-start(f32[40,128]{1,0:T(8,128)S(1)} %get-tuple-element.17.r_2_), channel_id=1, source_target_pairs={{0,112},{1,113},{2,114},{3,115},{4,116},{5,117},{6,118},{7,119},{8... | collective-permute-start | bytes 61448 | tf_op jit(solution)/shard_map/ppermute | solution.py:331
  62.4 4.9 %collective-permute-start.11 = (f32[40,128]{1,0:T(8,128)S(1)}, f32[40,128]{1,0:T(8,128)S(1)}, u32[]{:S(2)}, u32[]{:S(2)}) collective-permute-start(f32[40,128]{1,0:T(8,128)S(1)} %get-tuple-element.17.r_2_), channel_id=1, source_target_pairs={{0,80},{1,81},{2,82},{3,83},{4,84},{5,85},{6,86},{7,87},{8,88},{9,... | collective-permute-start | bytes 61448 | tf_op jit(solution)/shard_map/ppermute | solution.py:331
  63.5 3.8 %collective-permute-start.12 = (f32[40,128]{1,0:T(8,128)S(1)}, f32[40,128]{1,0:T(8,128)S(1)}, u32[]{:S(2)}, u32[]{:S(2)}) collective-permute-start(f32[40,128]{1,0:T(8,128)S(1)} %get-tuple-element.17.r_2_), channel_id=1, source_target_pairs={{0,64},{1,65},{2,66},{3,67},{4,68},{5,69},{6,70},{7,71},{8,72},{9,... | collective-permute-start | bytes 61448 | tf_op jit(solution)/shard_map/ppermute | solution.py:331
  64.2 5.0 %collective-permute-start.13 = (f32[40,128]{1,0:T(8,128)S(1)}, f32[40,128]{1,0:T(8,128)S(1)}, u32[]{:S(2)}, u32[]{:S(2)}) collective-permute-start(f32[40,128]{1,0:T(8,128)S(1)} %get-tuple-element.17.r_2_), channel_id=1, source_target_pairs={{0,48},{1,49},{2,50},{3,51},{4,52},{5,53},{6,54},{7,55},{8,56},{9,... | collective-permute-start | bytes 61448 | tf_op jit(solution)/shard_map/ppermute | solution.py:331
  66.8 3.8 %collective-permute-start.14 = (f32[40,128]{1,0:T(8,128)S(1)}, f32[40,128]{1,0:T(8,128)S(1)}, u32[]{:S(2)}, u32[]{:S(2)}) collective-permute-start(f32[40,128]{1,0:T(8,128)S(1)} %get-tuple-element.17.r_2_), channel_id=1, source_target_pairs={{0,16},{1,17},{2,18},{3,19},{4,20},{5,21},{6,22},{7,23},{8,24},{9,... | collective-permute-start | bytes 61448 | tf_op jit(solution)/shard_map/ppermute | solution.py:331

commit v7 on v6

--- a/solution.py
+++ b/solution.py
@@ -174,7 +174,6 @@
     band = block // (2 * SLOTS)
     sub = (block // SLOTS) % 2
     side = (band - my_band + 1 + bands) % bands
-    side = jnp.where(my_band % 2 == 1, side, 2 - side)
     flip = jnp.where(sub == my_sub, 0, 1)
     return (side * 2 + flip) * SLOTS + block % SLOTS
 
@@ -313,16 +312,12 @@
         ]
         return lax.ppermute(x, axes, pairs)
 
-    def swap(x, odd):
-        pairs = [
-            (l * 2 + h, (((l + odd) ^ 1) - odd) % bands * 2 + h) for l in range(bands) for h in range(2)
+    def pool_of(x):
+        return [
+            x if (away, flip) == (0, 0) else shift(x, -away, flip)
+            for away in (-1, 0, 1)
+            for flip in (0, 1)
         ]
-        return lax.ppermute(x, axes, pairs)
-
-    def pool_of(x):
-        other = shift(x, 0, 1)
-        chip, far = swap(x, 0), swap(x, 1)
-        return [chip, swap(other, 0), x, other, far, swap(other, 1)]
 
     def trade(x, mask):
         pairs = [

time: 72 us -> 71 us (0.986)
  starting transfers between devices: 28.2 us -> 25.5 us
  waiting for transfers between devices: 8.35 us -> 9.97 us
    ppermute x4 -> x0, starting transfers between devices: 11.2 us -> none  [swap(): return lax.ppermute(x, axes, pairs)]
    ppermute x1 -> x5, starting transfers between devices: 3.36 us -> 12 us  [shift(): return lax.ppermute(x, axes, pairs)]
    ppermute x1 -> x5, waiting for transfers between devices: 0.01 us -> 4.59 us  [shift(): return lax.ppermute(x, axes, pairs)]
    ppermute x4 -> x0, waiting for transfers between devices: 4.04 us -> none  [swap(): return lax.ppermute(x, axes, pairs)]
    ppermute x10, waiting for transfers between devices: 4.31 us -> 5.38 us  [trade(): return lax.ppermute(x, axes, pairs)]
  transfers between devices with their start and end apart: 15 -> 15, of which waited for: 4 -> 8; matrix products, arithmetic and copies ran while one was open for 0% -> 0% of each run, Pallas kernels for 0% -> 0%
where the time goes in v7:
time: 71 us; the launch traced here: 70.7 us
  Pallas kernels  31.6 us (45%)
  starting transfers between devices  25.5 us (36%)
  waiting for transfers between devices  9.97 us (14%)
  between operations  1.98 us (3%)
  local copies, waits for them, and re-layouts  1.65 us (2%)
    pallas_call x1, Pallas kernels, on_device(): pl.pallas_call(lambda *r: solve(bands, *r), out_shape=[arr(TASKS - 1, NF...  29 us
    ppermute x10, starting transfers between devices, trade(): return lax.ppermute(x, axes, pairs)  13.6 us
    ppermute x5, starting transfers between devices, shift(): return lax.ppermute(x, axes, pairs)  12 us
    ppermute x10, waiting for transfers between devices, trade(): return lax.ppermute(x, axes, pairs)  5.38 us
    ppermute x5, waiting for transfers between devices, shift(): return lax.ppermute(x, axes, pairs)  4.59 us
  transfers between devices with their start and end apart: 15, of which 8 were waited for; matrix products, arithmetic and copies ran while one was open for 0% of the time, Pallas kernels for 0%

profile of v7, /device:TPU:0, one launch (start us, length us, event | category | flops | bytes accessed | tf_op | source)
XLA Modules:
  0.0 70.7 jit_solution(15888686199335245981)
XLA Ops:
  0.6 0.7 %constant_dynamic-update-slice_fusion.1 = f32[35,8,128]{2,1,0:T(8,128)S(1)} fusion(f32[3,8,128]{2,1,0:T(8,128)} %param.6), kind=kLoop, calls=%fused_computation.1 | loop fusion | bytes 24576
  1.3 0.0 copy-start
  1.3 0.9 %constant_dynamic-update-slice_fusion.r_3_ = f32[35,8,128]{2,1,0:T(8,128)S(1)} fusion(f32[35,8,128]{2,1,0:T(8,128)S(1)} %constant_dynamic-update-slice_fusion.1, f32[32,8,128]{2,1,0:T(8,128)} %param.7), kind=kLoop, calls=%fused_computation | loop fusion | bytes 262144 | tf_op jit(solution)/shard_map/concatenate | solution.py:328
  2.3 0.1 collective-permute-start
  2.4 4.9 %collective-permute-start.1 = (f32[35,8,128]{2,1,0:T(8,128)S(1)}, f32[35,8,128]{2,1,0:T(8,128)S(1)}, u32[]{:S(2)}, u32[]{:S(2)}) collective-permute-start(f32[35,8,128]{2,1,0:T(8,128)S(1)} %constant_dynamic-update-slice_fusion.r_3_), channel_id=1, source_target_pairs={{0,3},{1,2},{2,5},{3,4},{4,7},{5,6},{6,9},{7,8},{8,11},{9,10},{10,... | collective-permute-start | bytes 430088 | tf_op jit(solution)/shard_map/ppermute | solution.py:313
  7.3 0.3 collective-permute-start.2
  7.6 3.7 %collective-permute-start.3 = (f32[35,8,128]{2,1,0:T(8,128)S(1)}, f32[35,8,128]{2,1,0:T(8,128)S(1)}, u32[]{:S(2)}, u32[]{:S(2)}) collective-permute-start(f32[35,8,128]{2,1,0:T(8,128)S(1)} %constant_dynamic-update-slice_fusion.r_3_), channel_id=1, source_target_pairs={{0,126},{1,127},{2,0},{3,1},{4,2},{5,3},{6,4},{7,5},{8,6},{9,7},{1... | collective-permute-start | bytes 430088 | tf_op jit(solution)/shard_map/ppermute | solution.py:313
  11.3 3.0 %collective-permute-start.4 = (f32[35,8,128]{2,1,0:T(8,128)S(1)}, f32[35,8,128]{2,1,0:T(8,128)S(1)}, u32[]{:S(2)}, u32[]{:S(2)}) collective-permute-start(f32[35,8,128]{2,1,0:T(8,128)S(1)} %constant_dynamic-update-slice_fusion.r_3_), channel_id=1, source_target_pairs={{0,127},{1,126},{2,1},{3,0},{4,3},{5,2},{6,5},{7,4},{8,7},{9,6},{1... | collective-permute-start | bytes 430088 | tf_op jit(solution)/shard_map/ppermute | solution.py:313
  14.3 0.0 collective-permute-done.r_1_
  14.3 1.7 %collective-permute-done.1.r_2_ = f32[35,8,128]{2,1,0:T(8,128)S(1)} collective-permute-done((f32[35,8,128]{2,1,0:T(8,128)S(1)}, f32[35,8,128]{2,1,0:T(8,128)S(1)}, u32[]{:S(2)}, u32[]{:S(2)}) %collective-permute-start.1) | collective-permute-done | bytes 143392 | tf_op jit(solution)/shard_map/ppermute | solution.py:313
  15.9 0.0 collective-permute-done.2.r_4_
  15.9 0.0 collective-permute-done.3.r_5_
  16.0 2.9 %collective-permute-done.4.r_6_ = f32[35,8,128]{2,1,0:T(8,128)S(1)} collective-permute-done((f32[35,8,128]{2,1,0:T(8,128)S(1)}, f32[35,8,128]{2,1,0:T(8,128)S(1)}, u32[]{:S(2)}, u32[]{:S(2)}) %collective-permute-start.4) | collective-permute-done | bytes 143392 | tf_op jit(solution)/shard_map/ppermute | solution.py:313
  18.9 0.0 copy-done
  18.9 1.3 %pack.1 = (f32[3,152,128]{2,1,0:T(8,128)S(1)}, f32[152,128]{1,0:T(8,128)S(1)}, f32[152,128]{1,0:T(8,128)S(1)}, f32[152,128]{1,0:T(8,128)S(1)}, f32[152,128]{1,0:T(8,128)S(1)}, /*index=5*/f32[152,128]{1,0:T(8,128)S(1)}) custom-call(s32[4,8]{1,0:T(4,128)S(1)} %copy-done, f32[35,8,128]{2,1,0:T(8,128)S(1)} %collective-permute-done.r_1_, ...), custom_call_target="tpu_custom_call" | custom-call | tf_op jit(solution)/shard_map/pack/pallas_call | solution.py:329
  20.1 3.3 %collective-permute-start.5 = (f32[152,128]{1,0:T(8,128)S(1)}, f32[152,128]{1,0:T(8,128)S(1)}, u32[]{:S(2)}, u32[]{:S(2)}) collective-permute-start(f32[152,128]{1,0:T(8,128)S(1)} %get-tuple-element.11), channel_id=1, source_target_pairs={{0,112},{1,113},{2,114},{3,115},{4,116},{5,117},{6,118},{7,119},{8... | collective-permute-start | bytes 233480 | tf_op jit(solution)/shard_map/ppermute | solution.py:326
  23.4 0.0 collective-permute-start.6
  23.4 1.1 %collective-permute-start.7 = (f32[152,128]{1,0:T(8,128)S(1)}, f32[152,128]{1,0:T(8,128)S(1)}, u32[]{:S(2)}, u32[]{:S(2)}) collective-permute-start(f32[152,128]{1,0:T(8,128)S(1)} %get-tuple-element.13), channel_id=1, source_target_pairs={{0,64},{1,65},{2,66},{3,67},{4,68},{5,69},{6,70},{7,71},{8,72},{9,... | collective-permute-start | bytes 233480 | tf_op jit(solution)/shard_map/ppermute | solution.py:326
  24.6 1.0 %collective-permute-start.8 = (f32[152,128]{1,0:T(8,128)S(1)}, f32[152,128]{1,0:T(8,128)S(1)}, u32[]{:S(2)}, u32[]{:S(2)}) collective-permute-start(f32[152,128]{1,0:T(8,128)S(1)} %get-tuple-element.14), channel_id=1, source_target_pairs={{0,48},{1,49},{2,50},{3,51},{4,52},{5,53},{6,54},{7,55},{8,56},{9,... | collective-permute-start | bytes 233480 | tf_op jit(solution)/shard_map/ppermute | solution.py:326
  25.5 1.4 %collective-permute-start.9 = (f32[152,128]{1,0:T(8,128)S(1)}, f32[152,128]{1,0:T(8,128)S(1)}, u32[]{:S(2)}, u32[]{:S(2)}) collective-permute-start(f32[152,128]{1,0:T(8,128)S(1)} %get-tuple-element.15), channel_id=1, source_target_pairs={{0,16},{1,17},{2,18},{3,19},{4,20},{5,21},{6,22},{7,23},{8,24},{9,... | collective-permute-start | bytes 233480 | tf_op jit(solution)/shard_map/ppermute | solution.py:326
  28.2 0.0 copy-start.1
  28.2 0.0 collective-permute-done.5.r_4_
  28.2 1.1 %collective-permute-done.6.r_5_ = f32[152,128]{1,0:T(8,128)S(1)} collective-permute-done((f32[152,128]{1,0:T(8,128)S(1)}, f32[152,128]{1,0:T(8,128)S(1)}, u32[]{:S(2)}, u32[]{:S(2)}) %collective-permute-start.6) | collective-permute-done | bytes 77856 | tf_op jit(solution)/shard_map/ppermute | solution.py:326
  29.3 0.8 %collective-permute-done.7.r_6_ = f32[152,128]{1,0:T(8,128)S(1)} collective-permute-done((f32[152,128]{1,0:T(8,128)S(1)}, f32[152,128]{1,0:T(8,128)S(1)}, u32[]{:S(2)}, u32[]{:S(2)}) %collective-permute-start.7) | collective-permute-done | bytes 77856 | tf_op jit(solution)/shard_map/ppermute | solution.py:326
  30.1 0.1 collective-permute-done.8.r_7_
  30.2 0.0 collective-permute-done.9.r_8_
  30.2 0.0 copy-done.1
  30.2 29.0 %solve.1 = (f32[2,40,128]{2,1,0:T(8,128)S(1)}, f32[40,128]{1,0:T(8,128)S(1)}) custom-call(s32[128]{0:T(128)S(1)} %copy-done.1, f32[1]{0:T(128)S(6)} %copy.9.r_1_, f32[1]{0:T(128)S(6)} %copy.10.r_2_, f32[3,152,128]{2,1,0:T(8,128)S(1)} %get-tuple-element.10.r_3_, f32[152,128]{1,0:T(8,128)S(1)} %collective-permute-done.5.r_4_, ...), custom_call_target="tpu_custom_call" | custom-call | tf_op jit(solution)/shard_map/solve/pallas_call | solution.py:339
  59.3 2.4 %collective-permute-start.10 = (f32[40,128]{1,0:T(8,128)S(1)}, f32[40,128]{1,0:T(8,128)S(1)}, u32[]{:S(2)}, u32[]{:S(2)}) collective-permute-start(f32[40,128]{1,0:T(8,128)S(1)} %get-tuple-element.17.r_2_), channel_id=1, source_target_pairs={{0,112},{1,113},{2,114},{3,115},{4,116},{5,117},{6,118},{7,119},{8... | collective-permute-start | bytes 61448 | tf_op jit(solution)/shard_map/ppermute | solution.py:326
  61.7 1.6 %collective-permute-start.11 = (f32[40,128]{1,0:T(8,128)S(1)}, f32[40,128]{1,0:T(8,128)S(1)}, u32[]{:S(2)}, u32[]{:S(2)}) collective-permute-start(f32[40,128]{1,0:T(8,128)S(1)} %get-tuple-element.17.r_2_), channel_id=1, source_target_pairs={{0,80},{1,81},{2,82},{3,83},{4,84},{5,85},{6,86},{7,87},{8,88},{9,... | collective-permute-start | bytes 61448 | tf_op jit(solution)/shard_map/ppermute | solution.py:326
  63.3 1.1 %collective-permute-start.12 = (f32[40,128]{1,0:T(8,128)S(1)}, f32[40,128]{1,0:T(8,128)S(1)}, u32[]{:S(2)}, u32[]{:S(2)}) collective-permute-start(f32[40,128]{1,0:T(8,128)S(1)} %get-tuple-element.17.r_2_), channel_id=1, source_target_pairs={{0,64},{1,65},{2,66},{3,67},{4,68},{5,69},{6,70},{7,71},{8,72},{9,... | collective-permute-start | bytes 61448 | tf_op jit(solution)/shard_map/ppermute | solution.py:326
  64.5 0.6 collective-permute-start.13
  65.1 1.0 %collective-permute-start.14 = (f32[40,128]{1,0:T(8,128)S(1)}, f32[40,128]{1,0:T(8,128)S(1)}, u32[]{:S(2)}, u32[]{:S(2)}) collective-permute-start(f32[40,128]{1,0:T(8,128)S(1)} %get-tuple-element.17.r_2_), channel_id=1, source_target_pairs={{0,16},{1,17},{2,18},{3,19},{4,20},{5,21},{6,22},{7,23},{8,24},{9,... | collective-permute-start | bytes 61448 | tf_op jit(solution)/shard_map/ppermute | solution.py:326
  66.0 0.0 collective-permute-done.10.r_3_
  66.0 0.3 collective-permute-done.11.r_4_
  66.4 0.7 %collective-permute-done.12.r_5_ = f32[40,128]{1,0:T(8,128)S(1)} collective-permute-done((f32[40,128]{1,0:T(8,128)S(1)}, f32[40,128]{1,0:T(8,128)S(1)}, u32[]{:S(2)}, u32[]{:S(2)}) %collective-permute-start.12) | collective-permute-done | bytes 20512 | tf_op jit(solution)/shard_map/ppermute | solution.py:326
  67.1 2.4 %collective-permute-done.13.r_6_ = f32[40,128]{1,0:T(8,128)S(1)} collective-permute-done((f32[40,128]{1,0:T(8,128)S(1)}, f32[40,128]{1,0:T(8,128)S(1)}, u32[]{:S(2)}, u32[]{:S(2)}) %collective-permute-start.13) | collective-permute-done | bytes 20512 | tf_op jit(solution)/shard_map/ppermute | solution.py:326
  69.4 0.0 collective-permute-done.14.r_7_
  69.4 1.3 %assemble.1 = (f32[32,8,128]{2,1,0:T(8,128)}, f32[8,128]{1,0:T(8,128)}) custom-call(s32[128]{0:T(128)S(1)} %copy-done.1, f32[2,40,128]{2,1,0:T(8,128)S(1)} %get-tuple-element.16.r_1_, f32[40,128]{1,0:T(8,128)S(1)} %get-tuple-element.17.r_2_, f32[40,128]{1,0:T(8,128)S(1)} %collective-permute-done.10.r_3_, f32[40,128]{1,0:T(8,128)S(1)} %collective-permute-done.11.r_4_, ...), custom_call_target="tpu_custom_call" | custom-call | tf_op jit(solution)/shard_map/assemble/pallas_call | solution.py:354
Async XLA Ops:
  1.3 17.5 %copy-start = (s32[4,8]{1,0:T(4,128)S(1)}, s32[4,8]{1,0:T(4,128)}, u32[]{:S(2)}) copy-start(s32[4,8]{1,0:T(4,128)} %r_0_.3) | copy-start | bytes 388
  2.3 12.0 %collective-permute-start = (f32[35,8,128]{2,1,0:T(8,128)S(1)}, f32[35,8,128]{2,1,0:T(8,128)S(1)}, u32[]{:S(2)}, u32[]{:S(2)}) collective-permute-start(f32[35,8,128]{2,1,0:T(8,128)S(1)} %constant_dynamic-update-slice_fusion.r_3_), channel_id=1, source_target_pairs={{0,2},{1,3},{2,4},{3,5},{4,6},{5,7},{6,8},{7,9},{8,10},{9,11},{10,... | collective-permute-start | bytes 430088 | tf_op jit(solution)/shard_map/ppermute | solution.py:313
  2.4 13.6 %collective-permute-start.1 = (f32[35,8,128]{2,1,0:T(8,128)S(1)}, f32[35,8,128]{2,1,0:T(8,128)S(1)}, u32[]{:S(2)}, u32[]{:S(2)}) collective-permute-start(f32[35,8,128]{2,1,0:T(8,128)S(1)} %constant_dynamic-update-slice_fusion.r_3_), channel_id=1, source_target_pairs={{0,3},{1,2},{2,5},{3,4},{4,7},{5,6},{6,9},{7,8},{8,11},{9,10},{10,... | collective-permute-start | bytes 430088 | tf_op jit(solution)/shard_map/ppermute | solution.py:313
  7.3 8.7 %collective-permute-start.2 = (f32[35,8,128]{2,1,0:T(8,128)S(1)}, f32[35,8,128]{2,1,0:T(8,128)S(1)}, u32[]{:S(2)}, u32[]{:S(2)}) collective-permute-start(f32[35,8,128]{2,1,0:T(8,128)S(1)} %constant_dynamic-update-slice_fusion.r_3_), channel_id=1, source_target_pairs={{0,1},{1,0},{2,3},{3,2},{4,5},{5,4},{6,7},{7,6},{8,9},{9,8},{10,11... | collective-permute-start | bytes 430088 | tf_op jit(solution)/shard_map/ppermute | solution.py:313
  7.6 8.4 %collective-permute-start.3 = (f32[35,8,128]{2,1,0:T(8,128)S(1)}, f32[35,8,128]{2,1,0:T(8,128)S(1)}, u32[]{:S(2)}, u32[]{:S(2)}) collective-permute-start(f32[35,8,128]{2,1,0:T(8,128)S(1)} %constant_dynamic-update-slice_fusion.r_3_), channel_id=1, source_target_pairs={{0,126},{1,127},{2,0},{3,1},{4,2},{5,3},{6,4},{7,5},{8,6},{9,7},{1... | collective-permute-start | bytes 430088 | tf_op jit(solution)/shard_map/ppermute | solution.py:313
  11.3 7.6 %collective-permute-start.4 = (f32[35,8,128]{2,1,0:T(8,128)S(1)}, f32[35,8,128]{2,1,0:T(8,128)S(1)}, u32[]{:S(2)}, u32[]{:S(2)}) collective-permute-start(f32[35,8,128]{2,1,0:T(8,128)S(1)} %constant_dynamic-update-slice_fusion.r_3_), channel_id=1, source_target_pairs={{0,127},{1,126},{2,1},{3,0},{4,3},{5,2},{6,5},{7,4},{8,7},{9,6},{1... | collective-permute-start | bytes 430088 | tf_op jit(solution)/shard_map/ppermute | solution.py:313
  20.1 8.1 %collective-permute-start.5 = (f32[152,128]{1,0:T(8,128)S(1)}, f32[152,128]{1,0:T(8,128)S(1)}, u32[]{:S(2)}, u32[]{:S(2)}) collective-permute-start(f32[152,128]{1,0:T(8,128)S(1)} %get-tuple-element.11), channel_id=1, source_target_pairs={{0,112},{1,113},{2,114},{3,115},{4,116},{5,117},{6,118},{7,119},{8... | collective-permute-start | bytes 233480 | tf_op jit(solution)/shard_map/ppermute | solution.py:326
  23.4 5.9 %collective-permute-start.6 = (f32[152,128]{1,0:T(8,128)S(1)}, f32[152,128]{1,0:T(8,128)S(1)}, u32[]{:S(2)}, u32[]{:S(2)}) collective-permute-start(f32[152,128]{1,0:T(8,128)S(1)} %get-tuple-element.12), channel_id=1, source_target_pairs={{0,80},{1,81},{2,82},{3,83},{4,84},{5,85},{6,86},{7,87},{8,88},{9,... | collective-permute-start | bytes 233480 | tf_op jit(solution)/shard_map/ppermute | solution.py:326
  23.4 6.6 %collective-permute-start.7 = (f32[152,128]{1,0:T(8,128)S(1)}, f32[152,128]{1,0:T(8,128)S(1)}, u32[]{:S(2)}, u32[]{:S(2)}) collective-permute-start(f32[152,128]{1,0:T(8,128)S(1)} %get-tuple-element.13), channel_id=1, source_target_pairs={{0,64},{1,65},{2,66},{3,67},{4,68},{5,69},{6,70},{7,71},{8,72},{9,... | collective-permute-start | bytes 233480 | tf_op jit(solution)/shard_map/ppermute | solution.py:326
  24.6 5.6 %collective-permute-start.8 = (f32[152,128]{1,0:T(8,128)S(1)}, f32[152,128]{1,0:T(8,128)S(1)}, u32[]{:S(2)}, u32[]{:S(2)}) collective-permute-start(f32[152,128]{1,0:T(8,128)S(1)} %get-tuple-element.14), channel_id=1, source_target_pairs={{0,48},{1,49},{2,50},{3,51},{4,52},{5,53},{6,54},{7,55},{8,56},{9,... | collective-permute-start | bytes 233480 | tf_op jit(solution)/shard_map/ppermute | solution.py:326
  25.5 4.7 %collective-permute-start.9 = (f32[152,128]{1,0:T(8,128)S(1)}, f32[152,128]{1,0:T(8,128)S(1)}, u32[]{:S(2)}, u32[]{:S(2)}) collective-permute-start(f32[152,128]{1,0:T(8,128)S(1)} %get-tuple-element.15), channel_id=1, source_target_pairs={{0,16},{1,17},{2,18},{3,19},{4,20},{5,21},{6,22},{7,23},{8,24},{9,... | collective-permute-start | bytes 233480 | tf_op jit(solution)/shard_map/ppermute | solution.py:326
  28.2 2.0 %copy-start.1 = (s32[128]{0:T(128)S(1)}, s32[128]{0:T(128)}, u32[]{:S(2)}) copy-start(s32[128]{0:T(128)} %r_0_.5) | copy-start | bytes 1540
  59.3 6.8 %collective-permute-start.10 = (f32[40,128]{1,0:T(8,128)S(1)}, f32[40,128]{1,0:T(8,128)S(1)}, u32[]{:S(2)}, u32[]{:S(2)}) collective-permute-start(f32[40,128]{1,0:T(8,128)S(1)} %get-tuple-element.17.r_2_), channel_id=1, source_target_pairs={{0,112},{1,113},{2,114},{3,115},{4,116},{5,117},{6,118},{7,119},{8... | collective-permute-start | bytes 61448 | tf_op jit(solution)/shard_map/ppermute | solution.py:326
  61.7 4.7 %collective-permute-start.11 = (f32[40,128]{1,0:T(8,128)S(1)}, f32[40,128]{1,0:T(8,128)S(1)}, u32[]{:S(2)}, u32[]{:S(2)}) collective-permute-start(f32[40,128]{1,0:T(8,128)S(1)} %get-tuple-element.17.r_2_), channel_id=1, source_target_pairs={{0,80},{1,81},{2,82},{3,83},{4,84},{5,85},{6,86},{7,87},{8,88},{9,... | collective-permute-start | bytes 61448 | tf_op jit(solution)/shard_map/ppermute | solution.py:326
  63.3 3.8 %collective-permute-start.12 = (f32[40,128]{1,0:T(8,128)S(1)}, f32[40,128]{1,0:T(8,128)S(1)}, u32[]{:S(2)}, u32[]{:S(2)}) collective-permute-start(f32[40,128]{1,0:T(8,128)S(1)} %get-tuple-element.17.r_2_), channel_id=1, source_target_pairs={{0,64},{1,65},{2,66},{3,67},{4,68},{5,69},{6,70},{7,71},{8,72},{9,... | collective-permute-start | bytes 61448 | tf_op jit(solution)/shard_map/ppermute | solution.py:326
  64.5 5.0 %collective-permute-start.13 = (f32[40,128]{1,0:T(8,128)S(1)}, f32[40,128]{1,0:T(8,128)S(1)}, u32[]{:S(2)}, u32[]{:S(2)}) collective-permute-start(f32[40,128]{1,0:T(8,128)S(1)} %get-tuple-element.17.r_2_), channel_id=1, source_target_pairs={{0,48},{1,49},{2,50},{3,51},{4,52},{5,53},{6,54},{7,55},{8,56},{9,... | collective-permute-start | bytes 61448 | tf_op jit(solution)/shard_map/ppermute | solution.py:326
  65.1 4.4 %collective-permute-start.14 = (f32[40,128]{1,0:T(8,128)S(1)}, f32[40,128]{1,0:T(8,128)S(1)}, u32[]{:S(2)}, u32[]{:S(2)}) collective-permute-start(f32[40,128]{1,0:T(8,128)S(1)} %get-tuple-element.17.r_2_), channel_id=1, source_target_pairs={{0,16},{1,17},{2,18},{3,19},{4,20},{5,21},{6,22},{7,23},{8,24},{9,... | collective-permute-start | bytes 61448 | tf_op jit(solution)/shard_map/ppermute | solution.py:326
